TPU v7x, 32 devices: a whole 2x2x4 slice. The times are simulated.
32 devices in a mesh: seq: 8 (over z, y), band: 4 (over x, core).
Axes of the slice: x: 2, y: 2, z: 4, core: 2. Of those that a mesh axis runs over, the one named last changes fastest.
Arguments:
- tokens: bfloat16 [4, 2048, 1024], P('band', 'seq'), may hold values from -6 to 6
- ln_gain: float32 [1024], replicated, may hold values from 0.25 to 12
- w_qkv: bfloat16 [1024, 3072], P('band', 'seq'), may hold values from -0.1875 to 0.1875
- w_out: bfloat16 [1024, 1024], P('band', 'seq'), may hold values from -0.1875 to 0.1875
- dec_gain: float32 [1024], replicated, may hold values from 0.25 to 12
- w_kv: bfloat16 [1024, 2048], P('band', 'seq'), may hold values from -0.1875 to 0.1875
- w_final: bfloat16 [1024, 96], P('band', 'seq'), may hold values from -0.1875 to 0.1875
- reach: int32 [2048], P('seq'), may hold values from 1 to 128, as said below
- grid_query: bfloat16 [4, 2048, 1024], P('band', 'seq'), may hold values from -128 to 128
- neighbours: int32 [2048, 8], P('seq'), may hold values from 0 to 2047, as said below
- counts: int32 [2048], P('seq'), may hold values from 1 to 8, as said below
Outputs:
- fields: bfloat16 [4, 96, 2048], P('band', None, 'seq')
Inputs may be any that keep to these rules, and one draw needn't show every extreme that they name: Every device's block of 256 tokens holds a token of reach 128. `neighbours`: grid points are in blocks of 256 rows, block s lying over mesh tokens s * 256 to (s + 1) * 256 - 1. Of one block's used slots (slot below counts), at most 12 name tokens of any one other block; one mesh block is named so by exactly 12 used slots of every other block. Unused slots name tokens of the point's own block. `counts`: every block of 256 grid points has a point with all 8 slots used.
All inputs are finite; a program needn't handle non-finite values.
Results may differ from a plain program's by a relative error of at most 0.025.
The roundings to bfloat16 on the way count: a program that leaves them out, or rounds other values in their place, can miss the bound.
Values may be sent and summed in bfloat16 or wider, within the bound.
No kernel may reach another device: no remote copies, remote signals or barrier semaphores. Data moves between devices by JAX's collectives and lax.ppermute only.
A program may use at most 64 MiB of HBM per device.

v0:
```python
import functools
import math

import jax
import jax.numpy as jnp
import numpy as np
from jax import lax
from jax.experimental import pallas as pl
from jax.experimental.pallas import tpu as pltpu
from jax.sharding import PartitionSpec as P

HEADS = 16
HALF = 128
C = 12
SLOTS = 16
EPSILON = 1e-05
NEG = -1e30
LANES = 128
GROUPS = 8
BANDS = 4
CHUNKS = (0, 2, 1, 3)
RING = (0, 2, 4, 6, 7, 5, 3, 1)
VMEM = 60 * 1024 * 1024
SMALL = pl.CostEstimate(flops=1000, bytes_accessed=1000, transcendentals=0)
F32 = jnp.float32
BF16 = jnp.bfloat16


def dot(a, b):
    return jnp.dot(a, b, preferred_element_type=F32)


def dot_nt(a, b):
    return lax.dot_general(a, b, (((1,), (1,)), ((), ())), preferred_element_type=F32)


def layer_norm(values, gain):
    values = values.astype(F32)
    centred = values - jnp.mean(values, axis=-1, keepdims=True)
    spread = jnp.mean(centred * centred, axis=-1, keepdims=True)
    return (centred * lax.rsqrt(spread + EPSILON) * gain).astype(BF16)


def here_at(riding):
    return lax.axis_index("seq"), (lax.axis_index("band") % 2 if riding else 0)


def ring_spots(riding):
    if not riding:
        return list(range(GROUPS)) + [0]
    seq, core = here_at(True)
    at_ring = jnp.where(seq % 2 == 0, seq // 2, GROUPS - 1 - seq // 2)
    turn = jnp.where(core == 0, GROUPS - 1, 1)
    spots = []
    for at in range(GROUPS):
        step = (at_ring + turn * at) % GROUPS
        spots.append(jnp.where(step < GROUPS // 2, 2 * step, 2 * GROUPS - 1 - 2 * step))
    return spots + [core]


def params(**more):
    return pltpu.CompilerParams(vmem_limit_bytes=VMEM, **more)


def full_spec(shape):
    return pl.BlockSpec(shape, lambda *_: (0,) * len(shape))


def own_first(rows, core, depth):
    parts = [rows[:, b * depth : (b + 1) * depth] for b in range(BANDS)]
    order = ((0, 1), (2, 3), (1, 0), (3, 2))
    return jnp.concatenate([jnp.where(core == 0, parts[a], parts[b]) for a, b in order], axis=1)


def as_column(row):
    return jnp.broadcast_to(row, (8, row.shape[1])).T[:, :1]


def prepare_kernel(
    total, riding, left, own, right, gain, reach, neighbours, counts, normed, bias, multiplicity
):
    place = here_at(riding)
    tok = own.shape[0]
    depth = own.shape[1] // BANDS
    for at, part in ((0, left), (HALF, own), (HALF + tok, right)):
        rows = layer_norm(part[...], gain[...])
        normed[at : at + part.shape[0], :] = own_first(rows, place[1], depth)

    first = place[0] * tok
    span = 3 * HALF
    row = lax.broadcasted_iota(jnp.int32, (HALF, span), 0)
    col = lax.broadcasted_iota(jnp.int32, (HALF, span), 1)
    away = jnp.abs(row + HALF - col)
    limit = as_column(reach[...])
    for block in range(tok // HALF):
        key = first + (block - 1) * HALF + col
        allowed = (away <= limit[block * HALF : (block + 1) * HALF, :]) & (key >= 0) & (key < total)
        bias[block] = jnp.where(allowed, 0.0, NEG)

    ids = neighbours[...].T
    used = as_column(counts[...])
    mesh = lax.broadcasted_iota(jnp.int32, multiplicity.shape, 1) + first
    here = jnp.zeros(multiplicity.shape, F32)
    for slot in range(ids.shape[1]):
        here += ((ids[:, slot : slot + 1] == mesh) & (slot < used)).astype(F32)
    multiplicity[...] = here


def prepare(total, riding, left, own, right, gain, reach, neighbours, counts):
    tok, width = own.shape
    operands = (left, own, right, gain, reach, neighbours, counts)
    outs = (
        jax.ShapeDtypeStruct((tok + 2 * HALF, width), BF16),
        jax.ShapeDtypeStruct((tok // HALF, HALF, 3 * HALF), F32),
        jax.ShapeDtypeStruct((neighbours.shape[1], tok), F32),
    )
    return pl.pallas_call(
        functools.partial(prepare_kernel, total, riding),
        out_shape=outs,
        in_specs=[pl.BlockSpec(memory_space=pltpu.VMEM)] * len(operands),
        out_specs=[pl.BlockSpec(memory_space=pltpu.VMEM)] * len(outs),
        compiler_params=params(),
        cost_estimate=SMALL,
        name="prepare",
    )(*operands)


def tables_kernel(tok, count, neighbours, counts, low, rank, tri, *refs):
    weights, (multiplicity, requested) = refs[:count], refs[count : count + 2]
    first = lax.axis_index("seq") * tok
    slots = neighbours.shape[0]
    ids = neighbours[...].T
    used = as_column(counts[...])
    start = low[...]
    elsewhere = start != first
    hits = []
    for slot in range(slots):
        which = ids[:, slot : slot + 1]
        hits.append(
            ((which >= start) & (which < start + tok) & (slot < used) & elsewhere).astype(F32)
        )
    running = dot(tri[...], sum(hits).astype(BF16))
    order = rank[...]
    asked = jnp.zeros(hits[0].shape, F32)
    there = jnp.zeros(hits[0].shape, F32)
    for slot in range(slots):
        mine = jnp.where(running == order, hits[slot], 0.0)
        there += mine
        offset = (ids[:, slot : slot + 1] - start).astype(F32)
        asked += jnp.where(mine > 0, offset, 0.0)
        running += hits[slot]
    multiplicity[...] = there
    asked = jnp.sum(asked, axis=0, keepdims=True)
    requested[...] = asked.astype(BF16)
    if weights:
        payload = refs[-1]
        at = 0
        for weight in weights:
            depth, columns = weight.shape
            for first in range(0, columns, LANES):
                payload[at : at + depth, :] = weight[:, first : first + LANES]
                at += depth
        payload[at:, :] = jnp.broadcast_to(asked, (SLOTS, LANES)).astype(BF16)


def tables(tok, neighbours, counts, shards, weights):
    points = neighbours.shape[1]
    remote = shards * SLOTS
    column = np.arange(remote)
    low = (column // SLOTS * tok).astype(np.int32)[None]
    rank = (column % SLOTS).astype(np.float32)[None]
    tri = np.tril(np.ones((points, points), np.float32), -1).astype(BF16)
    operands = (neighbours, counts, low, rank, tri) + weights
    outs = (
        jax.ShapeDtypeStruct((points, remote), F32),
        jax.ShapeDtypeStruct((1, remote), BF16),
    )
    if weights:
        rows = sum(weight.shape[0] * weight.shape[1] // LANES for weight in weights) + SLOTS
        outs += (jax.ShapeDtypeStruct((rows, LANES), BF16),)
    return pl.pallas_call(
        functools.partial(tables_kernel, tok, len(weights)),
        out_shape=outs,
        in_specs=[pl.BlockSpec(memory_space=pltpu.VMEM)] * len(operands),
        out_specs=[pl.BlockSpec(memory_space=pltpu.VMEM)] * len(outs),
        compiler_params=params(),
        cost_estimate=SMALL,
        name="tables",
    )(*operands)


def pair_attend(queries, keys, values, bias, weights_of):
    rows = queries.shape[0]
    lane = lax.broadcasted_iota(jnp.int32, (rows, LANES), 1)
    first = lane < LANES // 2
    zero = jnp.zeros_like(queries)
    both = jnp.concatenate(
        [jnp.where(first, queries, zero), jnp.where(first, zero, queries)], axis=0
    )
    scores = dot_nt(both, keys)
    scores = scores + jnp.concatenate([bias, bias], axis=0)
    top = jnp.max(scores, axis=-1, keepdims=True)
    weights = weights_of(jnp.exp(scores - top)).astype(BF16)
    summed = dot(weights, jnp.concatenate([values, jnp.ones_like(values)], axis=1))
    share = summed[:, :LANES] / summed[:, LANES:]
    return jnp.where(first, share[:rows], share[rows:]).astype(BF16)


def start_loads(spots, pieces, layout, scratch, arrived, rows, core=None):
    copies = {}
    for n, (piece, (at, half)) in enumerate(zip(pieces, layout)):
        place = scratch.at[spots[at]]
        if half is None:
            copy = pltpu.make_async_copy(piece.at[:, :, rows, :], place, arrived.at[n])
        else:
            to = half if core is None else (1 - core if half else core)
            copy = pltpu.make_async_copy(piece.at[:, rows, :], place.at[to], arrived.at[n])
        copy.start()
        copies.setdefault(at, []).append(copy)
    return copies


def wait_group(copies, at):
    for copy in copies.get(at, ()):
        copy.wait()


def lanes_of(block, depth, start, count):
    rows = block.shape[0] * block.shape[1] * depth if block.ndim == 4 else block.shape[0] * depth
    columns = [
        block[..., start + g * depth : start + (g + 1) * depth, :].reshape(rows, LANES)
        for g in range(count)
    ]
    return columns[0] if count == 1 else jnp.concatenate(columns, axis=1)


SMEM = pl.BlockSpec(memory_space=pltpu.SMEM)
VMEM_SPEC = pl.BlockSpec(memory_space=pltpu.VMEM)
ANY = pl.BlockSpec(memory_space=pl.ANY)


def projection(normed, weight, depth, per):
    return dot(normed, lanes_of(weight[...], depth, 0, per)).astype(BF16)


def project_kernel(layout, riding, normed, *refs):
    spots = ring_spots(riding)
    pieces = refs[: len(layout)]
    out, scratch, made, arrived, sent = refs[-5:]
    per = made.shape[1]
    depth = normed.shape[1] // BANDS
    copies = start_loads(spots, pieces, layout, scratch, arrived, slice(0, per * depth))
    writes = []
    for n, at in enumerate(copies):
        wait_group(copies, at)
        total = projection(normed[...], scratch.at[spots[at]], depth, per)
        for group in range(per):
            made[n, group] = total[:, group * LANES : (group + 1) * LANES]
        writes.append(
            pltpu.make_async_copy(made.at[n], out.at[pl.ds(spots[at] * per, per)], sent.at[n])
        )
        writes[-1].start()
    for write in writes:
        write.wait()


def project(riding, normed, pieces, before):
    rows, width = normed.shape
    layout = tuple(place for _, place in pieces)
    arrays = [array for array, _ in pieces]
    per = 3 * width // LANES // GROUPS
    count = len({at for at, _ in layout})
    more = [] if before is None else [before]
    return pl.pallas_call(
        functools.partial(project_kernel, layout, riding),
        out_shape=jax.ShapeDtypeStruct((GROUPS * per, rows, LANES), BF16),
        in_specs=[VMEM_SPEC] + [ANY] * (len(arrays) + len(more)),
        out_specs=ANY,
        scratch_shapes=[
            pltpu.VMEM((GROUPS, 2, 2, per * width // BANDS, LANES), BF16),
            pltpu.VMEM((count, per, rows, LANES), BF16),
            pltpu.SemaphoreType.DMA((len(arrays),)),
            pltpu.SemaphoreType.DMA((count,)),
        ],
        input_output_aliases={1 + len(arrays): 0} if more else {},
        compiler_params=params(),
        cost_estimate=SMALL,
        name="project",
    )(normed, *arrays, *more)


def attend_kernel(layout, ready, riding, normed, bias, *refs):
    spots = ring_spots(riding)
    pieces = refs[: len(layout)]
    made, attended, scratch, projected, arrived, loaded = refs[len(layout) :]
    width = normed.shape[1]
    depth = width // BANDS
    per = projected.shape[0] // GROUPS
    copies = start_loads(spots, pieces, layout, scratch, arrived, slice(0, per * depth))
    reads = []
    for n, at in enumerate(ready):
        place = pl.ds(spots[at] * per, per)
        reads.append(pltpu.make_async_copy(made.at[place], projected.at[place], loaded.at[n]))
        reads[-1].start()
    for at in copies:
        wait_group(copies, at)
        total = projection(normed[...], scratch.at[spots[at]], depth, per)
        for group in range(per):
            projected[spots[at] * per + group] = total[:, group * LANES : (group + 1) * LANES]
    for read in reads:
        read.wait()
    pairs = width // LANES
    scale = BF16(1.0 / math.sqrt(width // HEADS))
    for pair in range(pairs):
        for block in range(bias.shape[0]):
            at = block * HALF
            attended[at : at + HALF, pair * LANES : (pair + 1) * LANES] = pair_attend(
                projected[pair, at + HALF : at + 2 * HALF, :] * scale,
                projected[pairs + pair, at : at + 3 * HALF, :],
                projected[2 * pairs + pair, at : at + 3 * HALF, :],
                bias[block],
                lambda weights: weights,
            )


def attend(riding, normed, bias, pieces, made, ready):
    rows, width = normed.shape
    tok = rows - 2 * HALF
    layout = tuple(place for _, place in pieces)
    arrays = [array for array, _ in pieces]
    per = made.shape[0] // GROUPS
    return pl.pallas_call(
        functools.partial(attend_kernel, layout, ready, riding),
        out_shape=jax.ShapeDtypeStruct((tok, width), BF16),
        in_specs=[VMEM_SPEC, VMEM_SPEC] + [ANY] * (len(arrays) + 1),
        out_specs=VMEM_SPEC,
        scratch_shapes=[
            pltpu.VMEM((GROUPS, 2, 2, per * width // BANDS, LANES), BF16),
            pltpu.VMEM(made.shape, BF16),
            pltpu.SemaphoreType.DMA((len(arrays),)),
            pltpu.SemaphoreType.DMA((len(ready),)),
        ],
        compiler_params=params(),
        cost_estimate=SMALL,
        name="attend",
    )(normed, bias, *arrays, made)


def picked_rows(place, ids, spots, rows, asked, arrived):
    tok = rows.shape[0]
    if spots is None:
        which = ids[...]
    else:
        for at in range(GROUPS):
            asked[pl.ds(spots[at] * SLOTS, SLOTS), :] = jnp.broadcast_to(
                arrived[at, 0:1, :].astype(F32), (SLOTS, LANES)
            )
        count = GROUPS * SLOTS
        lane = lax.broadcasted_iota(jnp.int32, (count, LANES), 1)
        slot = lax.broadcasted_iota(jnp.int32, (count, LANES), 0) % SLOTS
        mine = jnp.where(lane == place[0] * SLOTS + slot, asked[...], 0.0)
        which = jnp.sum(mine, axis=1, keepdims=True).astype(jnp.int32)
    here = lax.broadcasted_iota(jnp.int32, (which.shape[0], tok), 1)
    return dot((which == here).astype(BF16), rows).astype(BF16)


def chunked(values, depth):
    return jnp.concatenate([values[:, b * depth : (b + 1) * depth] for b in CHUNKS], axis=1)


def mix_kernel(layout, riding, states, gain, *refs):
    place, spots = here_at(riding), ring_spots(riding)
    attended, refs = refs[0], refs[1:]
    ids = None
    if not riding:
        ids, refs = refs[0], refs[1:]
    pieces = refs[: len(layout)]
    decoded, found, mixed, scratch, asked, notes, arrived, noted = refs[len(layout) :]
    width = states.shape[1]
    depth = width // BANDS
    start = 3 * width // GROUPS // LANES * depth
    copies = start_loads(spots, pieces, layout, scratch, arrived, slice(start, start + depth))
    reads = []
    if riding:
        for piece, (at, core) in zip(pieces, layout):
            if core == 0:
                end = piece.shape[-2]
                reads.append(
                    pltpu.make_async_copy(
                        piece.at[0, end - SLOTS : end, :], notes.at[at], noted.at[at]
                    )
                )
                reads[-1].start()
    inputs = own_first(attended[...], place[1], depth)
    for at in range(GROUPS):
        wait_group(copies, at)
    for at in range(0, GROUPS, 2):
        columns = slice(at * LANES, (at + 2) * LANES)
        weight = [lanes_of(scratch[at + n], depth, 0, 1) for n in range(2)]
        total = dot(inputs, jnp.concatenate(weight, axis=1))
        mixed[:, columns] = (states[:, columns].astype(F32) + total).astype(BF16)
    for read in reads:
        read.wait()
    rows = chunked(layer_norm(mixed[...], gain[...]), depth)
    decoded[...] = rows
    found[...] = picked_rows(place, ids, spots if riding else None, rows, asked, notes)


def mix(states, attended, gain, ids, pieces, layout, shards):
    tok, width = states.shape
    more = [] if ids is None else [ids]
    return pl.pallas_call(
        functools.partial(mix_kernel, layout, ids is None),
        out_shape=(
            jax.ShapeDtypeStruct((tok, width), BF16),
            jax.ShapeDtypeStruct((shards * SLOTS, width), BF16),
        ),
        in_specs=[VMEM_SPEC] * (3 + len(more)) + [ANY] * len(pieces),
        out_specs=(VMEM_SPEC, VMEM_SPEC),
        scratch_shapes=[
            pltpu.VMEM((tok, width), BF16),
            pltpu.VMEM((GROUPS, 2, 2, width // BANDS, LANES), BF16),
            pltpu.VMEM((GROUPS * SLOTS, LANES), F32),
            pltpu.VMEM((GROUPS, SLOTS, LANES), BF16),
            pltpu.SemaphoreType.DMA((len(pieces),)),
            pltpu.SemaphoreType.DMA((GROUPS,)),
        ],
        compiler_params=params(),
        cost_estimate=SMALL,
        name="mix",
    )(states, gain, attended, *more, *pieces)


def decode_kernel(layout, each, riding, queries, decoded, fetched, here, there, *refs):
    spots = ring_spots(riding)
    pieces = refs[: len(layout)]
    fields, scratch, table, arrived = refs[len(layout) :]
    points, width = queries.shape
    depth = width // BANDS
    per = 2 * width // GROUPS // LANES
    kept = scratch.shape[3]
    copies = start_loads(
        spots, pieces, layout, scratch, arrived, slice(0, kept), spots[GROUPS]
    )
    inputs = jnp.concatenate([decoded[...], fetched[...]], axis=0)
    for at in range(GROUPS):
        wait_group(copies, at)
        spot = spots[at]
        total = dot(inputs, lanes_of(scratch[spot], depth, 0, per)).astype(BF16)
        for group in range(per):
            table[spot * per + group] = total[:, group * LANES : (group + 1) * LANES]

    pairs = width // LANES
    scale = BF16(1.0 / math.sqrt(width // HEADS))
    times = jnp.concatenate([here[...], there[...]], axis=1)
    bias = jnp.where(times > 0, 0.0, NEG)
    both = jnp.concatenate([times, times], axis=0)
    rows = []
    for pair in range(pairs):
        rows.append(
            pair_attend(
                queries[:, pair * LANES : (pair + 1) * LANES] * scale,
                table[pair],
                table[pairs + pair],
                bias,
                lambda weights: weights * both,
            )
        )
    gridded = jnp.concatenate(rows, axis=1)
    start = per * depth
    halves = depth // LANES
    height = (kept - start) // halves
    padded = jnp.zeros((GROUPS * height, points), F32)
    for chunk, band in enumerate(CHUNKS):
        for half in range(halves):
            at = start + half * height
            weight = scratch[:, chunk // 2, chunk % 2, at : at + height, :]
            first = band * depth + half * LANES
            padded += dot_nt(
                weight.reshape(GROUPS * height, LANES), gridded[:, first : first + LANES]
            )
    parts = [padded[group * height : group * height + each] for group in range(GROUPS)]
    fields[...] = jnp.concatenate(parts, axis=0).astype(BF16)


def decode(riding, queries, decoded, fetched, here, there, pieces, layout, outputs):
    points, width = queries.shape
    height = pieces[0].shape[-2]
    rows = decoded.shape[0] + fetched.shape[0]
    return pl.pallas_call(
        functools.partial(decode_kernel, layout, outputs // GROUPS, riding),
        out_shape=jax.ShapeDtypeStruct((outputs, points), BF16),
        in_specs=[VMEM_SPEC] * 5 + [ANY] * len(pieces),
        out_specs=VMEM_SPEC,
        scratch_shapes=[
            pltpu.VMEM((GROUPS, 2, 2, height, LANES), BF16),
            pltpu.VMEM((2 * width // LANES, rows, LANES), BF16),
            pltpu.SemaphoreType.DMA((len(pieces),)),
        ],
        compiler_params=params(),
        cost_estimate=SMALL,
        name="decode",
    )(queries, decoded, fetched, here, there, *pieces)


def stacked(*weights):
    parts = []
    for weight in weights:
        for at in range(0, weight.shape[-1], LANES):
            parts.append(weight[..., at : at + LANES])
    return jnp.concatenate(parts, axis=-2)


def pair_x(block, gate=None):
    if gate is not None:
        block, _ = lax.optimization_barrier((block, gate))
    other = lax.ppermute(block, "band", [(i, i ^ 2) for i in range(BANDS)])
    low = lax.axis_index("band") < 2
    return jnp.stack([jnp.where(low, block, other), jnp.where(low, other, block)])


def pair_core(block):
    other = swap_core(block)
    low = lax.axis_index("band") % 2 == 0
    return jnp.stack([jnp.where(low, block, other), jnp.where(low, other, block)])


def carry(block):
    pairs = []
    for i in range(GROUPS):
        here, there = RING[i] * BANDS, RING[(i + 1) % GROUPS] * BANDS
        for x in range(2):
            pairs.append((here + 2 * x, there + 2 * x))
            pairs.append((there + 2 * x + 1, here + 2 * x + 1))
    return lax.ppermute(block, ("seq", "band"), pairs)


def swap_core(block):
    return lax.ppermute(block, "band", [(i, i ^ 1) for i in range(BANDS)])


def chain_step(chains, step, gate=None):
    if gate is not None:
        *chains, _ = lax.optimization_barrier((*chains, gate))
    chains = [carry(block) for block in chains]
    pieces = []
    for half, block in enumerate(chains):
        pieces.append((block, (step, half)))
        pieces.append((swap_core(block), (GROUPS - step, 1 - half)))
    return chains, pieces


def ring_step(block, step, gate=None):
    if gate is not None:
        block, _ = lax.optimization_barrier((block, gate))
    block = carry(block)
    return block, [(block, (step, None)), (swap_core(block), (GROUPS - step, None))]


def last_step(block):
    half = lax.dynamic_index_in_dim(block, lax.axis_index("band") % 2, 0, keepdims=False)
    half = carry(half)
    return [(half, (GROUPS // 2, 0)), (swap_core(half), (GROUPS // 2, 1))]


def whole_blocks(*weights):
    parts = []
    for weight, height in weights:
        weight = lax.all_gather(weight, "seq", axis=1, tiled=True)
        weight = lax.all_gather(weight, "band", axis=0, tiled=True)
        depth, columns = weight.shape[0] // BANDS, weight.shape[1] // GROUPS
        weight = weight.reshape(2, 2, depth, GROUPS, columns).transpose(3, 1, 0, 2, 4)
        if height:
            weight = jnp.pad(
                weight.swapaxes(-1, -2), ((0, 0),) * 3 + ((0, height - columns), (0, 0))
            )
        parts.append(weight)
    return stacked(*parts)


def local(
    tokens, ln_gain, w_qkv, w_out, dec_gain, w_kv, w_final, reach, grid_query, neighbours, counts
):
    states = tokens[0]
    tok, width = states.shape
    shards, bands = lax.axis_size("seq"), lax.axis_size("band")
    outputs = w_final.shape[1] * shards
    height = -(-outputs // GROUPS // 16) * 16
    riding = (shards, bands) == (GROUPS, BANDS)
    up = [(i, i + 1) for i in range(shards - 1)]
    down = [(i + 1, i) for i in range(shards - 1)]
    left = lax.ppermute(states[tok - HALF :], "seq", up)
    right = lax.ppermute(states[:HALF], "seq", down)
    slots = (neighbours.T, counts.reshape(1, -1))
    there, requested, *payload = tables(tok, *slots, shards, (w_qkv, w_out) if riding else ())
    normed, bias, here = prepare(
        tok * shards, riding, left, states, right, ln_gain.reshape(1, width),
        reach.reshape(1, tok), *slots,
    )
    if riding:
        mine = pair_x(payload[0])
        mine, _, _ = lax.optimization_barrier((mine, left, right))
        other = swap_core(mine)
        pieces = [(mine, (0, 0)), (other, (0, 1))]
        chains, more = chain_step([mine, other], 1)
        pieces += more
        final = jnp.pad(w_final.T, ((0, height - w_final.shape[1]), (0, 0)))
        second = pair_core(pair_x(stacked(w_kv, final), chains[0]))
        later = [(second, (0, None))]
        chains[1], _ = lax.optimization_barrier((chains[1], normed))
        chains, more = chain_step(chains, 2)
        pieces += more
        normed, _ = lax.optimization_barrier((normed, chains[1]))
        made = project(riding, normed, pieces[:6], None)
        chains, more = chain_step(chains, 3)
        pieces += more
        last, more = chain_step(chains[:1], 4, (chains[1], made))
        pieces += more
        second, *_ = lax.optimization_barrier((second, chains[1], made, pieces[7][0], pieces[9][0]))
        later = [(second, (0, None))]
        block, more = ring_step(second, 1)
        later += more
        block, more = ring_step(block, 2, [pieces[n][0] for n in (11, 13, 15)])
        later += more
        attended = attend(riding, normed, bias, pieces[6:], made, (0, 1, 7))
        block, more = ring_step(block, 3, attended)
        later += more
        ids = None
    else:
        block = whole_blocks((w_qkv, 0), (w_out, 0))
        block = jnp.pad(block, ((0, 0),) * 3 + ((0, SLOTS), (0, 0)))
        pieces = [(block[at, half], (at, half)) for at in range(GROUPS) for half in range(2)]
        block = whole_blocks((w_kv, 0), (w_final, height))
        later = [(block[at], (at, None)) for at in range(GROUPS)]
        made = project(riding, normed, pieces[:6], None)
        attended = attend(riding, normed, bias, pieces[6:], made, tuple(range(3)))
        ids = lax.all_to_all(
            requested.reshape(shards, SLOTS).astype(jnp.int32), "seq", 0, 0, tiled=True
        ).reshape(shards * SLOTS, 1)
    layout = tuple(at for _, at in pieces)
    pieces = [piece for piece, _ in pieces]
    decoded, found = mix(
        states, attended, dec_gain.reshape(1, width), ids, pieces, layout, shards
    )
    fetched = lax.all_to_all(
        found.reshape(shards, SLOTS, width), "seq", split_axis=0, concat_axis=0, tiled=True
    )
    if riding:
        block, _ = lax.optimization_barrier((block, found))
        later += last_step(block)
    layout = tuple(at for _, at in later)
    pieces = [piece for piece, _ in later]
    fields = decode(
        riding, grid_query[0], decoded, fetched.reshape(shards * SLOTS, width), here, there,
        pieces, layout, outputs,
    )
    return fields[None]


def solution(mesh):
    return jax.shard_map(
        local,
        mesh=mesh,
        in_specs=(
            P("band", "seq", None),
            P(),
            P("band", "seq"),
            P("band", "seq"),
            P(),
            P("band", "seq"),
            P("band", "seq"),
            P("seq"),
            P("band", "seq", None),
            P("seq", None),
            P("seq"),
        ),
        out_specs=P("band", None, "seq"),
        check_vma=False,
    )
```

profile of v0, /device:TPU:0, one launch (start us, length us, event | category | flops | bytes accessed | tf_op | source)
XLA Modules:
  0.0 125.9 jit_solution(10658198263864452252)
XLA Ops:
  0.0 3.0 %tables.1 = (f32[256,128]{1,0:T(8,128)}, bf16[1,128]{1,0:T(2,128)(2,1)}, bf16[1040,128]{1,0:T(8,128)(2,1)}) custom-call(s32[8,256]{1,0:T(8,128)} %bitcast.34, s32[1,256]{1,0:T(1,128)} %bitcast.39, s32[1,128]{1,0:T(1,128)} %constant.32.clone.low, f32[1,128]{1,0:T(1,128)} %constant.33.clone.rank, bf16[256,256]{1,0:T(8,128)(2,1)} %constant.34.clone.tri, ...), custom_call_target="tpu_custom_call" | custom-call | flops 1000 | bytes 1000 | tf_op jit(solution)/shard_map/tables/pallas_call | solution.py:181
  3.0 2.9 %collective-permute-start.2 = (bf16[1040,128]{1,0:T(8,128)(2,1)}, bf16[1040,128]{1,0:T(8,128)(2,1)S(1)}, u32[]{:S(2)}, u32[]{:S(2)}) collective-permute-start(bf16[1040,128]{1,0:T(8,128)(2,1)} %get-tuple-element.22), channel_id=1, source_target_pairs={{0,2},{1,3},{2,0},{3,1},{4,6},{5,7},{6,4},{7,5},{8,10},{9,11},{10,... | collective-permute-start | bytes 798728 | tf_op jit(solution)/shard_map/ppermute | solution.py:517
  6.0 1.1 slice_bitcast_fusion
  7.1 3.4 %collective-permute-start = (bf16[128,1024]{1,0:T(8,128)(2,1)S(1)}, bf16[128,1024]{1,0:T(8,128)(2,1)S(1)}, u32[]{:S(2)}, u32[]{:S(2)}) collective-permute-start(bf16[128,1024]{1,0:T(8,128)(2,1)S(1)} %get-tuple-element.42), channel_id=1, source_target_pairs={{0,4},{4,8},{8,12},{12,16},{16,20},{20,24},{24,28},{1,5},{5,9},{9,... | collective-permute-start | bytes 786440 | tf_op jit(solution)/shard_map/ppermute | solution.py:592
  10.5 1.3 %collective-permute-start.1 = (bf16[128,1024]{1,0:T(8,128)(2,1)S(1)}, bf16[128,1024]{1,0:T(8,128)(2,1)S(1)}, u32[]{:S(2)}, u32[]{:S(2)}) collective-permute-start(bf16[128,1024]{1,0:T(8,128)(2,1)S(1)} %get-tuple-element.41), channel_id=1, source_target_pairs={{4,0},{8,4},{12,8},{16,12},{20,16},{24,20},{28,24},{5,1},{9,5},{13... | collective-permute-start | bytes 786440 | tf_op jit(solution)/shard_map/ppermute | solution.py:593
  11.8 0.8 collective-permute-done.2
  12.6 1.0 select_bitcast_fusion.3
  13.6 7.7 %collective-permute-done.left = bf16[128,1024]{1,0:T(8,128)(2,1)S(1)} collective-permute-done((bf16[128,1024]{1,0:T(8,128)(2,1)S(1)}, bf16[128,1024]{1,0:T(8,128)(2,1)S(1)}, u32[]{:S(2)}, u32[]{:S(2)}) %collective-permute-start) | collective-permute-done | bytes 262176 | tf_op jit(solution)/shard_map/ppermute | solution.py:592
  21.4 3.4 %collective-permute-start.6 = (bf16[2,1040,128]{2,1,0:T(8,128)(2,1)S(1)}, bf16[2,1040,128]{2,1,0:T(8,128)(2,1)S(1)}, u32[]{:S(2)}, u32[]{:S(2)}) collective-permute-start(bf16[2,1040,128]{2,1,0:T(8,128)(2,1)S(1)} %pad_maximum_fusion.1.refs_0_.refs_1_), channel_id=1, source_target_pairs={{0,8},{9,1},{2,10},{11,3},{8,16},{17,9},{10,18},{19,11},{16,24},{2... | collective-permute-start | bytes 1597448 | tf_op jit(solution)/shard_map/ppermute | solution.py:535
  24.8 1.9 %collective-permute-start.4 = (bf16[2,1040,128]{2,1,0:T(8,128)(2,1)S(1)}, bf16[2,1040,128]{2,1,0:T(8,128)(2,1)}, u32[]{:S(2)}, u32[]{:S(2)}) collective-permute-start(bf16[2,1040,128]{2,1,0:T(8,128)(2,1)S(1)} %collective-permute-done.3.refs_1_.refs_2_), channel_id=1, source_target_pairs={{0,8},{9,1},{2,10},{11,3},{8,16},{17,9},{10,18},{19,11},{16,24},{2... | collective-permute-start | bytes 1597448 | tf_op jit(solution)/shard_map/ppermute | solution.py:535
  26.7 3.5 %prepare.1 = (bf16[512,1024]{1,0:T(8,128)(2,1)}, f32[2,128,384]{2,1,0:T(8,128)}, f32[256,256]{1,0:T(8,128)}) custom-call(bf16[128,1024]{1,0:T(8,128)(2,1)} %copy-done.21, bf16[256,1024]{1,0:T(8,128)(2,1)} %bitcast.29, bf16[128,1024]{1,0:T(8,128)(2,1)} %copy-done.22, f32[1,1024]{1,0:T(1,128)} %bitcast.37, s32[1,256]{1,0:T(1,128)} %bitcast.41, ...), custom_call_target="tpu_custom_call" | custom-call | flops 1000 | bytes 1000 | tf_op jit(solution)/shard_map/prepare/pallas_call | solution.py:117
  30.2 1.4 %collective-permute-done.6.refs_2_.refs_3_ = bf16[2,1040,128]{2,1,0:T(8,128)(2,1)S(1)} collective-permute-done((bf16[2,1040,128]{2,1,0:T(8,128)(2,1)S(1)}, bf16[2,1040,128]{2,1,0:T(8,128)(2,1)S(1)}, u32[]{:S(2)}, u32[]{:S(2)}) %collective-permute-start.6) | collective-permute-done | bytes 532512 | tf_op jit(solution)/shard_map/ppermute | solution.py:535
  31.6 2.5 %collective-permute-start.7 = (bf16[2,1040,128]{2,1,0:T(8,128)(2,1)S(1)}, bf16[2,1040,128]{2,1,0:T(8,128)(2,1)S(1)}, u32[]{:S(2)}, u32[]{:S(2)}) collective-permute-start(bf16[2,1040,128]{2,1,0:T(8,128)(2,1)S(1)} %collective-permute-done.6.refs_2_.refs_3_), channel_id=1, source_target_pairs={{0,8},{9,1},{2,10},{11,3},{8,16},{17,9},{10,18},{19,11},{16,24},{2... | collective-permute-start | bytes 1597448 | tf_op jit(solution)/shard_map/ppermute | solution.py:535
  34.1 3.2 %collective-permute-done.4.refs_4_.refs_5_ = bf16[2,1040,128]{2,1,0:T(8,128)(2,1)} collective-permute-done((bf16[2,1040,128]{2,1,0:T(8,128)(2,1)S(1)}, bf16[2,1040,128]{2,1,0:T(8,128)(2,1)}, u32[]{:S(2)}, u32[]{:S(2)}) %collective-permute-start.4) | collective-permute-done | bytes 532512 | tf_op jit(solution)/shard_map/ppermute | solution.py:535
  37.3 2.6 %collective-permute-start.5 = (bf16[2,1040,128]{2,1,0:T(8,128)(2,1)}, bf16[2,1040,128]{2,1,0:T(8,128)(2,1)S(1)}, u32[]{:S(2)}, u32[]{:S(2)}) collective-permute-start(bf16[2,1040,128]{2,1,0:T(8,128)(2,1)} %collective-permute-done.4.refs_4_.refs_5_), channel_id=1, source_target_pairs={{0,8},{9,1},{2,10},{11,3},{8,16},{17,9},{10,18},{19,11},{16,24},{2... | collective-permute-start | bytes 1597448 | tf_op jit(solution)/shard_map/ppermute | solution.py:535
  40.0 0.6 collective-permute-start.18
  40.6 0.5 collective-permute-start.15
  41.1 2.0 %collective-permute-done.7.refs_0_.refs_7_ = bf16[2,1040,128]{2,1,0:T(8,128)(2,1)S(1)} collective-permute-done((bf16[2,1040,128]{2,1,0:T(8,128)(2,1)S(1)}, bf16[2,1040,128]{2,1,0:T(8,128)(2,1)S(1)}, u32[]{:S(2)}, u32[]{:S(2)}) %collective-permute-start.7) | collective-permute-done | bytes 532512 | tf_op jit(solution)/shard_map/ppermute | solution.py:535
  43.0 2.5 %collective-permute-start.10 = (bf16[2,1040,128]{2,1,0:T(8,128)(2,1)S(1)}, bf16[2,1040,128]{2,1,0:T(8,128)(2,1)S(1)}, u32[]{:S(2)}, u32[]{:S(2)}) collective-permute-start(bf16[2,1040,128]{2,1,0:T(8,128)(2,1)S(1)} %collective-permute-done.7.refs_0_.refs_7_), channel_id=1, source_target_pairs={{0,8},{9,1},{2,10},{11,3},{8,16},{17,9},{10,18},{19,11},{16,24},{2... | collective-permute-start | bytes 1597448 | tf_op jit(solution)/shard_map/ppermute | solution.py:535
  45.5 3.3 %collective-permute-done.5.refs_2_.refs_9_ = bf16[2,1040,128]{2,1,0:T(8,128)(2,1)S(1)} collective-permute-done((bf16[2,1040,128]{2,1,0:T(8,128)(2,1)}, bf16[2,1040,128]{2,1,0:T(8,128)(2,1)S(1)}, u32[]{:S(2)}, u32[]{:S(2)}) %collective-permute-start.5) | collective-permute-done | bytes 532512 | tf_op jit(solution)/shard_map/ppermute | solution.py:535
  48.8 2.4 %collective-permute-start.12 = (bf16[2,1040,128]{2,1,0:T(8,128)(2,1)S(1)}, bf16[2,1040,128]{2,1,0:T(8,128)(2,1)S(1)}, u32[]{:S(2)}, u32[]{:S(2)}) collective-permute-start(bf16[2,1040,128]{2,1,0:T(8,128)(2,1)S(1)} %collective-permute-done.5.refs_2_.refs_9_), channel_id=1, source_target_pairs={{0,8},{9,1},{2,10},{11,3},{8,16},{17,9},{10,18},{19,11},{16,24},{2... | collective-permute-start | bytes 1597448 | tf_op jit(solution)/shard_map/ppermute | solution.py:535
  51.2 0.8 pad_maximum_fusion.2
  52.0 0.6 collective-permute-start.8
  52.6 0.2 copy-done.12
  52.8 0.8 copy-done.13
  53.6 0.5 collective-permute-start.9
  54.1 5.3 %project.1.refs_10_ = bf16[24,512,128]{2,1,0:T(8,128)(2,1)} custom-call(bf16[512,1024]{1,0:T(8,128)(2,1)} %get-tuple-element.25.normed, bf16[2,1040,128]{2,1,0:T(8,128)(2,1)} %copy-done, bf16[2,1040,128]{2,1,0:T(8,128)(2,1)} %copy-done.10, bf16[2,1040,128]{2,1,0:T(8,128)(2,1)} %copy-done.11, bf16[2,1040,128]{2,1,0:T(8,128)(2,1)} %copy-done.12, ...), custom_call_target="tpu_custom_call" | custom-call | flops 1000 | bytes 1000 | tf_op jit(solution)/shard_map/project/pallas_call | solution.py:274
  59.5 0.7 collective-permute-done.12.refs_6_.refs_13_
  60.1 2.5 %collective-permute-start.16 = (bf16[2,1040,128]{2,1,0:T(8,128)(2,1)S(1)}, bf16[2,1040,128]{2,1,0:T(8,128)(2,1)}, u32[]{:S(2)}, u32[]{:S(2)}) collective-permute-start(bf16[2,1040,128]{2,1,0:T(8,128)(2,1)S(1)} %collective-permute-done.10.refs_4_.refs_11_), channel_id=1, source_target_pairs={{0,8},{9,1},{2,10},{11,3},{8,16},{17,9},{10,18},{19,11},{16,24},{2... | collective-permute-start | bytes 1597448 | tf_op jit(solution)/shard_map/ppermute | solution.py:535
  62.6 1.0 select_bitcast_fusion.1
  63.7 1.6 %collective-permute-start.20 = (bf16[2,2,544,128]{3,2,1,0:T(8,128)(2,1)S(1)}, bf16[2,2,544,128]{3,2,1,0:T(8,128)(2,1)}, u32[]{:S(2)}, u32[]{:S(2)}) collective-permute-start(bf16[2,2,544,128]{3,2,1,0:T(8,128)(2,1)S(1)} %pad_maximum_fusion.refs_0_), channel_id=1, source_target_pairs={{0,8},{9,1},{2,10},{11,3},{8,16},{17,9},{10,18},{19,11},{16,24},{2... | collective-permute-start | bytes 1671176 | tf_op jit(solution)/shard_map/ppermute | solution.py:535
  65.4 0.5 collective-permute-start.13
  65.9 3.6 %collective-permute-done.16.refs_8_.refs_15_ = bf16[2,1040,128]{2,1,0:T(8,128)(2,1)} collective-permute-done((bf16[2,1040,128]{2,1,0:T(8,128)(2,1)S(1)}, bf16[2,1040,128]{2,1,0:T(8,128)(2,1)}, u32[]{:S(2)}, u32[]{:S(2)}) %collective-permute-start.16) | collective-permute-done | bytes 532512 | tf_op jit(solution)/shard_map/ppermute | solution.py:535
  69.5 5.9 %collective-permute-done.20.refs_1_ = bf16[2,2,544,128]{3,2,1,0:T(8,128)(2,1)} collective-permute-done((bf16[2,2,544,128]{3,2,1,0:T(8,128)(2,1)S(1)}, bf16[2,2,544,128]{3,2,1,0:T(8,128)(2,1)}, u32[]{:S(2)}, u32[]{:S(2)}) %collective-permute-start.20) | collective-permute-done | bytes 557088 | tf_op jit(solution)/shard_map/ppermute | solution.py:535
  75.5 2.5 %collective-permute-start.22 = (bf16[2,2,544,128]{3,2,1,0:T(8,128)(2,1)}, bf16[2,2,544,128]{3,2,1,0:T(8,128)(2,1)}, u32[]{:S(2)}, u32[]{:S(2)}) collective-permute-start(bf16[2,2,544,128]{3,2,1,0:T(8,128)(2,1)} %collective-permute-done.20.refs_1_), channel_id=1, source_target_pairs={{0,8},{9,1},{2,10},{11,3},{8,16},{17,9},{10,18},{19,11},{16,24},{2... | collective-permute-start | bytes 1671176 | tf_op jit(solution)/shard_map/ppermute | solution.py:535
  78.0 10.9 %attend.1.refs_0_ = bf16[256,1024]{1,0:T(8,128)(2,1)} custom-call(bf16[512,1024]{1,0:T(8,128)(2,1)} %get-tuple-element.25.normed, f32[2,128,384]{2,1,0:T(8,128)} %get-tuple-element.26.bias, bf16[2,1040,128]{2,1,0:T(8,128)(2,1)} %copy-done.2, bf16[2,1040,128]{2,1,0:T(8,128)(2,1)} %copy-done.6, bf16[2,1040,128]{2,1,0:T(8,128)(2,1)} %copy-done.3, ...), custom_call_target="tpu_custom_call" | custom-call | flops 1000 | bytes 1000 | tf_op jit(solution)/shard_map/attend/pallas_call | solution.py:332
  88.9 1.6 %collective-permute-start.24 = (bf16[2,2,544,128]{3,2,1,0:T(8,128)(2,1)}, bf16[2,2,544,128]{3,2,1,0:T(8,128)(2,1)S(1)}, u32[]{:S(2)}, u32[]{:S(2)}) collective-permute-start(bf16[2,2,544,128]{3,2,1,0:T(8,128)(2,1)} %collective-permute-done.22.refs_3_), channel_id=1, source_target_pairs={{0,8},{9,1},{2,10},{11,3},{8,16},{17,9},{10,18},{19,11},{16,24},{2... | collective-permute-start | bytes 1671176 | tf_op jit(solution)/shard_map/ppermute | solution.py:535
  90.6 5.1 %mix.1 = (bf16[256,1024]{1,0:T(8,128)(2,1)}, bf16[128,1024]{1,0:T(8,128)(2,1)}) custom-call(bf16[256,1024]{1,0:T(8,128)(2,1)} %bitcast.30, f32[1,1024]{1,0:T(1,128)} %bitcast.38, bf16[256,1024]{1,0:T(8,128)(2,1)} %attend.1.refs_0_, bf16[2,1040,128]{2,1,0:T(8,128)(2,1)} %copy-done, bf16[2,1040,128]{2,1,0:T(8,128)(2,1)} %copy-done.10, ...), custom_call_target="tpu_custom_call" | custom-call | flops 1000 | bytes 1000 | tf_op jit(solution)/shard_map/mix/pallas_call | solution.py:412
  95.7 0.6 collective-permute-start.23
  96.3 2.5 %collective-permute-done.24.refs_5_ = bf16[2,2,544,128]{3,2,1,0:T(8,128)(2,1)S(1)} collective-permute-done((bf16[2,2,544,128]{3,2,1,0:T(8,128)(2,1)}, bf16[2,2,544,128]{3,2,1,0:T(8,128)(2,1)S(1)}, u32[]{:S(2)}, u32[]{:S(2)}) %collective-permute-start.24) | collective-permute-done | bytes 557088 | tf_op jit(solution)/shard_map/ppermute | solution.py:535
  98.7 1.6 %collective-permute-start.26 = (bf16[2,544,128]{2,1,0:T(8,128)(2,1)S(1)}, bf16[2,544,128]{2,1,0:T(8,128)(2,1)S(1)}, u32[]{:S(2)}, u32[]{:S(2)}) collective-permute-start(bf16[2,544,128]{2,1,0:T(8,128)(2,1)S(1)} %dynamic-slice_bitcast_fusion), channel_id=1, source_target_pairs={{0,8},{9,1},{2,10},{11,3},{8,16},{17,9},{10,18},{19,11},{16,24},{2... | collective-permute-start | bytes 835592 | tf_op jit(solution)/shard_map/ppermute | solution.py:535
  100.4 3.6 %all-to-all-start = ((bf16[8,16,1024]{2,1,0:T(8,128)(2,1)}), bf16[8,16,1024]{2,1,0:T(8,128)(2,1)S(1)}, u32[]{:S(2)}, u32[]{:S(2)}) async-start(bf16[8,16,1024]{2,1,0:T(8,128)(2,1)} %bitcast.33), calls=%async_computation | async-start | bytes 524288 | tf_op jit(solution)/shard_map/all_to_all | solution.py:645
  104.0 1.3 %collective-permute-done.26.refs_7_ = bf16[2,544,128]{2,1,0:T(8,128)(2,1)S(1)} collective-permute-done((bf16[2,544,128]{2,1,0:T(8,128)(2,1)S(1)}, bf16[2,544,128]{2,1,0:T(8,128)(2,1)S(1)}, u32[]{:S(2)}, u32[]{:S(2)}) %collective-permute-start.26) | collective-permute-done | bytes 278560 | tf_op jit(solution)/shard_map/ppermute | solution.py:535
  105.4 8.2 %all-to-all-done = bf16[8,16,1024]{2,1,0:T(8,128)(2,1)S(1)} async-done(((bf16[8,16,1024]{2,1,0:T(8,128)(2,1)}), bf16[8,16,1024]{2,1,0:T(8,128)(2,1)S(1)}, u32[]{:S(2)}, u32[]{:S(2)}) %all-to-all-start) | async-done | bytes 262176 | tf_op jit(solution)/shard_map/all_to_all | solution.py:645
  113.7 0.6 copy-done.15
  114.3 0.2 copy-done.17
  114.5 0.2 copy-done.18
  114.8 10.9 %decode.1 = bf16[96,256]{1,0:T(8,128)(2,1)} custom-call(bf16[256,1024]{1,0:T(8,128)(2,1)} %bitcast.32, bf16[256,1024]{1,0:T(8,128)(2,1)} %get-tuple-element.28.decoded, bf16[128,1024]{1,0:T(8,128)(2,1)} %bitcast.31, f32[256,256]{1,0:T(8,128)} %get-tuple-element.30.here, f32[256,128]{1,0:T(8,128)} %get-tuple-element.31.there, ...), custom_call_target="tpu_custom_call" | custom-call | flops 1000 | bytes 1000 | tf_op jit(solution)/shard_map/decode/pallas_call | solution.py:490
  (77 shorter events, 0.4 us)
Async XLA Ops:
  0.0 39.9 %copy-start.24 = (bf16[256,12]{0,1:T(8,128)(2,1)S(1)}, bf16[256,12]{0,1:T(8,128)(2,1)}, u32[]{:S(2)}) copy-start(bf16[256,12]{0,1:T(8,128)(2,1)} %param.20) | copy-start | bytes 18436
  0.0 39.9 %copy-start.23 = (bf16[256,256]{1,0:T(8,128)(2,1)S(1)}, bf16[256,256]{1,0:T(8,128)(2,1)}, u32[]{:S(2)}) copy-start(bf16[256,256]{1,0:T(8,128)(2,1)} %param.19) | copy-start | bytes 393220
  3.0 9.5 %collective-permute-start.2 = (bf16[1040,128]{1,0:T(8,128)(2,1)}, bf16[1040,128]{1,0:T(8,128)(2,1)S(1)}, u32[]{:S(2)}, u32[]{:S(2)}) collective-permute-start(bf16[1040,128]{1,0:T(8,128)(2,1)} %get-tuple-element.22), channel_id=1, source_target_pairs={{0,2},{1,3},{2,0},{3,1},{4,6},{5,7},{6,4},{7,5},{8,10},{9,11},{10,... | collective-permute-start | bytes 798728 | tf_op jit(solution)/shard_map/ppermute | solution.py:517
  7.1 14.3 %collective-permute-start = (bf16[128,1024]{1,0:T(8,128)(2,1)S(1)}, bf16[128,1024]{1,0:T(8,128)(2,1)S(1)}, u32[]{:S(2)}, u32[]{:S(2)}) collective-permute-start(bf16[128,1024]{1,0:T(8,128)(2,1)S(1)} %get-tuple-element.42), channel_id=1, source_target_pairs={{0,4},{4,8},{8,12},{12,16},{16,20},{20,24},{24,28},{1,5},{5,9},{9,... | collective-permute-start | bytes 786440 | tf_op jit(solution)/shard_map/ppermute | solution.py:592
  10.5 10.9 %collective-permute-start.1 = (bf16[128,1024]{1,0:T(8,128)(2,1)S(1)}, bf16[128,1024]{1,0:T(8,128)(2,1)S(1)}, u32[]{:S(2)}, u32[]{:S(2)}) collective-permute-start(bf16[128,1024]{1,0:T(8,128)(2,1)S(1)} %get-tuple-element.41), channel_id=1, source_target_pairs={{4,0},{8,4},{12,8},{16,12},{20,16},{24,20},{28,24},{5,1},{9,5},{13... | collective-permute-start | bytes 786440 | tf_op jit(solution)/shard_map/ppermute | solution.py:593
  13.6 40.5 %copy-start = (bf16[2,1040,128]{2,1,0:T(8,128)(2,1)}, bf16[2,1040,128]{2,1,0:T(8,128)(2,1)S(1)}, u32[]{:S(2)}) copy-start(bf16[2,1040,128]{2,1,0:T(8,128)(2,1)S(1)} %pad_maximum_fusion.1.refs_0_.refs_1_) | copy-start | bytes 1597444
  21.4 5.4 %copy-start.21 = (bf16[128,1024]{1,0:T(8,128)(2,1)}, bf16[128,1024]{1,0:T(8,128)(2,1)S(1)}, u32[]{:S(2)}) copy-start(bf16[128,1024]{1,0:T(8,128)(2,1)S(1)} %collective-permute-done.left) | copy-start | bytes 786436
  21.4 5.4 %copy-start.22 = (bf16[128,1024]{1,0:T(8,128)(2,1)}, bf16[128,1024]{1,0:T(8,128)(2,1)S(1)}, u32[]{:S(2)}) copy-start(bf16[128,1024]{1,0:T(8,128)(2,1)S(1)} %collective-permute-done.1.right) | copy-start | bytes 786436
  21.4 3.4 %collective-permute-start.3 = (bf16[2,1040,128]{2,1,0:T(8,128)(2,1)S(1)}, bf16[2,1040,128]{2,1,0:T(8,128)(2,1)S(1)}, u32[]{:S(2)}, u32[]{:S(2)}) collective-permute-start(bf16[2,1040,128]{2,1,0:T(8,128)(2,1)S(1)} %pad_maximum_fusion.1.refs_0_.refs_1_), channel_id=1, source_target_pairs={{0,1},{1,0},{2,3},{3,2},{4,5},{5,4},{6,7},{7,6},{8,9},{9,8},{10,11... | collective-permute-start | bytes 1597448 | tf_op jit(solution)/shard_map/ppermute | solution.py:539
  21.4 10.2 %collective-permute-start.6 = (bf16[2,1040,128]{2,1,0:T(8,128)(2,1)S(1)}, bf16[2,1040,128]{2,1,0:T(8,128)(2,1)S(1)}, u32[]{:S(2)}, u32[]{:S(2)}) collective-permute-start(bf16[2,1040,128]{2,1,0:T(8,128)(2,1)S(1)} %pad_maximum_fusion.1.refs_0_.refs_1_), channel_id=1, source_target_pairs={{0,8},{9,1},{2,10},{11,3},{8,16},{17,9},{10,18},{19,11},{16,24},{2... | collective-permute-start | bytes 1597448 | tf_op jit(solution)/shard_map/ppermute | solution.py:535
  24.8 29.3 %copy-start.10 = (bf16[2,1040,128]{2,1,0:T(8,128)(2,1)}, bf16[2,1040,128]{2,1,0:T(8,128)(2,1)S(1)}, u32[]{:S(2)}) copy-start(bf16[2,1040,128]{2,1,0:T(8,128)(2,1)S(1)} %collective-permute-done.3.refs_1_.refs_2_) | copy-start | bytes 1597444
  24.8 12.5 %collective-permute-start.4 = (bf16[2,1040,128]{2,1,0:T(8,128)(2,1)S(1)}, bf16[2,1040,128]{2,1,0:T(8,128)(2,1)}, u32[]{:S(2)}, u32[]{:S(2)}) collective-permute-start(bf16[2,1040,128]{2,1,0:T(8,128)(2,1)S(1)} %collective-permute-done.3.refs_1_.refs_2_), channel_id=1, source_target_pairs={{0,8},{9,1},{2,10},{11,3},{8,16},{17,9},{10,18},{19,11},{16,24},{2... | collective-permute-start | bytes 1597448 | tf_op jit(solution)/shard_map/ppermute | solution.py:535
  31.6 20.4 %copy-start.11 = (bf16[2,1040,128]{2,1,0:T(8,128)(2,1)}, bf16[2,1040,128]{2,1,0:T(8,128)(2,1)S(1)}, u32[]{:S(2)}) copy-start(bf16[2,1040,128]{2,1,0:T(8,128)(2,1)S(1)} %collective-permute-done.6.refs_2_.refs_3_) | copy-start | bytes 1597444
  31.6 11.4 %collective-permute-start.7 = (bf16[2,1040,128]{2,1,0:T(8,128)(2,1)S(1)}, bf16[2,1040,128]{2,1,0:T(8,128)(2,1)S(1)}, u32[]{:S(2)}, u32[]{:S(2)}) collective-permute-start(bf16[2,1040,128]{2,1,0:T(8,128)(2,1)S(1)} %collective-permute-done.6.refs_2_.refs_3_), channel_id=1, source_target_pairs={{0,8},{9,1},{2,10},{11,3},{8,16},{17,9},{10,18},{19,11},{16,24},{2... | collective-permute-start | bytes 1597448 | tf_op jit(solution)/shard_map/ppermute | solution.py:535
  37.3 11.5 %collective-permute-start.5 = (bf16[2,1040,128]{2,1,0:T(8,128)(2,1)}, bf16[2,1040,128]{2,1,0:T(8,128)(2,1)S(1)}, u32[]{:S(2)}, u32[]{:S(2)}) collective-permute-start(bf16[2,1040,128]{2,1,0:T(8,128)(2,1)} %collective-permute-done.4.refs_4_.refs_5_), channel_id=1, source_target_pairs={{0,8},{9,1},{2,10},{11,3},{8,16},{17,9},{10,18},{19,11},{16,24},{2... | collective-permute-start | bytes 1597448 | tf_op jit(solution)/shard_map/ppermute | solution.py:535
  40.0 11.3 %collective-permute-start.18 = (bf16[544,128]{1,0:T(8,128)(2,1)S(1)}, bf16[544,128]{1,0:T(8,128)(2,1)S(1)}, u32[]{:S(2)}, u32[]{:S(2)}) collective-permute-start(bf16[544,128]{1,0:T(8,128)(2,1)S(1)} %pad_maximum_fusion.3), channel_id=1, source_target_pairs={{0,2},{1,3},{2,0},{3,1},{4,6},{5,7},{6,4},{7,5},{8,10},{9,11},{10,... | collective-permute-start | bytes 417800 | tf_op jit(solution)/shard_map/ppermute | solution.py:517
  40.6 11.4 %collective-permute-start.14 = (bf16[2,1040,128]{2,1,0:T(8,128)(2,1)S(1)}, bf16[2,1040,128]{2,1,0:T(8,128)(2,1)S(1)}, u32[]{:S(2)}, u32[]{:S(2)}) collective-permute-start(bf16[2,1040,128]{2,1,0:T(8,128)(2,1)S(1)} %collective-permute-done.6.refs_2_.refs_3_), channel_id=1, source_target_pairs={{0,1},{1,0},{2,3},{3,2},{4,5},{5,4},{6,7},{7,6},{8,9},{9,8},{10,11... | collective-permute-start | bytes 1597448 | tf_op jit(solution)/shard_map/ppermute | solution.py:539
  40.6 12.3 %collective-permute-start.15 = (bf16[2,1040,128]{2,1,0:T(8,128)(2,1)}, bf16[2,1040,128]{2,1,0:T(8,128)(2,1)S(1)}, u32[]{:S(2)}, u32[]{:S(2)}) collective-permute-start(bf16[2,1040,128]{2,1,0:T(8,128)(2,1)} %collective-permute-done.4.refs_4_.refs_5_), channel_id=1, source_target_pairs={{0,1},{1,0},{2,3},{3,2},{4,5},{5,4},{6,7},{7,6},{8,9},{9,8},{10,11... | collective-permute-start | bytes 1597448 | tf_op jit(solution)/shard_map/ppermute | solution.py:539
  43.0 16.4 %copy-start.2 = (bf16[2,1040,128]{2,1,0:T(8,128)(2,1)}, bf16[2,1040,128]{2,1,0:T(8,128)(2,1)S(1)}, u32[]{:S(2)}) copy-start(bf16[2,1040,128]{2,1,0:T(8,128)(2,1)S(1)} %collective-permute-done.7.refs_0_.refs_7_) | copy-start | bytes 1597444
  43.0 16.4 %collective-permute-start.10 = (bf16[2,1040,128]{2,1,0:T(8,128)(2,1)S(1)}, bf16[2,1040,128]{2,1,0:T(8,128)(2,1)S(1)}, u32[]{:S(2)}, u32[]{:S(2)}) collective-permute-start(bf16[2,1040,128]{2,1,0:T(8,128)(2,1)S(1)} %collective-permute-done.7.refs_0_.refs_7_), channel_id=1, source_target_pairs={{0,8},{9,1},{2,10},{11,3},{8,16},{17,9},{10,18},{19,11},{16,24},{2... | collective-permute-start | bytes 1597448 | tf_op jit(solution)/shard_map/ppermute | solution.py:535
  48.8 10.6 %copy-start.3 = (bf16[2,1040,128]{2,1,0:T(8,128)(2,1)}, bf16[2,1040,128]{2,1,0:T(8,128)(2,1)S(1)}, u32[]{:S(2)}) copy-start(bf16[2,1040,128]{2,1,0:T(8,128)(2,1)S(1)} %collective-permute-done.5.refs_2_.refs_9_) | copy-start | bytes 1597444
  48.8 11.3 %collective-permute-start.12 = (bf16[2,1040,128]{2,1,0:T(8,128)(2,1)S(1)}, bf16[2,1040,128]{2,1,0:T(8,128)(2,1)S(1)}, u32[]{:S(2)}, u32[]{:S(2)}) collective-permute-start(bf16[2,1040,128]{2,1,0:T(8,128)(2,1)S(1)} %collective-permute-done.5.refs_2_.refs_9_), channel_id=1, source_target_pairs={{0,8},{9,1},{2,10},{11,3},{8,16},{17,9},{10,18},{19,11},{16,24},{2... | collective-permute-start | bytes 1597448 | tf_op jit(solution)/shard_map/ppermute | solution.py:535
  52.0 10.6 %collective-permute-start.19 = (bf16[2,544,128]{2,1,0:T(8,128)(2,1)}, bf16[2,544,128]{2,1,0:T(8,128)(2,1)}, u32[]{:S(2)}, u32[]{:S(2)}) collective-permute-start(bf16[2,544,128]{2,1,0:T(8,128)(2,1)} %pad_maximum_fusion.2), channel_id=1, source_target_pairs={{0,1},{1,0},{2,3},{3,2},{4,5},{5,4},{6,7},{7,6},{8,9},{9,8},{10,11... | collective-permute-start | bytes 835592 | tf_op jit(solution)/shard_map/ppermute | solution.py:539
  52.0 11.7 %collective-permute-start.8 = (bf16[2,1040,128]{2,1,0:T(8,128)(2,1)S(1)}, bf16[2,1040,128]{2,1,0:T(8,128)(2,1)S(1)}, u32[]{:S(2)}, u32[]{:S(2)}) collective-permute-start(bf16[2,1040,128]{2,1,0:T(8,128)(2,1)S(1)} %collective-permute-done.7.refs_0_.refs_7_), channel_id=1, source_target_pairs={{0,1},{1,0},{2,3},{3,2},{4,5},{5,4},{6,7},{7,6},{8,9},{9,8},{10,11... | collective-permute-start | bytes 1597448 | tf_op jit(solution)/shard_map/ppermute | solution.py:539
  53.6 10.1 %collective-permute-start.9 = (bf16[2,1040,128]{2,1,0:T(8,128)(2,1)S(1)}, bf16[2,1040,128]{2,1,0:T(8,128)(2,1)}, u32[]{:S(2)}, u32[]{:S(2)}) collective-permute-start(bf16[2,1040,128]{2,1,0:T(8,128)(2,1)S(1)} %collective-permute-done.5.refs_2_.refs_9_), channel_id=1, source_target_pairs={{0,1},{1,0},{2,3},{3,2},{4,5},{5,4},{6,7},{7,6},{8,9},{9,8},{10,11... | collective-permute-start | bytes 1597448 | tf_op jit(solution)/shard_map/ppermute | solution.py:539
  59.5 18.5 %copy-start.4 = (bf16[2,1040,128]{2,1,0:T(8,128)(2,1)}, bf16[2,1040,128]{2,1,0:T(8,128)(2,1)S(1)}, u32[]{:S(2)}) copy-start(bf16[2,1040,128]{2,1,0:T(8,128)(2,1)S(1)} %collective-permute-done.10.refs_4_.refs_11_) | copy-start | bytes 1597444
  60.1 17.8 %copy-start.5 = (bf16[2,1040,128]{2,1,0:T(8,128)(2,1)}, bf16[2,1040,128]{2,1,0:T(8,128)(2,1)S(1)}, u32[]{:S(2)}) copy-start(bf16[2,1040,128]{2,1,0:T(8,128)(2,1)S(1)} %collective-permute-done.12.refs_6_.refs_13_) | copy-start | bytes 1597444
  60.1 9.4 %collective-permute-start.16 = (bf16[2,1040,128]{2,1,0:T(8,128)(2,1)S(1)}, bf16[2,1040,128]{2,1,0:T(8,128)(2,1)}, u32[]{:S(2)}, u32[]{:S(2)}) collective-permute-start(bf16[2,1040,128]{2,1,0:T(8,128)(2,1)S(1)} %collective-permute-done.10.refs_4_.refs_11_), channel_id=1, source_target_pairs={{0,8},{9,1},{2,10},{11,3},{8,16},{17,9},{10,18},{19,11},{16,24},{2... | collective-permute-start | bytes 1597448 | tf_op jit(solution)/shard_map/ppermute | solution.py:535
  63.7 25.2 %copy-start.1 = (bf16[2,2,544,128]{3,2,1,0:T(8,128)(2,1)}, bf16[2,2,544,128]{3,2,1,0:T(8,128)(2,1)S(1)}, u32[]{:S(2)}) copy-start(bf16[2,2,544,128]{3,2,1,0:T(8,128)(2,1)S(1)} %pad_maximum_fusion.refs_0_) | copy-start | bytes 1671172
  63.7 14.3 %copy-start.6 = (bf16[2,1040,128]{2,1,0:T(8,128)(2,1)}, bf16[2,1040,128]{2,1,0:T(8,128)(2,1)S(1)}, u32[]{:S(2)}) copy-start(bf16[2,1040,128]{2,1,0:T(8,128)(2,1)S(1)} %collective-permute-done.8.refs_1_.refs_8_) | copy-start | bytes 1597444
  63.7 11.8 %collective-permute-start.20 = (bf16[2,2,544,128]{3,2,1,0:T(8,128)(2,1)S(1)}, bf16[2,2,544,128]{3,2,1,0:T(8,128)(2,1)}, u32[]{:S(2)}, u32[]{:S(2)}) collective-permute-start(bf16[2,2,544,128]{3,2,1,0:T(8,128)(2,1)S(1)} %pad_maximum_fusion.refs_0_), channel_id=1, source_target_pairs={{0,8},{9,1},{2,10},{11,3},{8,16},{17,9},{10,18},{19,11},{16,24},{2... | collective-permute-start | bytes 1671176 | tf_op jit(solution)/shard_map/ppermute | solution.py:535
  65.4 4.2 %collective-permute-start.11 = (bf16[2,1040,128]{2,1,0:T(8,128)(2,1)S(1)}, bf16[2,1040,128]{2,1,0:T(8,128)(2,1)S(1)}, u32[]{:S(2)}, u32[]{:S(2)}) collective-permute-start(bf16[2,1040,128]{2,1,0:T(8,128)(2,1)S(1)} %collective-permute-done.10.refs_4_.refs_11_), channel_id=1, source_target_pairs={{0,1},{1,0},{2,3},{3,2},{4,5},{5,4},{6,7},{7,6},{8,9},{9,8},{10,11... | collective-permute-start | bytes 1597448 | tf_op jit(solution)/shard_map/ppermute | solution.py:539
  65.4 4.2 %collective-permute-start.13 = (bf16[2,1040,128]{2,1,0:T(8,128)(2,1)S(1)}, bf16[2,1040,128]{2,1,0:T(8,128)(2,1)S(1)}, u32[]{:S(2)}, u32[]{:S(2)}) collective-permute-start(bf16[2,1040,128]{2,1,0:T(8,128)(2,1)S(1)} %collective-permute-done.12.refs_6_.refs_13_), channel_id=1, source_target_pairs={{0,1},{1,0},{2,3},{3,2},{4,5},{5,4},{6,7},{7,6},{8,9},{9,8},{10,11... | collective-permute-start | bytes 1597448 | tf_op jit(solution)/shard_map/ppermute | solution.py:539
  69.5 6.0 %collective-permute-start.17 = (bf16[2,1040,128]{2,1,0:T(8,128)(2,1)}, bf16[2,1040,128]{2,1,0:T(8,128)(2,1)S(1)}, u32[]{:S(2)}, u32[]{:S(2)}) collective-permute-start(bf16[2,1040,128]{2,1,0:T(8,128)(2,1)} %collective-permute-done.16.refs_8_.refs_15_), channel_id=1, source_target_pairs={{0,1},{1,0},{2,3},{3,2},{4,5},{5,4},{6,7},{7,6},{8,9},{9,8},{10,11... | collective-permute-start | bytes 1597448 | tf_op jit(solution)/shard_map/ppermute | solution.py:539
  69.5 8.5 %copy-start.7 = (bf16[2,1040,128]{2,1,0:T(8,128)(2,1)}, bf16[2,1040,128]{2,1,0:T(8,128)(2,1)S(1)}, u32[]{:S(2)}) copy-start(bf16[2,1040,128]{2,1,0:T(8,128)(2,1)S(1)} %collective-permute-done.11.refs_5_.refs_12_) | copy-start | bytes 1597444
  69.5 8.5 %copy-start.8 = (bf16[2,1040,128]{2,1,0:T(8,128)(2,1)}, bf16[2,1040,128]{2,1,0:T(8,128)(2,1)S(1)}, u32[]{:S(2)}) copy-start(bf16[2,1040,128]{2,1,0:T(8,128)(2,1)S(1)} %collective-permute-done.13.refs_7_.refs_14_) | copy-start | bytes 1597444
  75.5 2.5 %copy-start.9 = (bf16[2,1040,128]{2,1,0:T(8,128)(2,1)}, bf16[2,1040,128]{2,1,0:T(8,128)(2,1)S(1)}, u32[]{:S(2)}) copy-start(bf16[2,1040,128]{2,1,0:T(8,128)(2,1)S(1)} %collective-permute-done.17.refs_9_.refs_16_) | copy-start | bytes 1597444
  75.5 13.4 %collective-permute-start.22 = (bf16[2,2,544,128]{3,2,1,0:T(8,128)(2,1)}, bf16[2,2,544,128]{3,2,1,0:T(8,128)(2,1)}, u32[]{:S(2)}, u32[]{:S(2)}) collective-permute-start(bf16[2,2,544,128]{3,2,1,0:T(8,128)(2,1)} %collective-permute-done.20.refs_1_), channel_id=1, source_target_pairs={{0,8},{9,1},{2,10},{11,3},{8,16},{17,9},{10,18},{19,11},{16,24},{2... | collective-permute-start | bytes 1671176 | tf_op jit(solution)/shard_map/ppermute | solution.py:535
  88.9 9.8 %collective-permute-start.24 = (bf16[2,2,544,128]{3,2,1,0:T(8,128)(2,1)}, bf16[2,2,544,128]{3,2,1,0:T(8,128)(2,1)S(1)}, u32[]{:S(2)}, u32[]{:S(2)}) collective-permute-start(bf16[2,2,544,128]{3,2,1,0:T(8,128)(2,1)} %collective-permute-done.22.refs_3_), channel_id=1, source_target_pairs={{0,8},{9,1},{2,10},{11,3},{8,16},{17,9},{10,18},{19,11},{16,24},{2... | collective-permute-start | bytes 1671176 | tf_op jit(solution)/shard_map/ppermute | solution.py:535
  90.6 14.8 %collective-permute-start.21 = (bf16[2,2,544,128]{3,2,1,0:T(8,128)(2,1)}, bf16[2,2,544,128]{3,2,1,0:T(8,128)(2,1)S(1)}, u32[]{:S(2)}, u32[]{:S(2)}) collective-permute-start(bf16[2,2,544,128]{3,2,1,0:T(8,128)(2,1)} %collective-permute-done.20.refs_1_), channel_id=1, source_target_pairs={{0,1},{1,0},{2,3},{3,2},{4,5},{5,4},{6,7},{7,6},{8,9},{9,8},{10,11... | collective-permute-start | bytes 1671176 | tf_op jit(solution)/shard_map/ppermute | solution.py:539
  95.7 17.9 %collective-permute-start.23 = (bf16[2,2,544,128]{3,2,1,0:T(8,128)(2,1)}, bf16[2,2,544,128]{3,2,1,0:T(8,128)(2,1)S(1)}, u32[]{:S(2)}, u32[]{:S(2)}) collective-permute-start(bf16[2,2,544,128]{3,2,1,0:T(8,128)(2,1)} %collective-permute-done.22.refs_3_), channel_id=1, source_target_pairs={{0,1},{1,0},{2,3},{3,2},{4,5},{5,4},{6,7},{7,6},{8,9},{9,8},{10,11... | collective-permute-start | bytes 1671176 | tf_op jit(solution)/shard_map/ppermute | solution.py:539
  98.7 14.9 %copy-start.14 = (bf16[2,2,544,128]{3,2,1,0:T(8,128)(2,1)}, bf16[2,2,544,128]{3,2,1,0:T(8,128)(2,1)S(1)}, u32[]{:S(2)}) copy-start(bf16[2,2,544,128]{3,2,1,0:T(8,128)(2,1)S(1)} %collective-permute-done.24.refs_5_) | copy-start | bytes 1671172
  98.7 6.6 %collective-permute-start.26 = (bf16[2,544,128]{2,1,0:T(8,128)(2,1)S(1)}, bf16[2,544,128]{2,1,0:T(8,128)(2,1)S(1)}, u32[]{:S(2)}, u32[]{:S(2)}) collective-permute-start(bf16[2,544,128]{2,1,0:T(8,128)(2,1)S(1)} %dynamic-slice_bitcast_fusion), channel_id=1, source_target_pairs={{0,8},{9,1},{2,10},{11,3},{8,16},{17,9},{10,18},{19,11},{16,24},{2... | collective-permute-start | bytes 835592 | tf_op jit(solution)/shard_map/ppermute | solution.py:535
  100.4 13.2 %collective-permute-start.25 = (bf16[2,2,544,128]{3,2,1,0:T(8,128)(2,1)S(1)}, bf16[2,2,544,128]{3,2,1,0:T(8,128)(2,1)S(1)}, u32[]{:S(2)}, u32[]{:S(2)}) collective-permute-start(bf16[2,2,544,128]{3,2,1,0:T(8,128)(2,1)S(1)} %collective-permute-done.24.refs_5_), channel_id=1, source_target_pairs={{0,1},{1,0},{2,3},{3,2},{4,5},{5,4},{6,7},{7,6},{8,9},{9,8},{10,11... | collective-permute-start | bytes 1671176 | tf_op jit(solution)/shard_map/ppermute | solution.py:539
  100.4 13.2 %all-to-all-start = ((bf16[8,16,1024]{2,1,0:T(8,128)(2,1)}), bf16[8,16,1024]{2,1,0:T(8,128)(2,1)S(1)}, u32[]{:S(2)}, u32[]{:S(2)}) async-start(bf16[8,16,1024]{2,1,0:T(8,128)(2,1)} %bitcast.33), calls=%async_computation | async-start | bytes 524288 | tf_op jit(solution)/shard_map/all_to_all | solution.py:645
  105.3 8.3 %copy-start.19 = (bf16[2,544,128]{2,1,0:T(8,128)(2,1)}, bf16[2,544,128]{2,1,0:T(8,128)(2,1)S(1)}, u32[]{:S(2)}) copy-start(bf16[2,544,128]{2,1,0:T(8,128)(2,1)S(1)} %collective-permute-done.26.refs_7_) | copy-start | bytes 835588
  105.3 8.3 %collective-permute-start.27 = (bf16[2,544,128]{2,1,0:T(8,128)(2,1)S(1)}, bf16[2,544,128]{2,1,0:T(8,128)(2,1)S(1)}, u32[]{:S(2)}, u32[]{:S(2)}) collective-permute-start(bf16[2,544,128]{2,1,0:T(8,128)(2,1)S(1)} %collective-permute-done.26.refs_7_), channel_id=1, source_target_pairs={{0,1},{1,0},{2,3},{3,2},{4,5},{5,4},{6,7},{7,6},{8,9},{9,8},{10,11... | collective-permute-start | bytes 835592 | tf_op jit(solution)/shard_map/ppermute | solution.py:539
  105.4 8.3 %copy-start.16 = (bf16[2,2,544,128]{3,2,1,0:T(8,128)(2,1)}, bf16[2,2,544,128]{3,2,1,0:T(8,128)(2,1)S(1)}, u32[]{:S(2)}) copy-start(bf16[2,2,544,128]{3,2,1,0:T(8,128)(2,1)S(1)} %collective-permute-done.21.refs_2_) | copy-start | bytes 1671172
  (6 other events, 5.4 us)
where the time goes:
time: 126 us
  waiting for transfers between devices  40.7 us (32%)
  starting transfers between devices  39.7 us (32%)
  Pallas kernels  38.7 us (31%)
  local copies, waits for them, and re-layouts  3.33 us (3%)
  other arithmetic  2.88 us (2%)
    ppermute x11, starting transfers between devices, carry(): return lax.ppermute(block, ('seq', 'band'), pairs)  25.1 us
    ppermute x11, waiting for transfers between devices, carry(): return lax.ppermute(block, ('seq', 'band'), pairs)  23.9 us
    pallas_call x1, Pallas kernels, attend(): pl.pallas_call(functools.partial(attend_kernel, layout, ready, riding), o...  10.9 us
    pallas_call x1, Pallas kernels, decode(): pl.pallas_call(functools.partial(decode_kernel, layout, outputs // GROUPS...  10.9 us
    all_to_all x1, waiting for transfers between devices, local(): lax.all_to_all(found.reshape(shards, SLOTS, width), 'seq', split_axis=0,...  8.24 us
    ppermute x1, waiting for transfers between devices, local(): left = lax.ppermute(states[tok - HALF:], 'seq', up)  7.72 us
    pallas_call x1, Pallas kernels, project(): pl.pallas_call(functools.partial(project_kernel, layout, riding), out_sha...  5.29 us
    pallas_call x1, Pallas kernels, mix(): pl.pallas_call(functools.partial(mix_kernel, layout, ids is None), out_sh...  5.12 us
  transfers between devices with their start and end apart: 29, of which 12 were waited for; matrix products, arithmetic and copies ran while one was open for 3% of the time, Pallas kernels for 20%

commit v1 on v0

--- a/solution.py
+++ b/solution.py
@@ -557,10 +557,11 @@
     return block, [(block, (step, None)), (swap_core(block), (GROUPS - step, None))]
 
 
-def last_step(block):
+def last_step(block, gate):
     half = lax.dynamic_index_in_dim(block, lax.axis_index("band") % 2, 0, keepdims=False)
     half = carry(half)
-    return [(half, (GROUPS // 2, 0)), (swap_core(half), (GROUPS // 2, 1))]
+    handed, _ = lax.optimization_barrier((half, gate))
+    return [(half, (GROUPS // 2, 0)), (swap_core(handed), (GROUPS // 2, 1))]
 
 
 def whole_blocks(*weights):
@@ -647,7 +648,7 @@
     )
     if riding:
         block, _ = lax.optimization_barrier((block, found))
-        later += last_step(block)
+        later += last_step(block, fetched)
     layout = tuple(at for _, at in later)
     pieces = [piece for piece, _ in later]
     fields = decode(

time: 126 us -> 123 us (0.976)
  waiting for transfers between devices: 40.7 us -> 37.1 us
    ppermute x11, waiting for transfers between devices: 23.9 us -> 20.1 us  [carry(): return lax.ppermute(block, ('seq', 'band'), pairs)]
    ppermute x13, waiting for transfers between devices: 0.03 us -> 1.52 us  [swap_core(): return lax.ppermute(block, 'band', [(i, i ^ 1) for i in range(BANDS)])]
    all_to_all x1, waiting for transfers between devices: 8.24 us -> 6.95 us  [local(): lax.all_to_all(found.reshape(shards, SLOTS, width), 'seq', split_axis=0,...]
  transfers between devices with their start and end apart: 29 -> 29, of which waited for: 12 -> 11; matrix products, arithmetic and copies ran while one was open for 3% -> 3% of each run, Pallas kernels for 20% -> 20%
where the time goes in v1:
time: 123 us; the launch traced here: 122 us
  starting transfers between devices  40 us (33%)
  Pallas kernels  38.7 us (31%)
  waiting for transfers between devices  37.1 us (30%)
  local copies, waits for them, and re-layouts  2.89 us (2%)
  other arithmetic  2.88 us (2%)
    ppermute x11, starting transfers between devices, carry(): return lax.ppermute(block, ('seq', 'band'), pairs)  25.7 us
    ppermute x11, waiting for transfers between devices, carry(): return lax.ppermute(block, ('seq', 'band'), pairs)  20.1 us
    pallas_call x1, Pallas kernels, attend(): pl.pallas_call(functools.partial(attend_kernel, layout, ready, riding), o...  10.9 us
    pallas_call x1, Pallas kernels, decode(): pl.pallas_call(functools.partial(decode_kernel, layout, outputs // GROUPS...  10.9 us
    ppermute x1, waiting for transfers between devices, local(): left = lax.ppermute(states[tok - HALF:], 'seq', up)  7.72 us
    all_to_all x1, waiting for transfers between devices, local(): lax.all_to_all(found.reshape(shards, SLOTS, width), 'seq', split_axis=0,...  6.95 us
    pallas_call x1, Pallas kernels, project(): pl.pallas_call(functools.partial(project_kernel, layout, riding), out_sha...  5.29 us
    pallas_call x1, Pallas kernels, mix(): pl.pallas_call(functools.partial(mix_kernel, layout, ids is None), out_sh...  5.11 us
  transfers between devices with their start and end apart: 29, of which 11 were waited for; matrix products, arithmetic and copies ran while one was open for 3% of the time, Pallas kernels for 20%

profile of v1, /device:TPU:0, one launch (start us, length us, event | category | flops | bytes accessed | tf_op | source)
XLA Modules:
  0.0 122.2 jit_solution(4774817094432451310)
XLA Ops:
  0.0 3.0 %tables.1 = (f32[256,128]{1,0:T(8,128)}, bf16[1,128]{1,0:T(2,128)(2,1)}, bf16[1040,128]{1,0:T(8,128)(2,1)}) custom-call(s32[8,256]{1,0:T(8,128)} %bitcast.34, s32[1,256]{1,0:T(1,128)} %bitcast.39, s32[1,128]{1,0:T(1,128)} %constant.32.clone.low, f32[1,128]{1,0:T(1,128)} %constant.33.clone.rank, bf16[256,256]{1,0:T(8,128)(2,1)} %constant.34.clone.tri, ...), custom_call_target="tpu_custom_call" | custom-call | flops 1000 | bytes 1000 | tf_op jit(solution)/shard_map/tables/pallas_call | solution.py:181
  3.0 2.9 %collective-permute-start.2 = (bf16[1040,128]{1,0:T(8,128)(2,1)}, bf16[1040,128]{1,0:T(8,128)(2,1)S(1)}, u32[]{:S(2)}, u32[]{:S(2)}) collective-permute-start(bf16[1040,128]{1,0:T(8,128)(2,1)} %get-tuple-element.23), channel_id=1, source_target_pairs={{0,2},{1,3},{2,0},{3,1},{4,6},{5,7},{6,4},{7,5},{8,10},{9,11},{10,... | collective-permute-start | bytes 798728 | tf_op jit(solution)/shard_map/ppermute | solution.py:517
  6.0 1.1 slice_bitcast_fusion
  7.1 3.4 %collective-permute-start = (bf16[128,1024]{1,0:T(8,128)(2,1)S(1)}, bf16[128,1024]{1,0:T(8,128)(2,1)S(1)}, u32[]{:S(2)}, u32[]{:S(2)}) collective-permute-start(bf16[128,1024]{1,0:T(8,128)(2,1)S(1)} %get-tuple-element.44), channel_id=1, source_target_pairs={{0,4},{4,8},{8,12},{12,16},{16,20},{20,24},{24,28},{1,5},{5,9},{9,... | collective-permute-start | bytes 786440 | tf_op jit(solution)/shard_map/ppermute | solution.py:593
  10.5 1.3 %collective-permute-start.1 = (bf16[128,1024]{1,0:T(8,128)(2,1)S(1)}, bf16[128,1024]{1,0:T(8,128)(2,1)S(1)}, u32[]{:S(2)}, u32[]{:S(2)}) collective-permute-start(bf16[128,1024]{1,0:T(8,128)(2,1)S(1)} %get-tuple-element.43), channel_id=1, source_target_pairs={{4,0},{8,4},{12,8},{16,12},{20,16},{24,20},{28,24},{5,1},{9,5},{13... | collective-permute-start | bytes 786440 | tf_op jit(solution)/shard_map/ppermute | solution.py:594
  11.8 0.8 collective-permute-done.2
  12.6 1.0 select_bitcast_fusion.3
  13.6 0.1 pad_maximum_fusion.1.refs_0_.refs_1_
  13.6 7.7 %collective-permute-done.left = bf16[128,1024]{1,0:T(8,128)(2,1)S(1)} collective-permute-done((bf16[128,1024]{1,0:T(8,128)(2,1)S(1)}, bf16[128,1024]{1,0:T(8,128)(2,1)S(1)}, u32[]{:S(2)}, u32[]{:S(2)}) %collective-permute-start) | collective-permute-done | bytes 262176 | tf_op jit(solution)/shard_map/ppermute | solution.py:593
  21.4 3.4 %collective-permute-start.6 = (bf16[2,1040,128]{2,1,0:T(8,128)(2,1)S(1)}, bf16[2,1040,128]{2,1,0:T(8,128)(2,1)S(1)}, u32[]{:S(2)}, u32[]{:S(2)}) collective-permute-start(bf16[2,1040,128]{2,1,0:T(8,128)(2,1)S(1)} %pad_maximum_fusion.1.refs_0_.refs_1_), channel_id=1, source_target_pairs={{0,8},{9,1},{2,10},{11,3},{8,16},{17,9},{10,18},{19,11},{16,24},{2... | collective-permute-start | bytes 1597448 | tf_op jit(solution)/shard_map/ppermute | solution.py:535
  24.8 1.9 %collective-permute-start.4 = (bf16[2,1040,128]{2,1,0:T(8,128)(2,1)S(1)}, bf16[2,1040,128]{2,1,0:T(8,128)(2,1)}, u32[]{:S(2)}, u32[]{:S(2)}) collective-permute-start(bf16[2,1040,128]{2,1,0:T(8,128)(2,1)S(1)} %collective-permute-done.3.refs_1_.refs_2_), channel_id=1, source_target_pairs={{0,8},{9,1},{2,10},{11,3},{8,16},{17,9},{10,18},{19,11},{16,24},{2... | collective-permute-start | bytes 1597448 | tf_op jit(solution)/shard_map/ppermute | solution.py:535
  26.7 3.5 %prepare.1 = (bf16[512,1024]{1,0:T(8,128)(2,1)}, f32[2,128,384]{2,1,0:T(8,128)}, f32[256,256]{1,0:T(8,128)}) custom-call(bf16[128,1024]{1,0:T(8,128)(2,1)} %copy-done.21, bf16[256,1024]{1,0:T(8,128)(2,1)} %bitcast.29, bf16[128,1024]{1,0:T(8,128)(2,1)} %copy-done.22, f32[1,1024]{1,0:T(1,128)} %bitcast.37, s32[1,256]{1,0:T(1,128)} %bitcast.41, ...), custom_call_target="tpu_custom_call" | custom-call | flops 1000 | bytes 1000 | tf_op jit(solution)/shard_map/prepare/pallas_call | solution.py:117
  30.2 1.4 %collective-permute-done.6.refs_2_.refs_3_ = bf16[2,1040,128]{2,1,0:T(8,128)(2,1)S(1)} collective-permute-done((bf16[2,1040,128]{2,1,0:T(8,128)(2,1)S(1)}, bf16[2,1040,128]{2,1,0:T(8,128)(2,1)S(1)}, u32[]{:S(2)}, u32[]{:S(2)}) %collective-permute-start.6) | collective-permute-done | bytes 532512 | tf_op jit(solution)/shard_map/ppermute | solution.py:535
  31.6 2.5 %collective-permute-start.7 = (bf16[2,1040,128]{2,1,0:T(8,128)(2,1)S(1)}, bf16[2,1040,128]{2,1,0:T(8,128)(2,1)S(1)}, u32[]{:S(2)}, u32[]{:S(2)}) collective-permute-start(bf16[2,1040,128]{2,1,0:T(8,128)(2,1)S(1)} %collective-permute-done.6.refs_2_.refs_3_), channel_id=1, source_target_pairs={{0,8},{9,1},{2,10},{11,3},{8,16},{17,9},{10,18},{19,11},{16,24},{2... | collective-permute-start | bytes 1597448 | tf_op jit(solution)/shard_map/ppermute | solution.py:535
  34.1 3.2 %collective-permute-done.4.refs_4_.refs_5_ = bf16[2,1040,128]{2,1,0:T(8,128)(2,1)} collective-permute-done((bf16[2,1040,128]{2,1,0:T(8,128)(2,1)S(1)}, bf16[2,1040,128]{2,1,0:T(8,128)(2,1)}, u32[]{:S(2)}, u32[]{:S(2)}) %collective-permute-start.4) | collective-permute-done | bytes 532512 | tf_op jit(solution)/shard_map/ppermute | solution.py:535
  37.3 2.6 %collective-permute-start.5 = (bf16[2,1040,128]{2,1,0:T(8,128)(2,1)}, bf16[2,1040,128]{2,1,0:T(8,128)(2,1)S(1)}, u32[]{:S(2)}, u32[]{:S(2)}) collective-permute-start(bf16[2,1040,128]{2,1,0:T(8,128)(2,1)} %collective-permute-done.4.refs_4_.refs_5_), channel_id=1, source_target_pairs={{0,8},{9,1},{2,10},{11,3},{8,16},{17,9},{10,18},{19,11},{16,24},{2... | collective-permute-start | bytes 1597448 | tf_op jit(solution)/shard_map/ppermute | solution.py:535
  40.0 0.6 collective-permute-start.18
  40.6 0.5 collective-permute-start.15
  41.1 2.0 %collective-permute-done.7.refs_0_.refs_7_ = bf16[2,1040,128]{2,1,0:T(8,128)(2,1)S(1)} collective-permute-done((bf16[2,1040,128]{2,1,0:T(8,128)(2,1)S(1)}, bf16[2,1040,128]{2,1,0:T(8,128)(2,1)S(1)}, u32[]{:S(2)}, u32[]{:S(2)}) %collective-permute-start.7) | collective-permute-done | bytes 532512 | tf_op jit(solution)/shard_map/ppermute | solution.py:535
  43.0 2.5 %collective-permute-start.10 = (bf16[2,1040,128]{2,1,0:T(8,128)(2,1)S(1)}, bf16[2,1040,128]{2,1,0:T(8,128)(2,1)S(1)}, u32[]{:S(2)}, u32[]{:S(2)}) collective-permute-start(bf16[2,1040,128]{2,1,0:T(8,128)(2,1)S(1)} %collective-permute-done.7.refs_0_.refs_7_), channel_id=1, source_target_pairs={{0,8},{9,1},{2,10},{11,3},{8,16},{17,9},{10,18},{19,11},{16,24},{2... | collective-permute-start | bytes 1597448 | tf_op jit(solution)/shard_map/ppermute | solution.py:535
  45.5 3.3 %collective-permute-done.5.refs_2_.refs_9_ = bf16[2,1040,128]{2,1,0:T(8,128)(2,1)S(1)} collective-permute-done((bf16[2,1040,128]{2,1,0:T(8,128)(2,1)}, bf16[2,1040,128]{2,1,0:T(8,128)(2,1)S(1)}, u32[]{:S(2)}, u32[]{:S(2)}) %collective-permute-start.5) | collective-permute-done | bytes 532512 | tf_op jit(solution)/shard_map/ppermute | solution.py:535
  48.8 2.4 %collective-permute-start.12 = (bf16[2,1040,128]{2,1,0:T(8,128)(2,1)S(1)}, bf16[2,1040,128]{2,1,0:T(8,128)(2,1)S(1)}, u32[]{:S(2)}, u32[]{:S(2)}) collective-permute-start(bf16[2,1040,128]{2,1,0:T(8,128)(2,1)S(1)} %collective-permute-done.5.refs_2_.refs_9_), channel_id=1, source_target_pairs={{0,8},{9,1},{2,10},{11,3},{8,16},{17,9},{10,18},{19,11},{16,24},{2... | collective-permute-start | bytes 1597448 | tf_op jit(solution)/shard_map/ppermute | solution.py:535
  51.2 0.8 pad_maximum_fusion.2
  52.0 0.6 collective-permute-start.8
  52.6 0.2 copy-done.12
  52.8 0.8 copy-done.13
  53.6 0.5 collective-permute-start.9
  54.1 5.3 %project.1.refs_10_ = bf16[24,512,128]{2,1,0:T(8,128)(2,1)} custom-call(bf16[512,1024]{1,0:T(8,128)(2,1)} %get-tuple-element.26.normed, bf16[2,1040,128]{2,1,0:T(8,128)(2,1)} %copy-done, bf16[2,1040,128]{2,1,0:T(8,128)(2,1)} %copy-done.10, bf16[2,1040,128]{2,1,0:T(8,128)(2,1)} %copy-done.11, bf16[2,1040,128]{2,1,0:T(8,128)(2,1)} %copy-done.12, ...), custom_call_target="tpu_custom_call" | custom-call | flops 1000 | bytes 1000 | tf_op jit(solution)/shard_map/project/pallas_call | solution.py:274
  59.5 0.7 collective-permute-done.12.refs_6_.refs_13_
  60.1 2.5 %collective-permute-start.16 = (bf16[2,1040,128]{2,1,0:T(8,128)(2,1)S(1)}, bf16[2,1040,128]{2,1,0:T(8,128)(2,1)}, u32[]{:S(2)}, u32[]{:S(2)}) collective-permute-start(bf16[2,1040,128]{2,1,0:T(8,128)(2,1)S(1)} %collective-permute-done.10.refs_4_.refs_11_), channel_id=1, source_target_pairs={{0,8},{9,1},{2,10},{11,3},{8,16},{17,9},{10,18},{19,11},{16,24},{2... | collective-permute-start | bytes 1597448 | tf_op jit(solution)/shard_map/ppermute | solution.py:535
  62.6 1.0 select_bitcast_fusion.1
  63.6 0.1 pad_maximum_fusion.refs_0_
  63.7 1.6 %collective-permute-start.20 = (bf16[2,2,544,128]{3,2,1,0:T(8,128)(2,1)S(1)}, bf16[2,2,544,128]{3,2,1,0:T(8,128)(2,1)}, u32[]{:S(2)}, u32[]{:S(2)}) collective-permute-start(bf16[2,2,544,128]{3,2,1,0:T(8,128)(2,1)S(1)} %pad_maximum_fusion.refs_0_), channel_id=1, source_target_pairs={{0,8},{9,1},{2,10},{11,3},{8,16},{17,9},{10,18},{19,11},{16,24},{2... | collective-permute-start | bytes 1671176 | tf_op jit(solution)/shard_map/ppermute | solution.py:535
  65.4 0.5 collective-permute-start.13
  65.9 3.6 %collective-permute-done.16.refs_8_.refs_15_ = bf16[2,1040,128]{2,1,0:T(8,128)(2,1)} collective-permute-done((bf16[2,1040,128]{2,1,0:T(8,128)(2,1)S(1)}, bf16[2,1040,128]{2,1,0:T(8,128)(2,1)}, u32[]{:S(2)}, u32[]{:S(2)}) %collective-permute-start.16) | collective-permute-done | bytes 532512 | tf_op jit(solution)/shard_map/ppermute | solution.py:535
  69.5 5.9 %collective-permute-done.20.refs_1_ = bf16[2,2,544,128]{3,2,1,0:T(8,128)(2,1)} collective-permute-done((bf16[2,2,544,128]{3,2,1,0:T(8,128)(2,1)S(1)}, bf16[2,2,544,128]{3,2,1,0:T(8,128)(2,1)}, u32[]{:S(2)}, u32[]{:S(2)}) %collective-permute-start.20) | collective-permute-done | bytes 557088 | tf_op jit(solution)/shard_map/ppermute | solution.py:535
  75.5 2.5 %collective-permute-start.22 = (bf16[2,2,544,128]{3,2,1,0:T(8,128)(2,1)}, bf16[2,2,544,128]{3,2,1,0:T(8,128)(2,1)}, u32[]{:S(2)}, u32[]{:S(2)}) collective-permute-start(bf16[2,2,544,128]{3,2,1,0:T(8,128)(2,1)} %collective-permute-done.20.refs_1_), channel_id=1, source_target_pairs={{0,8},{9,1},{2,10},{11,3},{8,16},{17,9},{10,18},{19,11},{16,24},{2... | collective-permute-start | bytes 1671176 | tf_op jit(solution)/shard_map/ppermute | solution.py:535
  78.0 10.9 %attend.1.refs_0_ = bf16[256,1024]{1,0:T(8,128)(2,1)} custom-call(bf16[512,1024]{1,0:T(8,128)(2,1)} %get-tuple-element.26.normed, f32[2,128,384]{2,1,0:T(8,128)} %get-tuple-element.27.bias, bf16[2,1040,128]{2,1,0:T(8,128)(2,1)} %copy-done.2, bf16[2,1040,128]{2,1,0:T(8,128)(2,1)} %copy-done.6, bf16[2,1040,128]{2,1,0:T(8,128)(2,1)} %copy-done.3, ...), custom_call_target="tpu_custom_call" | custom-call | flops 1000 | bytes 1000 | tf_op jit(solution)/shard_map/attend/pallas_call | solution.py:332
  88.9 1.6 %collective-permute-start.24 = (bf16[2,2,544,128]{3,2,1,0:T(8,128)(2,1)}, bf16[2,2,544,128]{3,2,1,0:T(8,128)(2,1)S(1)}, u32[]{:S(2)}, u32[]{:S(2)}) collective-permute-start(bf16[2,2,544,128]{3,2,1,0:T(8,128)(2,1)} %collective-permute-done.22.refs_3_), channel_id=1, source_target_pairs={{0,8},{9,1},{2,10},{11,3},{8,16},{17,9},{10,18},{19,11},{16,24},{2... | collective-permute-start | bytes 1671176 | tf_op jit(solution)/shard_map/ppermute | solution.py:535
  90.6 5.1 %mix.1 = (bf16[256,1024]{1,0:T(8,128)(2,1)}, bf16[128,1024]{1,0:T(8,128)(2,1)}) custom-call(bf16[256,1024]{1,0:T(8,128)(2,1)} %bitcast.30, f32[1,1024]{1,0:T(1,128)} %bitcast.38, bf16[256,1024]{1,0:T(8,128)(2,1)} %attend.1.refs_0_, bf16[2,1040,128]{2,1,0:T(8,128)(2,1)} %copy-done, bf16[2,1040,128]{2,1,0:T(8,128)(2,1)} %copy-done.10, ...), custom_call_target="tpu_custom_call" | custom-call | flops 1000 | bytes 1000 | tf_op jit(solution)/shard_map/mix/pallas_call | solution.py:412
  95.7 3.4 %all-to-all-start = ((bf16[8,16,1024]{2,1,0:T(8,128)(2,1)}), bf16[8,16,1024]{2,1,0:T(8,128)(2,1)S(1)}, u32[]{:S(2)}, u32[]{:S(2)}) async-start(bf16[8,16,1024]{2,1,0:T(8,128)(2,1)} %bitcast.33), calls=%async_computation | async-start | bytes 524288 | tf_op jit(solution)/shard_map/all_to_all | solution.py:646
  99.2 2.2 %collective-permute-start.26 = (bf16[2,544,128]{2,1,0:T(8,128)(2,1)S(1)}, bf16[2,544,128]{2,1,0:T(8,128)(2,1)S(1)}, u32[]{:S(2)}, u32[]{:S(2)}) collective-permute-start(bf16[2,544,128]{2,1,0:T(8,128)(2,1)S(1)} %dynamic-slice_bitcast_fusion), channel_id=1, source_target_pairs={{0,8},{9,1},{2,10},{11,3},{8,16},{17,9},{10,18},{19,11},{16,24},{2... | collective-permute-start | bytes 835592 | tf_op jit(solution)/shard_map/ppermute | solution.py:535
  101.4 0.5 collective-permute-start.23
  101.9 6.9 %all-to-all-done = bf16[8,16,1024]{2,1,0:T(8,128)(2,1)S(1)} async-done(((bf16[8,16,1024]{2,1,0:T(8,128)(2,1)}), bf16[8,16,1024]{2,1,0:T(8,128)(2,1)S(1)}, u32[]{:S(2)}, u32[]{:S(2)}) %all-to-all-start) | async-done | bytes 262176 | tf_op jit(solution)/shard_map/all_to_all | solution.py:646
  108.8 0.1 collective-permute-start.27
  109.0 1.5 %collective-permute-done.27.refs_8_ = bf16[2,544,128]{2,1,0:T(8,128)(2,1)S(1)} collective-permute-done((bf16[2,544,128]{2,1,0:T(8,128)(2,1)S(1)}, bf16[2,544,128]{2,1,0:T(8,128)(2,1)S(1)}, u32[]{:S(2)}, u32[]{:S(2)}) %collective-permute-start.27) | collective-permute-done | bytes 278560 | tf_op jit(solution)/shard_map/ppermute | solution.py:539
  110.5 0.7 copy-done.20
  111.1 10.9 %decode.1 = bf16[96,256]{1,0:T(8,128)(2,1)} custom-call(bf16[256,1024]{1,0:T(8,128)(2,1)} %bitcast.32, bf16[256,1024]{1,0:T(8,128)(2,1)} %get-tuple-element.29.decoded, bf16[128,1024]{1,0:T(8,128)(2,1)} %bitcast.31, f32[256,256]{1,0:T(8,128)} %get-tuple-element.31.here, f32[256,128]{1,0:T(8,128)} %get-tuple-element.32.there, ...), custom_call_target="tpu_custom_call" | custom-call | flops 1000 | bytes 1000 | tf_op jit(solution)/shard_map/decode/pallas_call | solution.py:490
  (77 shorter events, 0.2 us)
Async XLA Ops:
  0.0 39.9 %copy-start.24 = (bf16[256,12]{0,1:T(8,128)(2,1)S(1)}, bf16[256,12]{0,1:T(8,128)(2,1)}, u32[]{:S(2)}) copy-start(bf16[256,12]{0,1:T(8,128)(2,1)} %param.20) | copy-start | bytes 18436
  0.0 39.9 %copy-start.23 = (bf16[256,256]{1,0:T(8,128)(2,1)S(1)}, bf16[256,256]{1,0:T(8,128)(2,1)}, u32[]{:S(2)}) copy-start(bf16[256,256]{1,0:T(8,128)(2,1)} %param.19) | copy-start | bytes 393220
  3.0 9.5 %collective-permute-start.2 = (bf16[1040,128]{1,0:T(8,128)(2,1)}, bf16[1040,128]{1,0:T(8,128)(2,1)S(1)}, u32[]{:S(2)}, u32[]{:S(2)}) collective-permute-start(bf16[1040,128]{1,0:T(8,128)(2,1)} %get-tuple-element.23), channel_id=1, source_target_pairs={{0,2},{1,3},{2,0},{3,1},{4,6},{5,7},{6,4},{7,5},{8,10},{9,11},{10,... | collective-permute-start | bytes 798728 | tf_op jit(solution)/shard_map/ppermute | solution.py:517
  7.1 14.3 %collective-permute-start = (bf16[128,1024]{1,0:T(8,128)(2,1)S(1)}, bf16[128,1024]{1,0:T(8,128)(2,1)S(1)}, u32[]{:S(2)}, u32[]{:S(2)}) collective-permute-start(bf16[128,1024]{1,0:T(8,128)(2,1)S(1)} %get-tuple-element.44), channel_id=1, source_target_pairs={{0,4},{4,8},{8,12},{12,16},{16,20},{20,24},{24,28},{1,5},{5,9},{9,... | collective-permute-start | bytes 786440 | tf_op jit(solution)/shard_map/ppermute | solution.py:593
  10.5 10.9 %collective-permute-start.1 = (bf16[128,1024]{1,0:T(8,128)(2,1)S(1)}, bf16[128,1024]{1,0:T(8,128)(2,1)S(1)}, u32[]{:S(2)}, u32[]{:S(2)}) collective-permute-start(bf16[128,1024]{1,0:T(8,128)(2,1)S(1)} %get-tuple-element.43), channel_id=1, source_target_pairs={{4,0},{8,4},{12,8},{16,12},{20,16},{24,20},{28,24},{5,1},{9,5},{13... | collective-permute-start | bytes 786440 | tf_op jit(solution)/shard_map/ppermute | solution.py:594
  13.6 40.5 %copy-start = (bf16[2,1040,128]{2,1,0:T(8,128)(2,1)}, bf16[2,1040,128]{2,1,0:T(8,128)(2,1)S(1)}, u32[]{:S(2)}) copy-start(bf16[2,1040,128]{2,1,0:T(8,128)(2,1)S(1)} %pad_maximum_fusion.1.refs_0_.refs_1_) | copy-start | bytes 1597444
  21.4 5.4 %copy-start.21 = (bf16[128,1024]{1,0:T(8,128)(2,1)}, bf16[128,1024]{1,0:T(8,128)(2,1)S(1)}, u32[]{:S(2)}) copy-start(bf16[128,1024]{1,0:T(8,128)(2,1)S(1)} %collective-permute-done.left) | copy-start | bytes 786436
  21.4 5.4 %copy-start.22 = (bf16[128,1024]{1,0:T(8,128)(2,1)}, bf16[128,1024]{1,0:T(8,128)(2,1)S(1)}, u32[]{:S(2)}) copy-start(bf16[128,1024]{1,0:T(8,128)(2,1)S(1)} %collective-permute-done.1.right) | copy-start | bytes 786436
  21.4 3.4 %collective-permute-start.3 = (bf16[2,1040,128]{2,1,0:T(8,128)(2,1)S(1)}, bf16[2,1040,128]{2,1,0:T(8,128)(2,1)S(1)}, u32[]{:S(2)}, u32[]{:S(2)}) collective-permute-start(bf16[2,1040,128]{2,1,0:T(8,128)(2,1)S(1)} %pad_maximum_fusion.1.refs_0_.refs_1_), channel_id=1, source_target_pairs={{0,1},{1,0},{2,3},{3,2},{4,5},{5,4},{6,7},{7,6},{8,9},{9,8},{10,11... | collective-permute-start | bytes 1597448 | tf_op jit(solution)/shard_map/ppermute | solution.py:539
  21.4 10.2 %collective-permute-start.6 = (bf16[2,1040,128]{2,1,0:T(8,128)(2,1)S(1)}, bf16[2,1040,128]{2,1,0:T(8,128)(2,1)S(1)}, u32[]{:S(2)}, u32[]{:S(2)}) collective-permute-start(bf16[2,1040,128]{2,1,0:T(8,128)(2,1)S(1)} %pad_maximum_fusion.1.refs_0_.refs_1_), channel_id=1, source_target_pairs={{0,8},{9,1},{2,10},{11,3},{8,16},{17,9},{10,18},{19,11},{16,24},{2... | collective-permute-start | bytes 1597448 | tf_op jit(solution)/shard_map/ppermute | solution.py:535
  24.8 29.3 %copy-start.10 = (bf16[2,1040,128]{2,1,0:T(8,128)(2,1)}, bf16[2,1040,128]{2,1,0:T(8,128)(2,1)S(1)}, u32[]{:S(2)}) copy-start(bf16[2,1040,128]{2,1,0:T(8,128)(2,1)S(1)} %collective-permute-done.3.refs_1_.refs_2_) | copy-start | bytes 1597444
  24.8 12.5 %collective-permute-start.4 = (bf16[2,1040,128]{2,1,0:T(8,128)(2,1)S(1)}, bf16[2,1040,128]{2,1,0:T(8,128)(2,1)}, u32[]{:S(2)}, u32[]{:S(2)}) collective-permute-start(bf16[2,1040,128]{2,1,0:T(8,128)(2,1)S(1)} %collective-permute-done.3.refs_1_.refs_2_), channel_id=1, source_target_pairs={{0,8},{9,1},{2,10},{11,3},{8,16},{17,9},{10,18},{19,11},{16,24},{2... | collective-permute-start | bytes 1597448 | tf_op jit(solution)/shard_map/ppermute | solution.py:535
  31.6 20.4 %copy-start.11 = (bf16[2,1040,128]{2,1,0:T(8,128)(2,1)}, bf16[2,1040,128]{2,1,0:T(8,128)(2,1)S(1)}, u32[]{:S(2)}) copy-start(bf16[2,1040,128]{2,1,0:T(8,128)(2,1)S(1)} %collective-permute-done.6.refs_2_.refs_3_) | copy-start | bytes 1597444
  31.6 11.4 %collective-permute-start.7 = (bf16[2,1040,128]{2,1,0:T(8,128)(2,1)S(1)}, bf16[2,1040,128]{2,1,0:T(8,128)(2,1)S(1)}, u32[]{:S(2)}, u32[]{:S(2)}) collective-permute-start(bf16[2,1040,128]{2,1,0:T(8,128)(2,1)S(1)} %collective-permute-done.6.refs_2_.refs_3_), channel_id=1, source_target_pairs={{0,8},{9,1},{2,10},{11,3},{8,16},{17,9},{10,18},{19,11},{16,24},{2... | collective-permute-start | bytes 1597448 | tf_op jit(solution)/shard_map/ppermute | solution.py:535
  37.3 11.5 %collective-permute-start.5 = (bf16[2,1040,128]{2,1,0:T(8,128)(2,1)}, bf16[2,1040,128]{2,1,0:T(8,128)(2,1)S(1)}, u32[]{:S(2)}, u32[]{:S(2)}) collective-permute-start(bf16[2,1040,128]{2,1,0:T(8,128)(2,1)} %collective-permute-done.4.refs_4_.refs_5_), channel_id=1, source_target_pairs={{0,8},{9,1},{2,10},{11,3},{8,16},{17,9},{10,18},{19,11},{16,24},{2... | collective-permute-start | bytes 1597448 | tf_op jit(solution)/shard_map/ppermute | solution.py:535
  40.0 11.3 %collective-permute-start.18 = (bf16[544,128]{1,0:T(8,128)(2,1)S(1)}, bf16[544,128]{1,0:T(8,128)(2,1)S(1)}, u32[]{:S(2)}, u32[]{:S(2)}) collective-permute-start(bf16[544,128]{1,0:T(8,128)(2,1)S(1)} %pad_maximum_fusion.3), channel_id=1, source_target_pairs={{0,2},{1,3},{2,0},{3,1},{4,6},{5,7},{6,4},{7,5},{8,10},{9,11},{10,... | collective-permute-start | bytes 417800 | tf_op jit(solution)/shard_map/ppermute | solution.py:517
  40.6 11.4 %collective-permute-start.14 = (bf16[2,1040,128]{2,1,0:T(8,128)(2,1)S(1)}, bf16[2,1040,128]{2,1,0:T(8,128)(2,1)S(1)}, u32[]{:S(2)}, u32[]{:S(2)}) collective-permute-start(bf16[2,1040,128]{2,1,0:T(8,128)(2,1)S(1)} %collective-permute-done.6.refs_2_.refs_3_), channel_id=1, source_target_pairs={{0,1},{1,0},{2,3},{3,2},{4,5},{5,4},{6,7},{7,6},{8,9},{9,8},{10,11... | collective-permute-start | bytes 1597448 | tf_op jit(solution)/shard_map/ppermute | solution.py:539
  40.6 12.3 %collective-permute-start.15 = (bf16[2,1040,128]{2,1,0:T(8,128)(2,1)}, bf16[2,1040,128]{2,1,0:T(8,128)(2,1)S(1)}, u32[]{:S(2)}, u32[]{:S(2)}) collective-permute-start(bf16[2,1040,128]{2,1,0:T(8,128)(2,1)} %collective-permute-done.4.refs_4_.refs_5_), channel_id=1, source_target_pairs={{0,1},{1,0},{2,3},{3,2},{4,5},{5,4},{6,7},{7,6},{8,9},{9,8},{10,11... | collective-permute-start | bytes 1597448 | tf_op jit(solution)/shard_map/ppermute | solution.py:539
  43.0 16.4 %copy-start.2 = (bf16[2,1040,128]{2,1,0:T(8,128)(2,1)}, bf16[2,1040,128]{2,1,0:T(8,128)(2,1)S(1)}, u32[]{:S(2)}) copy-start(bf16[2,1040,128]{2,1,0:T(8,128)(2,1)S(1)} %collective-permute-done.7.refs_0_.refs_7_) | copy-start | bytes 1597444
  43.0 16.4 %collective-permute-start.10 = (bf16[2,1040,128]{2,1,0:T(8,128)(2,1)S(1)}, bf16[2,1040,128]{2,1,0:T(8,128)(2,1)S(1)}, u32[]{:S(2)}, u32[]{:S(2)}) collective-permute-start(bf16[2,1040,128]{2,1,0:T(8,128)(2,1)S(1)} %collective-permute-done.7.refs_0_.refs_7_), channel_id=1, source_target_pairs={{0,8},{9,1},{2,10},{11,3},{8,16},{17,9},{10,18},{19,11},{16,24},{2... | collective-permute-start | bytes 1597448 | tf_op jit(solution)/shard_map/ppermute | solution.py:535
  48.8 10.6 %copy-start.3 = (bf16[2,1040,128]{2,1,0:T(8,128)(2,1)}, bf16[2,1040,128]{2,1,0:T(8,128)(2,1)S(1)}, u32[]{:S(2)}) copy-start(bf16[2,1040,128]{2,1,0:T(8,128)(2,1)S(1)} %collective-permute-done.5.refs_2_.refs_9_) | copy-start | bytes 1597444
  48.8 11.3 %collective-permute-start.12 = (bf16[2,1040,128]{2,1,0:T(8,128)(2,1)S(1)}, bf16[2,1040,128]{2,1,0:T(8,128)(2,1)S(1)}, u32[]{:S(2)}, u32[]{:S(2)}) collective-permute-start(bf16[2,1040,128]{2,1,0:T(8,128)(2,1)S(1)} %collective-permute-done.5.refs_2_.refs_9_), channel_id=1, source_target_pairs={{0,8},{9,1},{2,10},{11,3},{8,16},{17,9},{10,18},{19,11},{16,24},{2... | collective-permute-start | bytes 1597448 | tf_op jit(solution)/shard_map/ppermute | solution.py:535
  52.0 10.6 %collective-permute-start.19 = (bf16[2,544,128]{2,1,0:T(8,128)(2,1)}, bf16[2,544,128]{2,1,0:T(8,128)(2,1)}, u32[]{:S(2)}, u32[]{:S(2)}) collective-permute-start(bf16[2,544,128]{2,1,0:T(8,128)(2,1)} %pad_maximum_fusion.2), channel_id=1, source_target_pairs={{0,1},{1,0},{2,3},{3,2},{4,5},{5,4},{6,7},{7,6},{8,9},{9,8},{10,11... | collective-permute-start | bytes 835592 | tf_op jit(solution)/shard_map/ppermute | solution.py:539
  52.0 11.7 %collective-permute-start.8 = (bf16[2,1040,128]{2,1,0:T(8,128)(2,1)S(1)}, bf16[2,1040,128]{2,1,0:T(8,128)(2,1)S(1)}, u32[]{:S(2)}, u32[]{:S(2)}) collective-permute-start(bf16[2,1040,128]{2,1,0:T(8,128)(2,1)S(1)} %collective-permute-done.7.refs_0_.refs_7_), channel_id=1, source_target_pairs={{0,1},{1,0},{2,3},{3,2},{4,5},{5,4},{6,7},{7,6},{8,9},{9,8},{10,11... | collective-permute-start | bytes 1597448 | tf_op jit(solution)/shard_map/ppermute | solution.py:539
  53.6 10.1 %collective-permute-start.9 = (bf16[2,1040,128]{2,1,0:T(8,128)(2,1)S(1)}, bf16[2,1040,128]{2,1,0:T(8,128)(2,1)}, u32[]{:S(2)}, u32[]{:S(2)}) collective-permute-start(bf16[2,1040,128]{2,1,0:T(8,128)(2,1)S(1)} %collective-permute-done.5.refs_2_.refs_9_), channel_id=1, source_target_pairs={{0,1},{1,0},{2,3},{3,2},{4,5},{5,4},{6,7},{7,6},{8,9},{9,8},{10,11... | collective-permute-start | bytes 1597448 | tf_op jit(solution)/shard_map/ppermute | solution.py:539
  59.5 18.5 %copy-start.4 = (bf16[2,1040,128]{2,1,0:T(8,128)(2,1)}, bf16[2,1040,128]{2,1,0:T(8,128)(2,1)S(1)}, u32[]{:S(2)}) copy-start(bf16[2,1040,128]{2,1,0:T(8,128)(2,1)S(1)} %collective-permute-done.10.refs_4_.refs_11_) | copy-start | bytes 1597444
  60.1 17.8 %copy-start.5 = (bf16[2,1040,128]{2,1,0:T(8,128)(2,1)}, bf16[2,1040,128]{2,1,0:T(8,128)(2,1)S(1)}, u32[]{:S(2)}) copy-start(bf16[2,1040,128]{2,1,0:T(8,128)(2,1)S(1)} %collective-permute-done.12.refs_6_.refs_13_) | copy-start | bytes 1597444
  60.1 9.4 %collective-permute-start.16 = (bf16[2,1040,128]{2,1,0:T(8,128)(2,1)S(1)}, bf16[2,1040,128]{2,1,0:T(8,128)(2,1)}, u32[]{:S(2)}, u32[]{:S(2)}) collective-permute-start(bf16[2,1040,128]{2,1,0:T(8,128)(2,1)S(1)} %collective-permute-done.10.refs_4_.refs_11_), channel_id=1, source_target_pairs={{0,8},{9,1},{2,10},{11,3},{8,16},{17,9},{10,18},{19,11},{16,24},{2... | collective-permute-start | bytes 1597448 | tf_op jit(solution)/shard_map/ppermute | solution.py:535
  63.7 25.2 %copy-start.1 = (bf16[2,2,544,128]{3,2,1,0:T(8,128)(2,1)}, bf16[2,2,544,128]{3,2,1,0:T(8,128)(2,1)S(1)}, u32[]{:S(2)}) copy-start(bf16[2,2,544,128]{3,2,1,0:T(8,128)(2,1)S(1)} %pad_maximum_fusion.refs_0_) | copy-start | bytes 1671172
  63.7 14.3 %copy-start.6 = (bf16[2,1040,128]{2,1,0:T(8,128)(2,1)}, bf16[2,1040,128]{2,1,0:T(8,128)(2,1)S(1)}, u32[]{:S(2)}) copy-start(bf16[2,1040,128]{2,1,0:T(8,128)(2,1)S(1)} %collective-permute-done.8.refs_1_.refs_8_) | copy-start | bytes 1597444
  63.7 11.8 %collective-permute-start.20 = (bf16[2,2,544,128]{3,2,1,0:T(8,128)(2,1)S(1)}, bf16[2,2,544,128]{3,2,1,0:T(8,128)(2,1)}, u32[]{:S(2)}, u32[]{:S(2)}) collective-permute-start(bf16[2,2,544,128]{3,2,1,0:T(8,128)(2,1)S(1)} %pad_maximum_fusion.refs_0_), channel_id=1, source_target_pairs={{0,8},{9,1},{2,10},{11,3},{8,16},{17,9},{10,18},{19,11},{16,24},{2... | collective-permute-start | bytes 1671176 | tf_op jit(solution)/shard_map/ppermute | solution.py:535
  65.4 4.2 %collective-permute-start.11 = (bf16[2,1040,128]{2,1,0:T(8,128)(2,1)S(1)}, bf16[2,1040,128]{2,1,0:T(8,128)(2,1)S(1)}, u32[]{:S(2)}, u32[]{:S(2)}) collective-permute-start(bf16[2,1040,128]{2,1,0:T(8,128)(2,1)S(1)} %collective-permute-done.10.refs_4_.refs_11_), channel_id=1, source_target_pairs={{0,1},{1,0},{2,3},{3,2},{4,5},{5,4},{6,7},{7,6},{8,9},{9,8},{10,11... | collective-permute-start | bytes 1597448 | tf_op jit(solution)/shard_map/ppermute | solution.py:539
  65.4 4.2 %collective-permute-start.13 = (bf16[2,1040,128]{2,1,0:T(8,128)(2,1)S(1)}, bf16[2,1040,128]{2,1,0:T(8,128)(2,1)S(1)}, u32[]{:S(2)}, u32[]{:S(2)}) collective-permute-start(bf16[2,1040,128]{2,1,0:T(8,128)(2,1)S(1)} %collective-permute-done.12.refs_6_.refs_13_), channel_id=1, source_target_pairs={{0,1},{1,0},{2,3},{3,2},{4,5},{5,4},{6,7},{7,6},{8,9},{9,8},{10,11... | collective-permute-start | bytes 1597448 | tf_op jit(solution)/shard_map/ppermute | solution.py:539
  69.5 6.0 %collective-permute-start.17 = (bf16[2,1040,128]{2,1,0:T(8,128)(2,1)}, bf16[2,1040,128]{2,1,0:T(8,128)(2,1)S(1)}, u32[]{:S(2)}, u32[]{:S(2)}) collective-permute-start(bf16[2,1040,128]{2,1,0:T(8,128)(2,1)} %collective-permute-done.16.refs_8_.refs_15_), channel_id=1, source_target_pairs={{0,1},{1,0},{2,3},{3,2},{4,5},{5,4},{6,7},{7,6},{8,9},{9,8},{10,11... | collective-permute-start | bytes 1597448 | tf_op jit(solution)/shard_map/ppermute | solution.py:539
  69.5 8.5 %copy-start.7 = (bf16[2,1040,128]{2,1,0:T(8,128)(2,1)}, bf16[2,1040,128]{2,1,0:T(8,128)(2,1)S(1)}, u32[]{:S(2)}) copy-start(bf16[2,1040,128]{2,1,0:T(8,128)(2,1)S(1)} %collective-permute-done.11.refs_5_.refs_12_) | copy-start | bytes 1597444
  69.5 8.5 %copy-start.8 = (bf16[2,1040,128]{2,1,0:T(8,128)(2,1)}, bf16[2,1040,128]{2,1,0:T(8,128)(2,1)S(1)}, u32[]{:S(2)}) copy-start(bf16[2,1040,128]{2,1,0:T(8,128)(2,1)S(1)} %collective-permute-done.13.refs_7_.refs_14_) | copy-start | bytes 1597444
  75.5 2.5 %copy-start.9 = (bf16[2,1040,128]{2,1,0:T(8,128)(2,1)}, bf16[2,1040,128]{2,1,0:T(8,128)(2,1)S(1)}, u32[]{:S(2)}) copy-start(bf16[2,1040,128]{2,1,0:T(8,128)(2,1)S(1)} %collective-permute-done.17.refs_9_.refs_16_) | copy-start | bytes 1597444
  75.5 13.4 %collective-permute-start.22 = (bf16[2,2,544,128]{3,2,1,0:T(8,128)(2,1)}, bf16[2,2,544,128]{3,2,1,0:T(8,128)(2,1)}, u32[]{:S(2)}, u32[]{:S(2)}) collective-permute-start(bf16[2,2,544,128]{3,2,1,0:T(8,128)(2,1)} %collective-permute-done.20.refs_1_), channel_id=1, source_target_pairs={{0,8},{9,1},{2,10},{11,3},{8,16},{17,9},{10,18},{19,11},{16,24},{2... | collective-permute-start | bytes 1671176 | tf_op jit(solution)/shard_map/ppermute | solution.py:535
  88.9 10.2 %collective-permute-start.24 = (bf16[2,2,544,128]{3,2,1,0:T(8,128)(2,1)}, bf16[2,2,544,128]{3,2,1,0:T(8,128)(2,1)S(1)}, u32[]{:S(2)}, u32[]{:S(2)}) collective-permute-start(bf16[2,2,544,128]{3,2,1,0:T(8,128)(2,1)} %collective-permute-done.22.refs_3_), channel_id=1, source_target_pairs={{0,8},{9,1},{2,10},{11,3},{8,16},{17,9},{10,18},{19,11},{16,24},{2... | collective-permute-start | bytes 1671176 | tf_op jit(solution)/shard_map/ppermute | solution.py:535
  95.7 13.1 %all-to-all-start = ((bf16[8,16,1024]{2,1,0:T(8,128)(2,1)}), bf16[8,16,1024]{2,1,0:T(8,128)(2,1)S(1)}, u32[]{:S(2)}, u32[]{:S(2)}) async-start(bf16[8,16,1024]{2,1,0:T(8,128)(2,1)} %bitcast.33), calls=%async_computation | async-start | bytes 524288 | tf_op jit(solution)/shard_map/all_to_all | solution.py:646
  99.1 11.3 %copy-start.14 = (bf16[2,2,544,128]{3,2,1,0:T(8,128)(2,1)}, bf16[2,2,544,128]{3,2,1,0:T(8,128)(2,1)S(1)}, u32[]{:S(2)}) copy-start(bf16[2,2,544,128]{3,2,1,0:T(8,128)(2,1)S(1)} %collective-permute-done.24.refs_5_) | copy-start | bytes 1671172
  99.2 9.6 %collective-permute-start.26 = (bf16[2,544,128]{2,1,0:T(8,128)(2,1)S(1)}, bf16[2,544,128]{2,1,0:T(8,128)(2,1)S(1)}, u32[]{:S(2)}, u32[]{:S(2)}) collective-permute-start(bf16[2,544,128]{2,1,0:T(8,128)(2,1)S(1)} %dynamic-slice_bitcast_fusion), channel_id=1, source_target_pairs={{0,8},{9,1},{2,10},{11,3},{8,16},{17,9},{10,18},{19,11},{16,24},{2... | collective-permute-start | bytes 835592 | tf_op jit(solution)/shard_map/ppermute | solution.py:535
  101.4 7.5 %collective-permute-start.21 = (bf16[2,2,544,128]{3,2,1,0:T(8,128)(2,1)}, bf16[2,2,544,128]{3,2,1,0:T(8,128)(2,1)S(1)}, u32[]{:S(2)}, u32[]{:S(2)}) collective-permute-start(bf16[2,2,544,128]{3,2,1,0:T(8,128)(2,1)} %collective-permute-done.20.refs_1_), channel_id=1, source_target_pairs={{0,1},{1,0},{2,3},{3,2},{4,5},{5,4},{6,7},{7,6},{8,9},{9,8},{10,11... | collective-permute-start | bytes 1671176 | tf_op jit(solution)/shard_map/ppermute | solution.py:539
  101.4 7.6 %collective-permute-start.23 = (bf16[2,2,544,128]{3,2,1,0:T(8,128)(2,1)}, bf16[2,2,544,128]{3,2,1,0:T(8,128)(2,1)S(1)}, u32[]{:S(2)}, u32[]{:S(2)}) collective-permute-start(bf16[2,2,544,128]{3,2,1,0:T(8,128)(2,1)} %collective-permute-done.22.refs_3_), channel_id=1, source_target_pairs={{0,1},{1,0},{2,3},{3,2},{4,5},{5,4},{6,7},{7,6},{8,9},{9,8},{10,11... | collective-permute-start | bytes 1671176 | tf_op jit(solution)/shard_map/ppermute | solution.py:539
  101.9 7.1 %collective-permute-start.25 = (bf16[2,2,544,128]{3,2,1,0:T(8,128)(2,1)S(1)}, bf16[2,2,544,128]{3,2,1,0:T(8,128)(2,1)S(1)}, u32[]{:S(2)}, u32[]{:S(2)}) collective-permute-start(bf16[2,2,544,128]{3,2,1,0:T(8,128)(2,1)S(1)} %collective-permute-done.24.refs_5_), channel_id=1, source_target_pairs={{0,1},{1,0},{2,3},{3,2},{4,5},{5,4},{6,7},{7,6},{8,9},{9,8},{10,11... | collective-permute-start | bytes 1671176 | tf_op jit(solution)/shard_map/ppermute | solution.py:539
  108.8 1.6 %copy-start.15 = (bf16[8,16,1024]{2,1,0:T(8,128)(2,1)}, bf16[8,16,1024]{2,1,0:T(8,128)(2,1)S(1)}, u32[]{:S(2)}) copy-start(bf16[8,16,1024]{2,1,0:T(8,128)(2,1)S(1)} %all-to-all-done) | copy-start | bytes 786436
  108.8 1.6 %copy-start.19 = (bf16[2,544,128]{2,1,0:T(8,128)(2,1)}, bf16[2,544,128]{2,1,0:T(8,128)(2,1)S(1)}, u32[]{:S(2)}) copy-start(bf16[2,544,128]{2,1,0:T(8,128)(2,1)S(1)} %collective-permute-done.26.refs_7_) | copy-start | bytes 835588
  108.8 1.6 %collective-permute-start.27 = (bf16[2,544,128]{2,1,0:T(8,128)(2,1)S(1)}, bf16[2,544,128]{2,1,0:T(8,128)(2,1)S(1)}, u32[]{:S(2)}, u32[]{:S(2)}) collective-permute-start(bf16[2,544,128]{2,1,0:T(8,128)(2,1)S(1)} %collective-permute-done.26.refs_7_), channel_id=1, source_target_pairs={{0,1},{1,0},{2,3},{3,2},{4,5},{5,4},{6,7},{7,6},{8,9},{9,8},{10,11... | collective-permute-start | bytes 835592 | tf_op jit(solution)/shard_map/ppermute | solution.py:539
  (6 other events, 6.9 us)

commit v2 on v1

--- a/solution.py
+++ b/solution.py
@@ -615,15 +615,18 @@
         made = project(riding, normed, pieces[:6], None)
         chains, more = chain_step(chains, 3)
         pieces += more
-        last, more = chain_step(chains[:1], 4, (chains[1], made))
-        pieces += more
+        end, _, _ = lax.optimization_barrier((chains[0], chains[1], made))
+        end = carry(end)
         second, *_ = lax.optimization_barrier((second, chains[1], made, pieces[7][0], pieces[9][0]))
         later = [(second, (0, None))]
         block, more = ring_step(second, 1)
         later += more
+        made = project(riding, normed, pieces[6:10], made)
+        handed, _ = lax.optimization_barrier((end, made))
+        pieces += [(end, (GROUPS // 2, 0)), (swap_core(handed), (GROUPS // 2, 1))]
         block, more = ring_step(block, 2, [pieces[n][0] for n in (11, 13, 15)])
         later += more
-        attended = attend(riding, normed, bias, pieces[6:], made, (0, 1, 7))
+        attended = attend(riding, normed, bias, pieces[10:], made, (0, 1, 7, 2, 6))
         block, more = ring_step(block, 3, attended)
         later += more
         ids = None

time: 123 us -> 121 us (0.984)
  waiting for transfers between devices: 37.1 us -> 32.3 us
  Pallas kernels: 38.7 us -> 41.9 us
    ppermute x11, waiting for transfers between devices: 20.1 us -> 14.5 us  [carry(): return lax.ppermute(block, ('seq', 'band'), pairs)]
    pallas_call x1 -> x2, Pallas kernels: 5.29 us -> 9.97 us  [project(): pl.pallas_call(functools.partial(project_kernel, layout, riding), out_sha...]
    ppermute x13, waiting for transfers between devices: 1.52 us -> 3.19 us  [swap_core(): return lax.ppermute(block, 'band', [(i, i ^ 1) for i in range(BANDS)])]
    pallas_call x1, Pallas kernels: 10.9 us -> 9.44 us  [attend(): pl.pallas_call(functools.partial(attend_kernel, layout, ready, riding), o...]
  transfers between devices with their start and end apart: 29 -> 29, of which waited for: 11 -> 11; matrix products, arithmetic and copies ran while one was open for 3% -> 4% of each run, Pallas kernels for 20% -> 23%
where the time goes in v2:
time: 121 us
  Pallas kernels  41.9 us (35%)
  starting transfers between devices  39.9 us (33%)
  waiting for transfers between devices  32.3 us (27%)
  local copies, waits for them, and re-layouts  3.35 us (3%)
  other arithmetic  2.87 us (2%)
    ppermute x11, starting transfers between devices, carry(): return lax.ppermute(block, ('seq', 'band'), pairs)  25.8 us
    ppermute x11, waiting for transfers between devices, carry(): return lax.ppermute(block, ('seq', 'band'), pairs)  14.5 us
    pallas_call x1, Pallas kernels, decode(): pl.pallas_call(functools.partial(decode_kernel, layout, outputs // GROUPS...  10.9 us
    pallas_call x2, Pallas kernels, project(): pl.pallas_call(functools.partial(project_kernel, layout, riding), out_sha...  9.97 us
    pallas_call x1, Pallas kernels, attend(): pl.pallas_call(functools.partial(attend_kernel, layout, ready, riding), o...  9.44 us
    ppermute x1, waiting for transfers between devices, local(): left = lax.ppermute(states[tok - HALF:], 'seq', up)  7.72 us
    all_to_all x1, waiting for transfers between devices, local(): lax.all_to_all(found.reshape(shards, SLOTS, width), 'seq', split_axis=0,...  6.07 us
    pallas_call x1, Pallas kernels, mix(): pl.pallas_call(functools.partial(mix_kernel, layout, ids is None), out_sh...  5.1 us
  transfers between devices with their start and end apart: 29, of which 11 were waited for; matrix products, arithmetic and copies ran while one was open for 4% of the time, Pallas kernels for 23%

profile of v2, /device:TPU:0, one launch (start us, length us, event | category | flops | bytes accessed | tf_op | source)
XLA Modules:
  0.0 120.9 jit_solution(13778157942635525114)
XLA Ops:
  0.0 3.1 %tables.1 = (f32[256,128]{1,0:T(8,128)}, bf16[1,128]{1,0:T(2,128)(2,1)}, bf16[1040,128]{1,0:T(8,128)(2,1)}) custom-call(s32[8,256]{1,0:T(8,128)} %bitcast.34, s32[1,256]{1,0:T(1,128)} %bitcast.39, s32[1,128]{1,0:T(1,128)} %constant.32.clone.low, f32[1,128]{1,0:T(1,128)} %constant.33.clone.rank, bf16[256,256]{1,0:T(8,128)(2,1)} %constant.34.clone.tri, ...), custom_call_target="tpu_custom_call" | custom-call | flops 1000 | bytes 1000 | tf_op jit(solution)/shard_map/tables/pallas_call | solution.py:181
  3.1 2.9 %collective-permute-start.2 = (bf16[1040,128]{1,0:T(8,128)(2,1)}, bf16[1040,128]{1,0:T(8,128)(2,1)S(1)}, u32[]{:S(2)}, u32[]{:S(2)}) collective-permute-start(bf16[1040,128]{1,0:T(8,128)(2,1)} %get-tuple-element.24), channel_id=1, source_target_pairs={{0,2},{1,3},{2,0},{3,1},{4,6},{5,7},{6,4},{7,5},{8,10},{9,11},{10,... | collective-permute-start | bytes 798728 | tf_op jit(solution)/shard_map/ppermute | solution.py:517
  6.0 1.1 slice_bitcast_fusion
  7.1 3.4 %collective-permute-start = (bf16[128,1024]{1,0:T(8,128)(2,1)S(1)}, bf16[128,1024]{1,0:T(8,128)(2,1)S(1)}, u32[]{:S(2)}, u32[]{:S(2)}) collective-permute-start(bf16[128,1024]{1,0:T(8,128)(2,1)S(1)} %get-tuple-element.46), channel_id=1, source_target_pairs={{0,4},{4,8},{8,12},{12,16},{16,20},{20,24},{24,28},{1,5},{5,9},{9,... | collective-permute-start | bytes 786440 | tf_op jit(solution)/shard_map/ppermute | solution.py:593
  10.5 1.3 %collective-permute-start.1 = (bf16[128,1024]{1,0:T(8,128)(2,1)S(1)}, bf16[128,1024]{1,0:T(8,128)(2,1)S(1)}, u32[]{:S(2)}, u32[]{:S(2)}) collective-permute-start(bf16[128,1024]{1,0:T(8,128)(2,1)S(1)} %get-tuple-element.45), channel_id=1, source_target_pairs={{4,0},{8,4},{12,8},{16,12},{20,16},{24,20},{28,24},{5,1},{9,5},{13... | collective-permute-start | bytes 786440 | tf_op jit(solution)/shard_map/ppermute | solution.py:594
  11.8 0.8 collective-permute-done.2
  12.6 1.0 select_bitcast_fusion.3
  13.7 7.7 %collective-permute-done.left = bf16[128,1024]{1,0:T(8,128)(2,1)S(1)} collective-permute-done((bf16[128,1024]{1,0:T(8,128)(2,1)S(1)}, bf16[128,1024]{1,0:T(8,128)(2,1)S(1)}, u32[]{:S(2)}, u32[]{:S(2)}) %collective-permute-start) | collective-permute-done | bytes 262176 | tf_op jit(solution)/shard_map/ppermute | solution.py:593
  21.4 3.4 %collective-permute-start.6 = (bf16[2,1040,128]{2,1,0:T(8,128)(2,1)S(1)}, bf16[2,1040,128]{2,1,0:T(8,128)(2,1)S(1)}, u32[]{:S(2)}, u32[]{:S(2)}) collective-permute-start(bf16[2,1040,128]{2,1,0:T(8,128)(2,1)S(1)} %pad_maximum_fusion.1.refs_0_.refs_1_), channel_id=1, source_target_pairs={{0,8},{9,1},{2,10},{11,3},{8,16},{17,9},{10,18},{19,11},{16,24},{2... | collective-permute-start | bytes 1597448 | tf_op jit(solution)/shard_map/ppermute | solution.py:535
  24.8 1.9 %collective-permute-start.4 = (bf16[2,1040,128]{2,1,0:T(8,128)(2,1)S(1)}, bf16[2,1040,128]{2,1,0:T(8,128)(2,1)S(1)}, u32[]{:S(2)}, u32[]{:S(2)}) collective-permute-start(bf16[2,1040,128]{2,1,0:T(8,128)(2,1)S(1)} %collective-permute-done.3.refs_1_.refs_2_), channel_id=1, source_target_pairs={{0,8},{9,1},{2,10},{11,3},{8,16},{17,9},{10,18},{19,11},{16,24},{2... | collective-permute-start | bytes 1597448 | tf_op jit(solution)/shard_map/ppermute | solution.py:535
  26.7 3.5 %prepare.1 = (bf16[512,1024]{1,0:T(8,128)(2,1)}, f32[2,128,384]{2,1,0:T(8,128)}, f32[256,256]{1,0:T(8,128)}) custom-call(bf16[128,1024]{1,0:T(8,128)(2,1)} %copy-done.19, bf16[256,1024]{1,0:T(8,128)(2,1)} %bitcast.29, bf16[128,1024]{1,0:T(8,128)(2,1)} %copy-done.20, f32[1,1024]{1,0:T(1,128)} %bitcast.37, s32[1,256]{1,0:T(1,128)} %bitcast.41, ...), custom_call_target="tpu_custom_call" | custom-call | flops 1000 | bytes 1000 | tf_op jit(solution)/shard_map/prepare/pallas_call | solution.py:117
  30.3 1.4 %collective-permute-done.6.refs_2_.refs_3_ = bf16[2,1040,128]{2,1,0:T(8,128)(2,1)S(1)} collective-permute-done((bf16[2,1040,128]{2,1,0:T(8,128)(2,1)S(1)}, bf16[2,1040,128]{2,1,0:T(8,128)(2,1)S(1)}, u32[]{:S(2)}, u32[]{:S(2)}) %collective-permute-start.6) | collective-permute-done | bytes 532512 | tf_op jit(solution)/shard_map/ppermute | solution.py:535
  31.6 2.5 %collective-permute-start.7 = (bf16[2,1040,128]{2,1,0:T(8,128)(2,1)S(1)}, bf16[2,1040,128]{2,1,0:T(8,128)(2,1)}, u32[]{:S(2)}, u32[]{:S(2)}) collective-permute-start(bf16[2,1040,128]{2,1,0:T(8,128)(2,1)S(1)} %collective-permute-done.6.refs_2_.refs_3_), channel_id=1, source_target_pairs={{0,8},{9,1},{2,10},{11,3},{8,16},{17,9},{10,18},{19,11},{16,24},{2... | collective-permute-start | bytes 1597448 | tf_op jit(solution)/shard_map/ppermute | solution.py:535
  34.1 3.2 %collective-permute-done.4.refs_4_.refs_5_ = bf16[2,1040,128]{2,1,0:T(8,128)(2,1)S(1)} collective-permute-done((bf16[2,1040,128]{2,1,0:T(8,128)(2,1)S(1)}, bf16[2,1040,128]{2,1,0:T(8,128)(2,1)S(1)}, u32[]{:S(2)}, u32[]{:S(2)}) %collective-permute-start.4) | collective-permute-done | bytes 532512 | tf_op jit(solution)/shard_map/ppermute | solution.py:535
  37.3 2.5 %collective-permute-start.5 = (bf16[2,1040,128]{2,1,0:T(8,128)(2,1)S(1)}, bf16[2,1040,128]{2,1,0:T(8,128)(2,1)}, u32[]{:S(2)}, u32[]{:S(2)}) collective-permute-start(bf16[2,1040,128]{2,1,0:T(8,128)(2,1)S(1)} %collective-permute-done.4.refs_4_.refs_5_), channel_id=1, source_target_pairs={{0,8},{9,1},{2,10},{11,3},{8,16},{17,9},{10,18},{19,11},{16,24},{2... | collective-permute-start | bytes 1597448 | tf_op jit(solution)/shard_map/ppermute | solution.py:535
  39.9 0.6 collective-permute-start.18
  40.5 0.5 collective-permute-start.13
  41.0 2.1 %collective-permute-done.7.refs_0_.refs_7_ = bf16[2,1040,128]{2,1,0:T(8,128)(2,1)} collective-permute-done((bf16[2,1040,128]{2,1,0:T(8,128)(2,1)S(1)}, bf16[2,1040,128]{2,1,0:T(8,128)(2,1)}, u32[]{:S(2)}, u32[]{:S(2)}) %collective-permute-start.7) | collective-permute-done | bytes 532512 | tf_op jit(solution)/shard_map/ppermute | solution.py:535
  43.0 2.6 %collective-permute-start.8 = (bf16[2,1040,128]{2,1,0:T(8,128)(2,1)}, bf16[2,1040,128]{2,1,0:T(8,128)(2,1)}, u32[]{:S(2)}, u32[]{:S(2)}) collective-permute-start(bf16[2,1040,128]{2,1,0:T(8,128)(2,1)} %collective-permute-done.7.refs_0_.refs_7_), channel_id=1, source_target_pairs={{0,8},{9,1},{2,10},{11,3},{8,16},{17,9},{10,18},{19,11},{16,24},{2... | collective-permute-start | bytes 1597448 | tf_op jit(solution)/shard_map/ppermute | solution.py:535
  45.6 3.1 %collective-permute-done.5.refs_2_.refs_9_ = bf16[2,1040,128]{2,1,0:T(8,128)(2,1)} collective-permute-done((bf16[2,1040,128]{2,1,0:T(8,128)(2,1)S(1)}, bf16[2,1040,128]{2,1,0:T(8,128)(2,1)}, u32[]{:S(2)}, u32[]{:S(2)}) %collective-permute-start.5) | collective-permute-done | bytes 532512 | tf_op jit(solution)/shard_map/ppermute | solution.py:535
  48.7 2.6 %collective-permute-start.10 = (bf16[2,1040,128]{2,1,0:T(8,128)(2,1)}, bf16[2,1040,128]{2,1,0:T(8,128)(2,1)}, u32[]{:S(2)}, u32[]{:S(2)}) collective-permute-start(bf16[2,1040,128]{2,1,0:T(8,128)(2,1)} %collective-permute-done.5.refs_2_.refs_9_), channel_id=1, source_target_pairs={{0,8},{9,1},{2,10},{11,3},{8,16},{17,9},{10,18},{19,11},{16,24},{2... | collective-permute-start | bytes 1597448 | tf_op jit(solution)/shard_map/ppermute | solution.py:535
  51.4 0.7 pad_maximum_fusion.2
  52.1 0.5 collective-permute-start.15
  52.6 0.1 collective-permute-start.16
  52.7 0.2 copy-done.5
  52.9 0.5 copy-done.6
  53.4 5.3 %project.2.refs_4_ = bf16[24,512,128]{2,1,0:T(8,128)(2,1)} custom-call(bf16[512,1024]{1,0:T(8,128)(2,1)} %get-tuple-element.27.normed, bf16[2,1040,128]{2,1,0:T(8,128)(2,1)} %copy-done, bf16[2,1040,128]{2,1,0:T(8,128)(2,1)} %copy-done.2, bf16[2,1040,128]{2,1,0:T(8,128)(2,1)} %copy-done.3, bf16[2,1040,128]{2,1,0:T(8,128)(2,1)} %copy-done.5, ...), custom_call_target="tpu_custom_call" | custom-call | flops 1000 | bytes 1000 | tf_op jit(solution)/shard_map/project/pallas_call | solution.py:274
  58.7 1.5 %collective-permute-done.10.refs_2_.refs_13_ = bf16[2,1040,128]{2,1,0:T(8,128)(2,1)} collective-permute-done((bf16[2,1040,128]{2,1,0:T(8,128)(2,1)}, bf16[2,1040,128]{2,1,0:T(8,128)(2,1)}, u32[]{:S(2)}, u32[]{:S(2)}) %collective-permute-start.10) | collective-permute-done | bytes 532512 | tf_op jit(solution)/shard_map/ppermute | solution.py:535
  60.3 2.5 %collective-permute-start.14 = (bf16[2,1040,128]{2,1,0:T(8,128)(2,1)}, bf16[2,1040,128]{2,1,0:T(8,128)(2,1)S(1)}, u32[]{:S(2)}, u32[]{:S(2)}) collective-permute-start(bf16[2,1040,128]{2,1,0:T(8,128)(2,1)} %collective-permute-done.8.refs_0_.refs_11_), channel_id=1, source_target_pairs={{0,8},{9,1},{2,10},{11,3},{8,16},{17,9},{10,18},{19,11},{16,24},{2... | collective-permute-start | bytes 1597448 | tf_op jit(solution)/shard_map/ppermute | solution.py:535
  62.7 1.0 select_bitcast_fusion.1
  63.8 1.6 %collective-permute-start.20 = (bf16[2,2,544,128]{3,2,1,0:T(8,128)(2,1)S(1)}, bf16[2,2,544,128]{3,2,1,0:T(8,128)(2,1)S(1)}, u32[]{:S(2)}, u32[]{:S(2)}) collective-permute-start(bf16[2,2,544,128]{3,2,1,0:T(8,128)(2,1)S(1)} %pad_maximum_fusion.refs_0_), channel_id=1, source_target_pairs={{0,8},{9,1},{2,10},{11,3},{8,16},{17,9},{10,18},{19,11},{16,24},{2... | collective-permute-start | bytes 1671176 | tf_op jit(solution)/shard_map/ppermute | solution.py:535
  65.5 4.7 %project.3.refs_6_ = bf16[24,512,128]{2,1,0:T(8,128)(2,1)} custom-call(bf16[512,1024]{1,0:T(8,128)(2,1)} %get-tuple-element.27.normed, bf16[2,1040,128]{2,1,0:T(8,128)(2,1)} %collective-permute-done.7.refs_0_.refs_7_, bf16[2,1040,128]{2,1,0:T(8,128)(2,1)} %collective-permute-done.15.refs_1_.refs_8_, ...), custom_call_target="tpu_custom_call", output_to_operand_aliasing={{}: (5, {})} | custom-call | flops 1000 | bytes 1000 | tf_op jit(solution)/shard_map/project/pallas_call | solution.py:274
  70.2 0.6 collective-permute-start.11
  70.7 0.1 collective-permute-start.17
  70.8 1.7 %collective-permute-done.11.refs_3_.refs_14_ = bf16[2,1040,128]{2,1,0:T(8,128)(2,1)S(1)} collective-permute-done((bf16[2,1040,128]{2,1,0:T(8,128)(2,1)}, bf16[2,1040,128]{2,1,0:T(8,128)(2,1)S(1)}, u32[]{:S(2)}, u32[]{:S(2)}) %collective-permute-start.11) | collective-permute-done | bytes 532512 | tf_op jit(solution)/shard_map/ppermute | solution.py:539
  72.5 3.2 %collective-permute-done.20.refs_1_ = bf16[2,2,544,128]{3,2,1,0:T(8,128)(2,1)S(1)} collective-permute-done((bf16[2,2,544,128]{3,2,1,0:T(8,128)(2,1)S(1)}, bf16[2,2,544,128]{3,2,1,0:T(8,128)(2,1)S(1)}, u32[]{:S(2)}, u32[]{:S(2)}) %collective-permute-start.20) | collective-permute-done | bytes 557088 | tf_op jit(solution)/shard_map/ppermute | solution.py:535
  75.7 2.7 %collective-permute-start.22 = (bf16[2,2,544,128]{3,2,1,0:T(8,128)(2,1)S(1)}, bf16[2,2,544,128]{3,2,1,0:T(8,128)(2,1)S(1)}, u32[]{:S(2)}, u32[]{:S(2)}) collective-permute-start(bf16[2,2,544,128]{3,2,1,0:T(8,128)(2,1)S(1)} %collective-permute-done.20.refs_1_), channel_id=1, source_target_pairs={{0,8},{9,1},{2,10},{11,3},{8,16},{17,9},{10,18},{19,11},{16,24},{2... | collective-permute-start | bytes 1671176 | tf_op jit(solution)/shard_map/ppermute | solution.py:535
  78.4 9.4 %attend.1.refs_0_ = bf16[256,1024]{1,0:T(8,128)(2,1)} custom-call(bf16[512,1024]{1,0:T(8,128)(2,1)} %get-tuple-element.27.normed, f32[2,128,384]{2,1,0:T(8,128)} %get-tuple-element.28.bias, bf16[2,1040,128]{2,1,0:T(8,128)(2,1)} %collective-permute-done.8.refs_0_.refs_11_, bf16[2,1040,128]{2,1,0:T(8,128)(2,1)} %copy-done.8, ...), custom_call_target="tpu_custom_call" | custom-call | flops 1000 | bytes 1000 | tf_op jit(solution)/shard_map/attend/pallas_call | solution.py:332
  87.9 1.6 %collective-permute-start.24 = (bf16[2,2,544,128]{3,2,1,0:T(8,128)(2,1)S(1)}, bf16[2,2,544,128]{3,2,1,0:T(8,128)(2,1)S(1)}, u32[]{:S(2)}, u32[]{:S(2)}) collective-permute-start(bf16[2,2,544,128]{3,2,1,0:T(8,128)(2,1)S(1)} %collective-permute-done.22.refs_3_), channel_id=1, source_target_pairs={{0,8},{9,1},{2,10},{11,3},{8,16},{17,9},{10,18},{19,11},{16,24},{2... | collective-permute-start | bytes 1671176 | tf_op jit(solution)/shard_map/ppermute | solution.py:535
  89.5 5.1 %mix.1 = (bf16[256,1024]{1,0:T(8,128)(2,1)}, bf16[128,1024]{1,0:T(8,128)(2,1)}) custom-call(bf16[256,1024]{1,0:T(8,128)(2,1)} %bitcast.30, f32[1,1024]{1,0:T(1,128)} %bitcast.38, bf16[256,1024]{1,0:T(8,128)(2,1)} %attend.1.refs_0_, bf16[2,1040,128]{2,1,0:T(8,128)(2,1)} %copy-done, bf16[2,1040,128]{2,1,0:T(8,128)(2,1)} %copy-done.2, ...), custom_call_target="tpu_custom_call" | custom-call | flops 1000 | bytes 1000 | tf_op jit(solution)/shard_map/mix/pallas_call | solution.py:412
  94.6 3.4 %all-to-all-start = ((bf16[8,16,1024]{2,1,0:T(8,128)(2,1)}), bf16[8,16,1024]{2,1,0:T(8,128)(2,1)S(1)}, u32[]{:S(2)}, u32[]{:S(2)}) async-start(bf16[8,16,1024]{2,1,0:T(8,128)(2,1)} %bitcast.33), calls=%async_computation | async-start | bytes 524288 | tf_op jit(solution)/shard_map/all_to_all | solution.py:649
  98.1 0.8 dynamic-slice_bitcast_fusion
  98.9 1.9 %collective-permute-start.26 = (bf16[2,544,128]{2,1,0:T(8,128)(2,1)}, bf16[2,544,128]{2,1,0:T(8,128)(2,1)S(1)}, u32[]{:S(2)}, u32[]{:S(2)}) collective-permute-start(bf16[2,544,128]{2,1,0:T(8,128)(2,1)} %dynamic-slice_bitcast_fusion), channel_id=1, source_target_pairs={{0,8},{9,1},{2,10},{11,3},{8,16},{17,9},{10,18},{19,11},{16,24},{2... | collective-permute-start | bytes 835592 | tf_op jit(solution)/shard_map/ppermute | solution.py:535
  100.8 0.5 collective-permute-start.23
  101.4 6.1 %all-to-all-done = bf16[8,16,1024]{2,1,0:T(8,128)(2,1)S(1)} async-done(((bf16[8,16,1024]{2,1,0:T(8,128)(2,1)}), bf16[8,16,1024]{2,1,0:T(8,128)(2,1)S(1)}, u32[]{:S(2)}, u32[]{:S(2)}) %all-to-all-start) | async-done | bytes 262176 | tf_op jit(solution)/shard_map/all_to_all | solution.py:649
  107.6 1.5 %collective-permute-done.27.refs_8_ = bf16[2,544,128]{2,1,0:T(8,128)(2,1)S(1)} collective-permute-done((bf16[2,544,128]{2,1,0:T(8,128)(2,1)S(1)}, bf16[2,544,128]{2,1,0:T(8,128)(2,1)S(1)}, u32[]{:S(2)}, u32[]{:S(2)}) %collective-permute-start.27) | collective-permute-done | bytes 278560 | tf_op jit(solution)/shard_map/ppermute | solution.py:539
  109.1 0.7 copy-done.18
  109.8 10.9 %decode.1 = bf16[96,256]{1,0:T(8,128)(2,1)} custom-call(bf16[256,1024]{1,0:T(8,128)(2,1)} %bitcast.32, bf16[256,1024]{1,0:T(8,128)(2,1)} %get-tuple-element.31.decoded, bf16[128,1024]{1,0:T(8,128)(2,1)} %bitcast.31, f32[256,256]{1,0:T(8,128)} %get-tuple-element.33.here, f32[256,128]{1,0:T(8,128)} %get-tuple-element.34.there, ...), custom_call_target="tpu_custom_call" | custom-call | flops 1000 | bytes 1000 | tf_op jit(solution)/shard_map/decode/pallas_call | solution.py:490
  (74 shorter events, 0.4 us)
Async XLA Ops:
  0.0 39.8 %copy-start.22 = (bf16[256,12]{0,1:T(8,128)(2,1)S(1)}, bf16[256,12]{0,1:T(8,128)(2,1)}, u32[]{:S(2)}) copy-start(bf16[256,12]{0,1:T(8,128)(2,1)} %param.20) | copy-start | bytes 18436
  0.0 39.8 %copy-start.21 = (bf16[256,256]{1,0:T(8,128)(2,1)S(1)}, bf16[256,256]{1,0:T(8,128)(2,1)}, u32[]{:S(2)}) copy-start(bf16[256,256]{1,0:T(8,128)(2,1)} %param.19) | copy-start | bytes 393220
  3.1 9.5 %collective-permute-start.2 = (bf16[1040,128]{1,0:T(8,128)(2,1)}, bf16[1040,128]{1,0:T(8,128)(2,1)S(1)}, u32[]{:S(2)}, u32[]{:S(2)}) collective-permute-start(bf16[1040,128]{1,0:T(8,128)(2,1)} %get-tuple-element.24), channel_id=1, source_target_pairs={{0,2},{1,3},{2,0},{3,1},{4,6},{5,7},{6,4},{7,5},{8,10},{9,11},{10,... | collective-permute-start | bytes 798728 | tf_op jit(solution)/shard_map/ppermute | solution.py:517
  7.1 14.3 %collective-permute-start = (bf16[128,1024]{1,0:T(8,128)(2,1)S(1)}, bf16[128,1024]{1,0:T(8,128)(2,1)S(1)}, u32[]{:S(2)}, u32[]{:S(2)}) collective-permute-start(bf16[128,1024]{1,0:T(8,128)(2,1)S(1)} %get-tuple-element.46), channel_id=1, source_target_pairs={{0,4},{4,8},{8,12},{12,16},{16,20},{20,24},{24,28},{1,5},{5,9},{9,... | collective-permute-start | bytes 786440 | tf_op jit(solution)/shard_map/ppermute | solution.py:593
  10.5 10.9 %collective-permute-start.1 = (bf16[128,1024]{1,0:T(8,128)(2,1)S(1)}, bf16[128,1024]{1,0:T(8,128)(2,1)S(1)}, u32[]{:S(2)}, u32[]{:S(2)}) collective-permute-start(bf16[128,1024]{1,0:T(8,128)(2,1)S(1)} %get-tuple-element.45), channel_id=1, source_target_pairs={{4,0},{8,4},{12,8},{16,12},{20,16},{24,20},{28,24},{5,1},{9,5},{13... | collective-permute-start | bytes 786440 | tf_op jit(solution)/shard_map/ppermute | solution.py:594
  13.6 39.1 %copy-start = (bf16[2,1040,128]{2,1,0:T(8,128)(2,1)}, bf16[2,1040,128]{2,1,0:T(8,128)(2,1)S(1)}, u32[]{:S(2)}) copy-start(bf16[2,1040,128]{2,1,0:T(8,128)(2,1)S(1)} %pad_maximum_fusion.1.refs_0_.refs_1_) | copy-start | bytes 1597444
  21.4 5.4 %copy-start.19 = (bf16[128,1024]{1,0:T(8,128)(2,1)}, bf16[128,1024]{1,0:T(8,128)(2,1)S(1)}, u32[]{:S(2)}) copy-start(bf16[128,1024]{1,0:T(8,128)(2,1)S(1)} %collective-permute-done.left) | copy-start | bytes 786436
  21.4 5.4 %copy-start.20 = (bf16[128,1024]{1,0:T(8,128)(2,1)}, bf16[128,1024]{1,0:T(8,128)(2,1)S(1)}, u32[]{:S(2)}) copy-start(bf16[128,1024]{1,0:T(8,128)(2,1)S(1)} %collective-permute-done.1.right) | copy-start | bytes 786436
  21.4 3.4 %collective-permute-start.3 = (bf16[2,1040,128]{2,1,0:T(8,128)(2,1)S(1)}, bf16[2,1040,128]{2,1,0:T(8,128)(2,1)S(1)}, u32[]{:S(2)}, u32[]{:S(2)}) collective-permute-start(bf16[2,1040,128]{2,1,0:T(8,128)(2,1)S(1)} %pad_maximum_fusion.1.refs_0_.refs_1_), channel_id=1, source_target_pairs={{0,1},{1,0},{2,3},{3,2},{4,5},{5,4},{6,7},{7,6},{8,9},{9,8},{10,11... | collective-permute-start | bytes 1597448 | tf_op jit(solution)/shard_map/ppermute | solution.py:539
  21.4 10.2 %collective-permute-start.6 = (bf16[2,1040,128]{2,1,0:T(8,128)(2,1)S(1)}, bf16[2,1040,128]{2,1,0:T(8,128)(2,1)S(1)}, u32[]{:S(2)}, u32[]{:S(2)}) collective-permute-start(bf16[2,1040,128]{2,1,0:T(8,128)(2,1)S(1)} %pad_maximum_fusion.1.refs_0_.refs_1_), channel_id=1, source_target_pairs={{0,8},{9,1},{2,10},{11,3},{8,16},{17,9},{10,18},{19,11},{16,24},{2... | collective-permute-start | bytes 1597448 | tf_op jit(solution)/shard_map/ppermute | solution.py:535
  24.8 27.9 %copy-start.2 = (bf16[2,1040,128]{2,1,0:T(8,128)(2,1)}, bf16[2,1040,128]{2,1,0:T(8,128)(2,1)S(1)}, u32[]{:S(2)}) copy-start(bf16[2,1040,128]{2,1,0:T(8,128)(2,1)S(1)} %collective-permute-done.3.refs_1_.refs_2_) | copy-start | bytes 1597444
  24.8 12.5 %collective-permute-start.4 = (bf16[2,1040,128]{2,1,0:T(8,128)(2,1)S(1)}, bf16[2,1040,128]{2,1,0:T(8,128)(2,1)S(1)}, u32[]{:S(2)}, u32[]{:S(2)}) collective-permute-start(bf16[2,1040,128]{2,1,0:T(8,128)(2,1)S(1)} %collective-permute-done.3.refs_1_.refs_2_), channel_id=1, source_target_pairs={{0,8},{9,1},{2,10},{11,3},{8,16},{17,9},{10,18},{19,11},{16,24},{2... | collective-permute-start | bytes 1597448 | tf_op jit(solution)/shard_map/ppermute | solution.py:535
  31.6 21.1 %copy-start.3 = (bf16[2,1040,128]{2,1,0:T(8,128)(2,1)}, bf16[2,1040,128]{2,1,0:T(8,128)(2,1)S(1)}, u32[]{:S(2)}) copy-start(bf16[2,1040,128]{2,1,0:T(8,128)(2,1)S(1)} %collective-permute-done.6.refs_2_.refs_3_) | copy-start | bytes 1597444
  31.6 11.4 %collective-permute-start.7 = (bf16[2,1040,128]{2,1,0:T(8,128)(2,1)S(1)}, bf16[2,1040,128]{2,1,0:T(8,128)(2,1)}, u32[]{:S(2)}, u32[]{:S(2)}) collective-permute-start(bf16[2,1040,128]{2,1,0:T(8,128)(2,1)S(1)} %collective-permute-done.6.refs_2_.refs_3_), channel_id=1, source_target_pairs={{0,8},{9,1},{2,10},{11,3},{8,16},{17,9},{10,18},{19,11},{16,24},{2... | collective-permute-start | bytes 1597448 | tf_op jit(solution)/shard_map/ppermute | solution.py:535
  37.3 15.4 %copy-start.4 = (bf16[2,1040,128]{2,1,0:T(8,128)(2,1)}, bf16[2,1040,128]{2,1,0:T(8,128)(2,1)S(1)}, u32[]{:S(2)}) copy-start(bf16[2,1040,128]{2,1,0:T(8,128)(2,1)S(1)} %collective-permute-done.4.refs_4_.refs_5_) | copy-start | bytes 1597444
  37.3 11.4 %collective-permute-start.5 = (bf16[2,1040,128]{2,1,0:T(8,128)(2,1)S(1)}, bf16[2,1040,128]{2,1,0:T(8,128)(2,1)}, u32[]{:S(2)}, u32[]{:S(2)}) collective-permute-start(bf16[2,1040,128]{2,1,0:T(8,128)(2,1)S(1)} %collective-permute-done.4.refs_4_.refs_5_), channel_id=1, source_target_pairs={{0,8},{9,1},{2,10},{11,3},{8,16},{17,9},{10,18},{19,11},{16,24},{2... | collective-permute-start | bytes 1597448 | tf_op jit(solution)/shard_map/ppermute | solution.py:535
  39.9 11.5 %collective-permute-start.18 = (bf16[544,128]{1,0:T(8,128)(2,1)S(1)}, bf16[544,128]{1,0:T(8,128)(2,1)S(1)}, u32[]{:S(2)}, u32[]{:S(2)}) collective-permute-start(bf16[544,128]{1,0:T(8,128)(2,1)S(1)} %pad_maximum_fusion.3), channel_id=1, source_target_pairs={{0,2},{1,3},{2,0},{3,1},{4,6},{5,7},{6,4},{7,5},{8,10},{9,11},{10,... | collective-permute-start | bytes 417800 | tf_op jit(solution)/shard_map/ppermute | solution.py:517
  40.5 11.6 %collective-permute-start.12 = (bf16[2,1040,128]{2,1,0:T(8,128)(2,1)S(1)}, bf16[2,1040,128]{2,1,0:T(8,128)(2,1)S(1)}, u32[]{:S(2)}, u32[]{:S(2)}) collective-permute-start(bf16[2,1040,128]{2,1,0:T(8,128)(2,1)S(1)} %collective-permute-done.6.refs_2_.refs_3_), channel_id=1, source_target_pairs={{0,1},{1,0},{2,3},{3,2},{4,5},{5,4},{6,7},{7,6},{8,9},{9,8},{10,11... | collective-permute-start | bytes 1597448 | tf_op jit(solution)/shard_map/ppermute | solution.py:539
  40.5 12.1 %collective-permute-start.13 = (bf16[2,1040,128]{2,1,0:T(8,128)(2,1)S(1)}, bf16[2,1040,128]{2,1,0:T(8,128)(2,1)S(1)}, u32[]{:S(2)}, u32[]{:S(2)}) collective-permute-start(bf16[2,1040,128]{2,1,0:T(8,128)(2,1)S(1)} %collective-permute-done.4.refs_4_.refs_5_), channel_id=1, source_target_pairs={{0,1},{1,0},{2,3},{3,2},{4,5},{5,4},{6,7},{7,6},{8,9},{9,8},{10,11... | collective-permute-start | bytes 1597448 | tf_op jit(solution)/shard_map/ppermute | solution.py:539
  43.0 15.7 %collective-permute-start.8 = (bf16[2,1040,128]{2,1,0:T(8,128)(2,1)}, bf16[2,1040,128]{2,1,0:T(8,128)(2,1)}, u32[]{:S(2)}, u32[]{:S(2)}) collective-permute-start(bf16[2,1040,128]{2,1,0:T(8,128)(2,1)} %collective-permute-done.7.refs_0_.refs_7_), channel_id=1, source_target_pairs={{0,8},{9,1},{2,10},{11,3},{8,16},{17,9},{10,18},{19,11},{16,24},{2... | collective-permute-start | bytes 1597448 | tf_op jit(solution)/shard_map/ppermute | solution.py:535
  48.7 11.5 %collective-permute-start.10 = (bf16[2,1040,128]{2,1,0:T(8,128)(2,1)}, bf16[2,1040,128]{2,1,0:T(8,128)(2,1)}, u32[]{:S(2)}, u32[]{:S(2)}) collective-permute-start(bf16[2,1040,128]{2,1,0:T(8,128)(2,1)} %collective-permute-done.5.refs_2_.refs_9_), channel_id=1, source_target_pairs={{0,8},{9,1},{2,10},{11,3},{8,16},{17,9},{10,18},{19,11},{16,24},{2... | collective-permute-start | bytes 1597448 | tf_op jit(solution)/shard_map/ppermute | solution.py:535
  52.1 10.6 %collective-permute-start.19 = (bf16[2,544,128]{2,1,0:T(8,128)(2,1)}, bf16[2,544,128]{2,1,0:T(8,128)(2,1)}, u32[]{:S(2)}, u32[]{:S(2)}) collective-permute-start(bf16[2,544,128]{2,1,0:T(8,128)(2,1)} %pad_maximum_fusion.2), channel_id=1, source_target_pairs={{0,1},{1,0},{2,3},{3,2},{4,5},{5,4},{6,7},{7,6},{8,9},{9,8},{10,11... | collective-permute-start | bytes 835592 | tf_op jit(solution)/shard_map/ppermute | solution.py:539
  52.1 11.7 %collective-permute-start.15 = (bf16[2,1040,128]{2,1,0:T(8,128)(2,1)}, bf16[2,1040,128]{2,1,0:T(8,128)(2,1)}, u32[]{:S(2)}, u32[]{:S(2)}) collective-permute-start(bf16[2,1040,128]{2,1,0:T(8,128)(2,1)} %collective-permute-done.7.refs_0_.refs_7_), channel_id=1, source_target_pairs={{0,1},{1,0},{2,3},{3,2},{4,5},{5,4},{6,7},{7,6},{8,9},{9,8},{10,11... | collective-permute-start | bytes 1597448 | tf_op jit(solution)/shard_map/ppermute | solution.py:539
  52.6 11.2 %collective-permute-start.16 = (bf16[2,1040,128]{2,1,0:T(8,128)(2,1)}, bf16[2,1040,128]{2,1,0:T(8,128)(2,1)}, u32[]{:S(2)}, u32[]{:S(2)}) collective-permute-start(bf16[2,1040,128]{2,1,0:T(8,128)(2,1)} %collective-permute-done.5.refs_2_.refs_9_), channel_id=1, source_target_pairs={{0,1},{1,0},{2,3},{3,2},{4,5},{5,4},{6,7},{7,6},{8,9},{9,8},{10,11... | collective-permute-start | bytes 1597448 | tf_op jit(solution)/shard_map/ppermute | solution.py:539
  60.3 10.5 %collective-permute-start.14 = (bf16[2,1040,128]{2,1,0:T(8,128)(2,1)}, bf16[2,1040,128]{2,1,0:T(8,128)(2,1)S(1)}, u32[]{:S(2)}, u32[]{:S(2)}) collective-permute-start(bf16[2,1040,128]{2,1,0:T(8,128)(2,1)} %collective-permute-done.8.refs_0_.refs_11_), channel_id=1, source_target_pairs={{0,8},{9,1},{2,10},{11,3},{8,16},{17,9},{10,18},{19,11},{16,24},{2... | collective-permute-start | bytes 1597448 | tf_op jit(solution)/shard_map/ppermute | solution.py:535
  63.8 6.3 %copy-start.1 = (bf16[2,2,544,128]{3,2,1,0:T(8,128)(2,1)}, bf16[2,2,544,128]{3,2,1,0:T(8,128)(2,1)S(1)}, u32[]{:S(2)}) copy-start(bf16[2,2,544,128]{3,2,1,0:T(8,128)(2,1)S(1)} %pad_maximum_fusion.refs_0_) | copy-start | bytes 1671172
  63.8 11.9 %collective-permute-start.20 = (bf16[2,2,544,128]{3,2,1,0:T(8,128)(2,1)S(1)}, bf16[2,2,544,128]{3,2,1,0:T(8,128)(2,1)S(1)}, u32[]{:S(2)}, u32[]{:S(2)}) collective-permute-start(bf16[2,2,544,128]{3,2,1,0:T(8,128)(2,1)S(1)} %pad_maximum_fusion.refs_0_), channel_id=1, source_target_pairs={{0,8},{9,1},{2,10},{11,3},{8,16},{17,9},{10,18},{19,11},{16,24},{2... | collective-permute-start | bytes 1671176 | tf_op jit(solution)/shard_map/ppermute | solution.py:535
  65.5 5.4 %collective-permute-start.9 = (bf16[2,1040,128]{2,1,0:T(8,128)(2,1)}, bf16[2,1040,128]{2,1,0:T(8,128)(2,1)S(1)}, u32[]{:S(2)}, u32[]{:S(2)}) collective-permute-start(bf16[2,1040,128]{2,1,0:T(8,128)(2,1)} %collective-permute-done.8.refs_0_.refs_11_), channel_id=1, source_target_pairs={{0,1},{1,0},{2,3},{3,2},{4,5},{5,4},{6,7},{7,6},{8,9},{9,8},{10,11... | collective-permute-start | bytes 1597448 | tf_op jit(solution)/shard_map/ppermute | solution.py:539
  70.2 2.3 %collective-permute-start.11 = (bf16[2,1040,128]{2,1,0:T(8,128)(2,1)}, bf16[2,1040,128]{2,1,0:T(8,128)(2,1)S(1)}, u32[]{:S(2)}, u32[]{:S(2)}) collective-permute-start(bf16[2,1040,128]{2,1,0:T(8,128)(2,1)} %collective-permute-done.10.refs_2_.refs_13_), channel_id=1, source_target_pairs={{0,1},{1,0},{2,3},{3,2},{4,5},{5,4},{6,7},{7,6},{8,9},{9,8},{10,11... | collective-permute-start | bytes 1597448 | tf_op jit(solution)/shard_map/ppermute | solution.py:539
  70.7 7.7 %copy-start.7 = (bf16[2,1040,128]{2,1,0:T(8,128)(2,1)}, bf16[2,1040,128]{2,1,0:T(8,128)(2,1)S(1)}, u32[]{:S(2)}) copy-start(bf16[2,1040,128]{2,1,0:T(8,128)(2,1)S(1)} %collective-permute-done.14.refs_4_.refs_15_) | copy-start | bytes 1597444
  70.7 5.0 %collective-permute-start.17 = (bf16[2,1040,128]{2,1,0:T(8,128)(2,1)S(1)}, bf16[2,1040,128]{2,1,0:T(8,128)(2,1)S(1)}, u32[]{:S(2)}, u32[]{:S(2)}) collective-permute-start(bf16[2,1040,128]{2,1,0:T(8,128)(2,1)S(1)} %collective-permute-done.14.refs_4_.refs_15_), channel_id=1, source_target_pairs={{0,1},{1,0},{2,3},{3,2},{4,5},{5,4},{6,7},{7,6},{8,9},{9,8},{10,11... | collective-permute-start | bytes 1597448 | tf_op jit(solution)/shard_map/ppermute | solution.py:539
  70.8 7.6 %copy-start.8 = (bf16[2,1040,128]{2,1,0:T(8,128)(2,1)}, bf16[2,1040,128]{2,1,0:T(8,128)(2,1)S(1)}, u32[]{:S(2)}) copy-start(bf16[2,1040,128]{2,1,0:T(8,128)(2,1)S(1)} %collective-permute-done.9.refs_1_.refs_12_) | copy-start | bytes 1597444
  72.5 6.0 %copy-start.9 = (bf16[2,1040,128]{2,1,0:T(8,128)(2,1)}, bf16[2,1040,128]{2,1,0:T(8,128)(2,1)S(1)}, u32[]{:S(2)}) copy-start(bf16[2,1040,128]{2,1,0:T(8,128)(2,1)S(1)} %collective-permute-done.11.refs_3_.refs_14_) | copy-start | bytes 1597444
  75.7 25.1 %copy-start.13 = (bf16[2,2,544,128]{3,2,1,0:T(8,128)(2,1)}, bf16[2,2,544,128]{3,2,1,0:T(8,128)(2,1)S(1)}, u32[]{:S(2)}) copy-start(bf16[2,2,544,128]{3,2,1,0:T(8,128)(2,1)S(1)} %collective-permute-done.20.refs_1_) | copy-start | bytes 1671172
  75.7 2.7 %copy-start.10 = (bf16[2,1040,128]{2,1,0:T(8,128)(2,1)}, bf16[2,1040,128]{2,1,0:T(8,128)(2,1)S(1)}, u32[]{:S(2)}) copy-start(bf16[2,1040,128]{2,1,0:T(8,128)(2,1)S(1)} %collective-permute-done.17.refs_5_.refs_16_) | copy-start | bytes 1597444
  75.7 12.2 %collective-permute-start.22 = (bf16[2,2,544,128]{3,2,1,0:T(8,128)(2,1)S(1)}, bf16[2,2,544,128]{3,2,1,0:T(8,128)(2,1)S(1)}, u32[]{:S(2)}, u32[]{:S(2)}) collective-permute-start(bf16[2,2,544,128]{3,2,1,0:T(8,128)(2,1)S(1)} %collective-permute-done.20.refs_1_), channel_id=1, source_target_pairs={{0,8},{9,1},{2,10},{11,3},{8,16},{17,9},{10,18},{19,11},{16,24},{2... | collective-permute-start | bytes 1671176 | tf_op jit(solution)/shard_map/ppermute | solution.py:535
  87.9 12.9 %copy-start.14 = (bf16[2,2,544,128]{3,2,1,0:T(8,128)(2,1)}, bf16[2,2,544,128]{3,2,1,0:T(8,128)(2,1)S(1)}, u32[]{:S(2)}) copy-start(bf16[2,2,544,128]{3,2,1,0:T(8,128)(2,1)S(1)} %collective-permute-done.22.refs_3_) | copy-start | bytes 1671172
  87.9 10.2 %collective-permute-start.24 = (bf16[2,2,544,128]{3,2,1,0:T(8,128)(2,1)S(1)}, bf16[2,2,544,128]{3,2,1,0:T(8,128)(2,1)S(1)}, u32[]{:S(2)}, u32[]{:S(2)}) collective-permute-start(bf16[2,2,544,128]{3,2,1,0:T(8,128)(2,1)S(1)} %collective-permute-done.22.refs_3_), channel_id=1, source_target_pairs={{0,8},{9,1},{2,10},{11,3},{8,16},{17,9},{10,18},{19,11},{16,24},{2... | collective-permute-start | bytes 1671176 | tf_op jit(solution)/shard_map/ppermute | solution.py:535
  94.6 12.8 %all-to-all-start = ((bf16[8,16,1024]{2,1,0:T(8,128)(2,1)}), bf16[8,16,1024]{2,1,0:T(8,128)(2,1)S(1)}, u32[]{:S(2)}, u32[]{:S(2)}) async-start(bf16[8,16,1024]{2,1,0:T(8,128)(2,1)} %bitcast.33), calls=%async_computation | async-start | bytes 524288 | tf_op jit(solution)/shard_map/all_to_all | solution.py:649
  98.1 11.0 %copy-start.11 = (bf16[2,2,544,128]{3,2,1,0:T(8,128)(2,1)}, bf16[2,2,544,128]{3,2,1,0:T(8,128)(2,1)S(1)}, u32[]{:S(2)}) copy-start(bf16[2,2,544,128]{3,2,1,0:T(8,128)(2,1)S(1)} %collective-permute-done.24.refs_5_) | copy-start | bytes 1671172
  98.9 8.6 %collective-permute-start.26 = (bf16[2,544,128]{2,1,0:T(8,128)(2,1)}, bf16[2,544,128]{2,1,0:T(8,128)(2,1)S(1)}, u32[]{:S(2)}, u32[]{:S(2)}) collective-permute-start(bf16[2,544,128]{2,1,0:T(8,128)(2,1)} %dynamic-slice_bitcast_fusion), channel_id=1, source_target_pairs={{0,8},{9,1},{2,10},{11,3},{8,16},{17,9},{10,18},{19,11},{16,24},{2... | collective-permute-start | bytes 835592 | tf_op jit(solution)/shard_map/ppermute | solution.py:535
  100.8 6.7 %collective-permute-start.21 = (bf16[2,2,544,128]{3,2,1,0:T(8,128)(2,1)S(1)}, bf16[2,2,544,128]{3,2,1,0:T(8,128)(2,1)S(1)}, u32[]{:S(2)}, u32[]{:S(2)}) collective-permute-start(bf16[2,2,544,128]{3,2,1,0:T(8,128)(2,1)S(1)} %collective-permute-done.20.refs_1_), channel_id=1, source_target_pairs={{0,1},{1,0},{2,3},{3,2},{4,5},{5,4},{6,7},{7,6},{8,9},{9,8},{10,11... | collective-permute-start | bytes 1671176 | tf_op jit(solution)/shard_map/ppermute | solution.py:539
  100.8 6.7 %collective-permute-start.23 = (bf16[2,2,544,128]{3,2,1,0:T(8,128)(2,1)S(1)}, bf16[2,2,544,128]{3,2,1,0:T(8,128)(2,1)S(1)}, u32[]{:S(2)}, u32[]{:S(2)}) collective-permute-start(bf16[2,2,544,128]{3,2,1,0:T(8,128)(2,1)S(1)} %collective-permute-done.22.refs_3_), channel_id=1, source_target_pairs={{0,1},{1,0},{2,3},{3,2},{4,5},{5,4},{6,7},{7,6},{8,9},{9,8},{10,11... | collective-permute-start | bytes 1671176 | tf_op jit(solution)/shard_map/ppermute | solution.py:539
  101.3 7.8 %collective-permute-start.25 = (bf16[2,2,544,128]{3,2,1,0:T(8,128)(2,1)S(1)}, bf16[2,2,544,128]{3,2,1,0:T(8,128)(2,1)}, u32[]{:S(2)}, u32[]{:S(2)}) collective-permute-start(bf16[2,2,544,128]{3,2,1,0:T(8,128)(2,1)S(1)} %collective-permute-done.24.refs_5_), channel_id=1, source_target_pairs={{0,1},{1,0},{2,3},{3,2},{4,5},{5,4},{6,7},{7,6},{8,9},{9,8},{10,11... | collective-permute-start | bytes 1671176 | tf_op jit(solution)/shard_map/ppermute | solution.py:539
  107.5 1.6 %copy-start.12 = (bf16[8,16,1024]{2,1,0:T(8,128)(2,1)}, bf16[8,16,1024]{2,1,0:T(8,128)(2,1)S(1)}, u32[]{:S(2)}) copy-start(bf16[8,16,1024]{2,1,0:T(8,128)(2,1)S(1)} %all-to-all-done) | copy-start | bytes 786436
  107.5 1.6 %copy-start.17 = (bf16[2,544,128]{2,1,0:T(8,128)(2,1)}, bf16[2,544,128]{2,1,0:T(8,128)(2,1)S(1)}, u32[]{:S(2)}) copy-start(bf16[2,544,128]{2,1,0:T(8,128)(2,1)S(1)} %collective-permute-done.26.refs_7_) | copy-start | bytes 835588
  107.5 1.6 %collective-permute-start.27 = (bf16[2,544,128]{2,1,0:T(8,128)(2,1)S(1)}, bf16[2,544,128]{2,1,0:T(8,128)(2,1)S(1)}, u32[]{:S(2)}, u32[]{:S(2)}) collective-permute-start(bf16[2,544,128]{2,1,0:T(8,128)(2,1)S(1)} %collective-permute-done.26.refs_7_), channel_id=1, source_target_pairs={{0,1},{1,0},{2,3},{3,2},{4,5},{5,4},{6,7},{7,6},{8,9},{9,8},{10,11... | collective-permute-start | bytes 835592 | tf_op jit(solution)/shard_map/ppermute | solution.py:539
  107.5 1.6 %copy-start.15 = (bf16[2,2,544,128]{3,2,1,0:T(8,128)(2,1)}, bf16[2,2,544,128]{3,2,1,0:T(8,128)(2,1)S(1)}, u32[]{:S(2)}) copy-start(bf16[2,2,544,128]{3,2,1,0:T(8,128)(2,1)S(1)} %collective-permute-done.21.refs_2_) | copy-start | bytes 1671172
  (4 other events, 3.9 us)

commit v3 on v2

--- a/solution.py
+++ b/solution.py
@@ -557,11 +557,10 @@
     return block, [(block, (step, None)), (swap_core(block), (GROUPS - step, None))]
 
 
-def last_step(block, gate):
+def last_step(block):
     half = lax.dynamic_index_in_dim(block, lax.axis_index("band") % 2, 0, keepdims=False)
     half = carry(half)
-    handed, _ = lax.optimization_barrier((half, gate))
-    return [(half, (GROUPS // 2, 0)), (swap_core(handed), (GROUPS // 2, 1))]
+    return [(half, (GROUPS // 2, 0)), (swap_core(half), (GROUPS // 2, 1))]
 
 
 def whole_blocks(*weights):
@@ -651,7 +650,7 @@
     )
     if riding:
         block, _ = lax.optimization_barrier((block, found))
-        later += last_step(block, fetched)
+        later += last_step(block)
     layout = tuple(at for _, at in later)
     pieces = [piece for piece, _ in later]
     fields = decode(

time: 121 us -> 126 us (1.041)
  waiting for transfers between devices: 32.3 us -> 36.7 us
    ppermute x11, waiting for transfers between devices: 14.5 us -> 18.5 us  [carry(): return lax.ppermute(block, ('seq', 'band'), pairs)]
    all_to_all x1, waiting for transfers between devices: 6.07 us -> 8.03 us  [local(): lax.all_to_all(found.reshape(shards, SLOTS, width), 'seq', split_axis=0,...]
    ppermute x13, waiting for transfers between devices: 3.19 us -> 1.69 us  [swap_core(): return lax.ppermute(block, 'band', [(i, i ^ 1) for i in range(BANDS)])]
  transfers between devices with their start and end apart: 29 -> 29, of which waited for: 11 -> 12; matrix products, arithmetic and copies ran while one was open for 4% -> 4% of each run, Pallas kernels for 23% -> 22%
where the time goes in v3:
time: 126 us; the launch traced here: 125 us
  Pallas kernels  42 us (33%)
  starting transfers between devices  39.7 us (32%)
  waiting for transfers between devices  36.7 us (29%)
  local copies, waits for them, and re-layouts  3.68 us (3%)
  other arithmetic  2.87 us (2%)
    ppermute x11, starting transfers between devices, carry(): return lax.ppermute(block, ('seq', 'band'), pairs)  25.5 us
    ppermute x11, waiting for transfers between devices, carry(): return lax.ppermute(block, ('seq', 'band'), pairs)  18.5 us
    pallas_call x1, Pallas kernels, decode(): pl.pallas_call(functools.partial(decode_kernel, layout, outputs // GROUPS...  10.9 us
    pallas_call x2, Pallas kernels, project(): pl.pallas_call(functools.partial(project_kernel, layout, riding), out_sha...  9.96 us
    pallas_call x1, Pallas kernels, attend(): pl.pallas_call(functools.partial(attend_kernel, layout, ready, riding), o...  9.46 us
    all_to_all x1, waiting for transfers between devices, local(): lax.all_to_all(found.reshape(shards, SLOTS, width), 'seq', split_axis=0,...  8.03 us
    ppermute x1, waiting for transfers between devices, local(): left = lax.ppermute(states[tok - HALF:], 'seq', up)  7.72 us
    pallas_call x1, Pallas kernels, mix(): pl.pallas_call(functools.partial(mix_kernel, layout, ids is None), out_sh...  5.13 us
  transfers between devices with their start and end apart: 29, of which 12 were waited for; matrix products, arithmetic and copies ran while one was open for 4% of the time, Pallas kernels for 22%

profile of v3, /device:TPU:0, one launch (start us, length us, event | category | flops | bytes accessed | tf_op | source)
XLA Modules:
  0.0 125.4 jit_solution(8115364224320705189)
XLA Ops:
  0.0 3.0 %tables.1 = (f32[256,128]{1,0:T(8,128)}, bf16[1,128]{1,0:T(2,128)(2,1)}, bf16[1040,128]{1,0:T(8,128)(2,1)}) custom-call(s32[8,256]{1,0:T(8,128)} %bitcast.34, s32[1,256]{1,0:T(1,128)} %bitcast.39, s32[1,128]{1,0:T(1,128)} %constant.32.clone.low, f32[1,128]{1,0:T(1,128)} %constant.33.clone.rank, bf16[256,256]{1,0:T(8,128)(2,1)} %constant.34.clone.tri, ...), custom_call_target="tpu_custom_call" | custom-call | flops 1000 | bytes 1000 | tf_op jit(solution)/shard_map/tables/pallas_call | solution.py:181
  3.0 2.9 %collective-permute-start.2 = (bf16[1040,128]{1,0:T(8,128)(2,1)}, bf16[1040,128]{1,0:T(8,128)(2,1)S(1)}, u32[]{:S(2)}, u32[]{:S(2)}) collective-permute-start(bf16[1040,128]{1,0:T(8,128)(2,1)} %get-tuple-element.23), channel_id=1, source_target_pairs={{0,2},{1,3},{2,0},{3,1},{4,6},{5,7},{6,4},{7,5},{8,10},{9,11},{10,... | collective-permute-start | bytes 798728 | tf_op jit(solution)/shard_map/ppermute | solution.py:517
  6.0 1.1 slice_bitcast_fusion
  7.0 3.4 %collective-permute-start = (bf16[128,1024]{1,0:T(8,128)(2,1)S(1)}, bf16[128,1024]{1,0:T(8,128)(2,1)S(1)}, u32[]{:S(2)}, u32[]{:S(2)}) collective-permute-start(bf16[128,1024]{1,0:T(8,128)(2,1)S(1)} %get-tuple-element.44), channel_id=1, source_target_pairs={{0,4},{4,8},{8,12},{12,16},{16,20},{20,24},{24,28},{1,5},{5,9},{9,... | collective-permute-start | bytes 786440 | tf_op jit(solution)/shard_map/ppermute | solution.py:592
  10.5 1.3 %collective-permute-start.1 = (bf16[128,1024]{1,0:T(8,128)(2,1)S(1)}, bf16[128,1024]{1,0:T(8,128)(2,1)S(1)}, u32[]{:S(2)}, u32[]{:S(2)}) collective-permute-start(bf16[128,1024]{1,0:T(8,128)(2,1)S(1)} %get-tuple-element.43), channel_id=1, source_target_pairs={{4,0},{8,4},{12,8},{16,12},{20,16},{24,20},{28,24},{5,1},{9,5},{13... | collective-permute-start | bytes 786440 | tf_op jit(solution)/shard_map/ppermute | solution.py:593
  11.8 0.8 collective-permute-done.2
  12.6 1.0 select_bitcast_fusion.3
  13.6 7.7 %collective-permute-done.left = bf16[128,1024]{1,0:T(8,128)(2,1)S(1)} collective-permute-done((bf16[128,1024]{1,0:T(8,128)(2,1)S(1)}, bf16[128,1024]{1,0:T(8,128)(2,1)S(1)}, u32[]{:S(2)}, u32[]{:S(2)}) %collective-permute-start) | collective-permute-done | bytes 262176 | tf_op jit(solution)/shard_map/ppermute | solution.py:592
  21.4 3.4 %collective-permute-start.6 = (bf16[2,1040,128]{2,1,0:T(8,128)(2,1)S(1)}, bf16[2,1040,128]{2,1,0:T(8,128)(2,1)S(1)}, u32[]{:S(2)}, u32[]{:S(2)}) collective-permute-start(bf16[2,1040,128]{2,1,0:T(8,128)(2,1)S(1)} %pad_maximum_fusion.1.refs_0_.refs_1_), channel_id=1, source_target_pairs={{0,8},{9,1},{2,10},{11,3},{8,16},{17,9},{10,18},{19,11},{16,24},{2... | collective-permute-start | bytes 1597448 | tf_op jit(solution)/shard_map/ppermute | solution.py:535
  24.8 1.9 %collective-permute-start.4 = (bf16[2,1040,128]{2,1,0:T(8,128)(2,1)S(1)}, bf16[2,1040,128]{2,1,0:T(8,128)(2,1)S(1)}, u32[]{:S(2)}, u32[]{:S(2)}) collective-permute-start(bf16[2,1040,128]{2,1,0:T(8,128)(2,1)S(1)} %collective-permute-done.3.refs_1_.refs_2_), channel_id=1, source_target_pairs={{0,8},{9,1},{2,10},{11,3},{8,16},{17,9},{10,18},{19,11},{16,24},{2... | collective-permute-start | bytes 1597448 | tf_op jit(solution)/shard_map/ppermute | solution.py:535
  26.7 3.5 %prepare.1 = (bf16[512,1024]{1,0:T(8,128)(2,1)}, f32[2,128,384]{2,1,0:T(8,128)}, f32[256,256]{1,0:T(8,128)}) custom-call(bf16[128,1024]{1,0:T(8,128)(2,1)} %copy-done.18, bf16[256,1024]{1,0:T(8,128)(2,1)} %bitcast.29, bf16[128,1024]{1,0:T(8,128)(2,1)} %copy-done.19, f32[1,1024]{1,0:T(1,128)} %bitcast.37, s32[1,256]{1,0:T(1,128)} %bitcast.41, ...), custom_call_target="tpu_custom_call" | custom-call | flops 1000 | bytes 1000 | tf_op jit(solution)/shard_map/prepare/pallas_call | solution.py:117
  30.2 1.4 %collective-permute-done.6.refs_2_.refs_3_ = bf16[2,1040,128]{2,1,0:T(8,128)(2,1)S(1)} collective-permute-done((bf16[2,1040,128]{2,1,0:T(8,128)(2,1)S(1)}, bf16[2,1040,128]{2,1,0:T(8,128)(2,1)S(1)}, u32[]{:S(2)}, u32[]{:S(2)}) %collective-permute-start.6) | collective-permute-done | bytes 532512 | tf_op jit(solution)/shard_map/ppermute | solution.py:535
  31.6 2.5 %collective-permute-start.7 = (bf16[2,1040,128]{2,1,0:T(8,128)(2,1)S(1)}, bf16[2,1040,128]{2,1,0:T(8,128)(2,1)}, u32[]{:S(2)}, u32[]{:S(2)}) collective-permute-start(bf16[2,1040,128]{2,1,0:T(8,128)(2,1)S(1)} %collective-permute-done.6.refs_2_.refs_3_), channel_id=1, source_target_pairs={{0,8},{9,1},{2,10},{11,3},{8,16},{17,9},{10,18},{19,11},{16,24},{2... | collective-permute-start | bytes 1597448 | tf_op jit(solution)/shard_map/ppermute | solution.py:535
  34.1 3.2 %collective-permute-done.4.refs_4_.refs_5_ = bf16[2,1040,128]{2,1,0:T(8,128)(2,1)S(1)} collective-permute-done((bf16[2,1040,128]{2,1,0:T(8,128)(2,1)S(1)}, bf16[2,1040,128]{2,1,0:T(8,128)(2,1)S(1)}, u32[]{:S(2)}, u32[]{:S(2)}) %collective-permute-start.4) | collective-permute-done | bytes 532512 | tf_op jit(solution)/shard_map/ppermute | solution.py:535
  37.3 2.5 %collective-permute-start.5 = (bf16[2,1040,128]{2,1,0:T(8,128)(2,1)S(1)}, bf16[2,1040,128]{2,1,0:T(8,128)(2,1)}, u32[]{:S(2)}, u32[]{:S(2)}) collective-permute-start(bf16[2,1040,128]{2,1,0:T(8,128)(2,1)S(1)} %collective-permute-done.4.refs_4_.refs_5_), channel_id=1, source_target_pairs={{0,8},{9,1},{2,10},{11,3},{8,16},{17,9},{10,18},{19,11},{16,24},{2... | collective-permute-start | bytes 1597448 | tf_op jit(solution)/shard_map/ppermute | solution.py:535
  39.8 0.6 collective-permute-start.18
  40.5 0.5 collective-permute-start.13
  41.0 2.1 %collective-permute-done.7.refs_0_.refs_7_ = bf16[2,1040,128]{2,1,0:T(8,128)(2,1)} collective-permute-done((bf16[2,1040,128]{2,1,0:T(8,128)(2,1)S(1)}, bf16[2,1040,128]{2,1,0:T(8,128)(2,1)}, u32[]{:S(2)}, u32[]{:S(2)}) %collective-permute-start.7) | collective-permute-done | bytes 532512 | tf_op jit(solution)/shard_map/ppermute | solution.py:535
  43.0 2.6 %collective-permute-start.8 = (bf16[2,1040,128]{2,1,0:T(8,128)(2,1)}, bf16[2,1040,128]{2,1,0:T(8,128)(2,1)}, u32[]{:S(2)}, u32[]{:S(2)}) collective-permute-start(bf16[2,1040,128]{2,1,0:T(8,128)(2,1)} %collective-permute-done.7.refs_0_.refs_7_), channel_id=1, source_target_pairs={{0,8},{9,1},{2,10},{11,3},{8,16},{17,9},{10,18},{19,11},{16,24},{2... | collective-permute-start | bytes 1597448 | tf_op jit(solution)/shard_map/ppermute | solution.py:535
  45.6 3.1 %collective-permute-done.5.refs_2_.refs_9_ = bf16[2,1040,128]{2,1,0:T(8,128)(2,1)} collective-permute-done((bf16[2,1040,128]{2,1,0:T(8,128)(2,1)S(1)}, bf16[2,1040,128]{2,1,0:T(8,128)(2,1)}, u32[]{:S(2)}, u32[]{:S(2)}) %collective-permute-start.5) | collective-permute-done | bytes 532512 | tf_op jit(solution)/shard_map/ppermute | solution.py:535
  48.7 2.6 %collective-permute-start.10 = (bf16[2,1040,128]{2,1,0:T(8,128)(2,1)}, bf16[2,1040,128]{2,1,0:T(8,128)(2,1)}, u32[]{:S(2)}, u32[]{:S(2)}) collective-permute-start(bf16[2,1040,128]{2,1,0:T(8,128)(2,1)} %collective-permute-done.5.refs_2_.refs_9_), channel_id=1, source_target_pairs={{0,8},{9,1},{2,10},{11,3},{8,16},{17,9},{10,18},{19,11},{16,24},{2... | collective-permute-start | bytes 1597448 | tf_op jit(solution)/shard_map/ppermute | solution.py:535
  51.3 0.7 pad_maximum_fusion.2
  52.1 0.5 collective-permute-start.15
  52.7 0.2 copy-done.5
  52.9 0.5 copy-done.6
  53.4 5.3 %project.2.refs_4_ = bf16[24,512,128]{2,1,0:T(8,128)(2,1)} custom-call(bf16[512,1024]{1,0:T(8,128)(2,1)} %get-tuple-element.26.normed, bf16[2,1040,128]{2,1,0:T(8,128)(2,1)} %copy-done, bf16[2,1040,128]{2,1,0:T(8,128)(2,1)} %copy-done.2, bf16[2,1040,128]{2,1,0:T(8,128)(2,1)} %copy-done.3, bf16[2,1040,128]{2,1,0:T(8,128)(2,1)} %copy-done.5, ...), custom_call_target="tpu_custom_call" | custom-call | flops 1000 | bytes 1000 | tf_op jit(solution)/shard_map/project/pallas_call | solution.py:274
  58.7 1.5 %collective-permute-done.10.refs_2_.refs_13_ = bf16[2,1040,128]{2,1,0:T(8,128)(2,1)} collective-permute-done((bf16[2,1040,128]{2,1,0:T(8,128)(2,1)}, bf16[2,1040,128]{2,1,0:T(8,128)(2,1)}, u32[]{:S(2)}, u32[]{:S(2)}) %collective-permute-start.10) | collective-permute-done | bytes 532512 | tf_op jit(solution)/shard_map/ppermute | solution.py:535
  60.2 2.5 %collective-permute-start.14 = (bf16[2,1040,128]{2,1,0:T(8,128)(2,1)}, bf16[2,1040,128]{2,1,0:T(8,128)(2,1)S(1)}, u32[]{:S(2)}, u32[]{:S(2)}) collective-permute-start(bf16[2,1040,128]{2,1,0:T(8,128)(2,1)} %collective-permute-done.8.refs_0_.refs_11_), channel_id=1, source_target_pairs={{0,8},{9,1},{2,10},{11,3},{8,16},{17,9},{10,18},{19,11},{16,24},{2... | collective-permute-start | bytes 1597448 | tf_op jit(solution)/shard_map/ppermute | solution.py:535
  62.7 1.0 select_bitcast_fusion.1
  63.8 1.6 %collective-permute-start.20 = (bf16[2,2,544,128]{3,2,1,0:T(8,128)(2,1)S(1)}, bf16[2,2,544,128]{3,2,1,0:T(8,128)(2,1)S(1)}, u32[]{:S(2)}, u32[]{:S(2)}) collective-permute-start(bf16[2,2,544,128]{3,2,1,0:T(8,128)(2,1)S(1)} %pad_maximum_fusion.refs_0_), channel_id=1, source_target_pairs={{0,8},{9,1},{2,10},{11,3},{8,16},{17,9},{10,18},{19,11},{16,24},{2... | collective-permute-start | bytes 1671176 | tf_op jit(solution)/shard_map/ppermute | solution.py:535
  65.4 4.7 %project.3.refs_6_ = bf16[24,512,128]{2,1,0:T(8,128)(2,1)} custom-call(bf16[512,1024]{1,0:T(8,128)(2,1)} %get-tuple-element.26.normed, bf16[2,1040,128]{2,1,0:T(8,128)(2,1)} %collective-permute-done.7.refs_0_.refs_7_, bf16[2,1040,128]{2,1,0:T(8,128)(2,1)} %collective-permute-done.15.refs_1_.refs_8_, ...), custom_call_target="tpu_custom_call", output_to_operand_aliasing={{}: (5, {})} | custom-call | flops 1000 | bytes 1000 | tf_op jit(solution)/shard_map/project/pallas_call | solution.py:274
  70.1 0.6 collective-permute-start.11
  70.8 1.7 %collective-permute-done.11.refs_3_.refs_14_ = bf16[2,1040,128]{2,1,0:T(8,128)(2,1)S(1)} collective-permute-done((bf16[2,1040,128]{2,1,0:T(8,128)(2,1)}, bf16[2,1040,128]{2,1,0:T(8,128)(2,1)S(1)}, u32[]{:S(2)}, u32[]{:S(2)}) %collective-permute-start.11) | collective-permute-done | bytes 532512 | tf_op jit(solution)/shard_map/ppermute | solution.py:539
  72.5 3.2 %collective-permute-done.20.refs_1_ = bf16[2,2,544,128]{3,2,1,0:T(8,128)(2,1)S(1)} collective-permute-done((bf16[2,2,544,128]{3,2,1,0:T(8,128)(2,1)S(1)}, bf16[2,2,544,128]{3,2,1,0:T(8,128)(2,1)S(1)}, u32[]{:S(2)}, u32[]{:S(2)}) %collective-permute-start.20) | collective-permute-done | bytes 557088 | tf_op jit(solution)/shard_map/ppermute | solution.py:535
  75.7 2.7 %collective-permute-start.22 = (bf16[2,2,544,128]{3,2,1,0:T(8,128)(2,1)S(1)}, bf16[2,2,544,128]{3,2,1,0:T(8,128)(2,1)}, u32[]{:S(2)}, u32[]{:S(2)}) collective-permute-start(bf16[2,2,544,128]{3,2,1,0:T(8,128)(2,1)S(1)} %collective-permute-done.20.refs_1_), channel_id=1, source_target_pairs={{0,8},{9,1},{2,10},{11,3},{8,16},{17,9},{10,18},{19,11},{16,24},{2... | collective-permute-start | bytes 1671176 | tf_op jit(solution)/shard_map/ppermute | solution.py:535
  78.4 9.5 %attend.1.refs_0_ = bf16[256,1024]{1,0:T(8,128)(2,1)} custom-call(bf16[512,1024]{1,0:T(8,128)(2,1)} %get-tuple-element.26.normed, f32[2,128,384]{2,1,0:T(8,128)} %get-tuple-element.27.bias, bf16[2,1040,128]{2,1,0:T(8,128)(2,1)} %collective-permute-done.8.refs_0_.refs_11_, bf16[2,1040,128]{2,1,0:T(8,128)(2,1)} %copy-done.8, ...), custom_call_target="tpu_custom_call" | custom-call | flops 1000 | bytes 1000 | tf_op jit(solution)/shard_map/attend/pallas_call | solution.py:332
  87.9 1.6 %collective-permute-start.24 = (bf16[2,2,544,128]{3,2,1,0:T(8,128)(2,1)}, bf16[2,2,544,128]{3,2,1,0:T(8,128)(2,1)S(1)}, u32[]{:S(2)}, u32[]{:S(2)}) collective-permute-start(bf16[2,2,544,128]{3,2,1,0:T(8,128)(2,1)} %collective-permute-done.22.refs_3_), channel_id=1, source_target_pairs={{0,8},{9,1},{2,10},{11,3},{8,16},{17,9},{10,18},{19,11},{16,24},{2... | collective-permute-start | bytes 1671176 | tf_op jit(solution)/shard_map/ppermute | solution.py:535
  89.5 5.1 %mix.1 = (bf16[256,1024]{1,0:T(8,128)(2,1)}, bf16[128,1024]{1,0:T(8,128)(2,1)}) custom-call(bf16[256,1024]{1,0:T(8,128)(2,1)} %bitcast.30, f32[1,1024]{1,0:T(1,128)} %bitcast.38, bf16[256,1024]{1,0:T(8,128)(2,1)} %attend.1.refs_0_, bf16[2,1040,128]{2,1,0:T(8,128)(2,1)} %copy-done, bf16[2,1040,128]{2,1,0:T(8,128)(2,1)} %copy-done.2, ...), custom_call_target="tpu_custom_call" | custom-call | flops 1000 | bytes 1000 | tf_op jit(solution)/shard_map/mix/pallas_call | solution.py:412
  94.7 0.6 collective-permute-start.23
  95.2 2.5 %collective-permute-done.24.refs_5_ = bf16[2,2,544,128]{3,2,1,0:T(8,128)(2,1)S(1)} collective-permute-done((bf16[2,2,544,128]{3,2,1,0:T(8,128)(2,1)}, bf16[2,2,544,128]{3,2,1,0:T(8,128)(2,1)S(1)}, u32[]{:S(2)}, u32[]{:S(2)}) %collective-permute-start.24) | collective-permute-done | bytes 557088 | tf_op jit(solution)/shard_map/ppermute | solution.py:535
  97.7 0.8 dynamic-slice_bitcast_fusion
  98.5 1.6 %collective-permute-start.26 = (bf16[2,544,128]{2,1,0:T(8,128)(2,1)}, bf16[2,544,128]{2,1,0:T(8,128)(2,1)S(1)}, u32[]{:S(2)}, u32[]{:S(2)}) collective-permute-start(bf16[2,544,128]{2,1,0:T(8,128)(2,1)} %dynamic-slice_bitcast_fusion), channel_id=1, source_target_pairs={{0,8},{9,1},{2,10},{11,3},{8,16},{17,9},{10,18},{19,11},{16,24},{2... | collective-permute-start | bytes 835592 | tf_op jit(solution)/shard_map/ppermute | solution.py:535
  100.1 3.6 %all-to-all-start = ((bf16[8,16,1024]{2,1,0:T(8,128)(2,1)}), bf16[8,16,1024]{2,1,0:T(8,128)(2,1)S(1)}, u32[]{:S(2)}, u32[]{:S(2)}) async-start(bf16[8,16,1024]{2,1,0:T(8,128)(2,1)} %bitcast.33), calls=%async_computation | async-start | bytes 524288 | tf_op jit(solution)/shard_map/all_to_all | solution.py:648
  103.7 1.5 %collective-permute-done.26.refs_7_ = bf16[2,544,128]{2,1,0:T(8,128)(2,1)S(1)} collective-permute-done((bf16[2,544,128]{2,1,0:T(8,128)(2,1)}, bf16[2,544,128]{2,1,0:T(8,128)(2,1)S(1)}, u32[]{:S(2)}, u32[]{:S(2)}) %collective-permute-start.26) | collective-permute-done | bytes 278560 | tf_op jit(solution)/shard_map/ppermute | solution.py:535
  105.3 8.0 %all-to-all-done = bf16[8,16,1024]{2,1,0:T(8,128)(2,1)S(1)} async-done(((bf16[8,16,1024]{2,1,0:T(8,128)(2,1)}), bf16[8,16,1024]{2,1,0:T(8,128)(2,1)S(1)}, u32[]{:S(2)}, u32[]{:S(2)}) %all-to-all-start) | async-done | bytes 262176 | tf_op jit(solution)/shard_map/all_to_all | solution.py:648
  113.3 0.6 copy-done.12
  114.2 0.2 copy-done.16
  114.4 10.9 %decode.1 = bf16[96,256]{1,0:T(8,128)(2,1)} custom-call(bf16[256,1024]{1,0:T(8,128)(2,1)} %bitcast.32, bf16[256,1024]{1,0:T(8,128)(2,1)} %get-tuple-element.30.decoded, bf16[128,1024]{1,0:T(8,128)(2,1)} %bitcast.31, f32[256,256]{1,0:T(8,128)} %get-tuple-element.32.here, f32[256,128]{1,0:T(8,128)} %get-tuple-element.33.there, ...), custom_call_target="tpu_custom_call" | custom-call | flops 1000 | bytes 1000 | tf_op jit(solution)/shard_map/decode/pallas_call | solution.py:490
  (72 shorter events, 0.7 us)
Async XLA Ops:
  0.0 39.8 %copy-start.21 = (bf16[256,12]{0,1:T(8,128)(2,1)S(1)}, bf16[256,12]{0,1:T(8,128)(2,1)}, u32[]{:S(2)}) copy-start(bf16[256,12]{0,1:T(8,128)(2,1)} %param.20) | copy-start | bytes 18436
  0.0 39.8 %copy-start.20 = (bf16[256,256]{1,0:T(8,128)(2,1)S(1)}, bf16[256,256]{1,0:T(8,128)(2,1)}, u32[]{:S(2)}) copy-start(bf16[256,256]{1,0:T(8,128)(2,1)} %param.19) | copy-start | bytes 393220
  3.0 9.5 %collective-permute-start.2 = (bf16[1040,128]{1,0:T(8,128)(2,1)}, bf16[1040,128]{1,0:T(8,128)(2,1)S(1)}, u32[]{:S(2)}, u32[]{:S(2)}) collective-permute-start(bf16[1040,128]{1,0:T(8,128)(2,1)} %get-tuple-element.23), channel_id=1, source_target_pairs={{0,2},{1,3},{2,0},{3,1},{4,6},{5,7},{6,4},{7,5},{8,10},{9,11},{10,... | collective-permute-start | bytes 798728 | tf_op jit(solution)/shard_map/ppermute | solution.py:517
  7.0 14.3 %collective-permute-start = (bf16[128,1024]{1,0:T(8,128)(2,1)S(1)}, bf16[128,1024]{1,0:T(8,128)(2,1)S(1)}, u32[]{:S(2)}, u32[]{:S(2)}) collective-permute-start(bf16[128,1024]{1,0:T(8,128)(2,1)S(1)} %get-tuple-element.44), channel_id=1, source_target_pairs={{0,4},{4,8},{8,12},{12,16},{16,20},{20,24},{24,28},{1,5},{5,9},{9,... | collective-permute-start | bytes 786440 | tf_op jit(solution)/shard_map/ppermute | solution.py:592
  10.5 10.9 %collective-permute-start.1 = (bf16[128,1024]{1,0:T(8,128)(2,1)S(1)}, bf16[128,1024]{1,0:T(8,128)(2,1)S(1)}, u32[]{:S(2)}, u32[]{:S(2)}) collective-permute-start(bf16[128,1024]{1,0:T(8,128)(2,1)S(1)} %get-tuple-element.43), channel_id=1, source_target_pairs={{4,0},{8,4},{12,8},{16,12},{20,16},{24,20},{28,24},{5,1},{9,5},{13... | collective-permute-start | bytes 786440 | tf_op jit(solution)/shard_map/ppermute | solution.py:593
  13.6 39.1 %copy-start = (bf16[2,1040,128]{2,1,0:T(8,128)(2,1)}, bf16[2,1040,128]{2,1,0:T(8,128)(2,1)S(1)}, u32[]{:S(2)}) copy-start(bf16[2,1040,128]{2,1,0:T(8,128)(2,1)S(1)} %pad_maximum_fusion.1.refs_0_.refs_1_) | copy-start | bytes 1597444
  21.4 5.4 %copy-start.18 = (bf16[128,1024]{1,0:T(8,128)(2,1)}, bf16[128,1024]{1,0:T(8,128)(2,1)S(1)}, u32[]{:S(2)}) copy-start(bf16[128,1024]{1,0:T(8,128)(2,1)S(1)} %collective-permute-done.left) | copy-start | bytes 786436
  21.4 5.4 %copy-start.19 = (bf16[128,1024]{1,0:T(8,128)(2,1)}, bf16[128,1024]{1,0:T(8,128)(2,1)S(1)}, u32[]{:S(2)}) copy-start(bf16[128,1024]{1,0:T(8,128)(2,1)S(1)} %collective-permute-done.1.right) | copy-start | bytes 786436
  21.4 3.4 %collective-permute-start.3 = (bf16[2,1040,128]{2,1,0:T(8,128)(2,1)S(1)}, bf16[2,1040,128]{2,1,0:T(8,128)(2,1)S(1)}, u32[]{:S(2)}, u32[]{:S(2)}) collective-permute-start(bf16[2,1040,128]{2,1,0:T(8,128)(2,1)S(1)} %pad_maximum_fusion.1.refs_0_.refs_1_), channel_id=1, source_target_pairs={{0,1},{1,0},{2,3},{3,2},{4,5},{5,4},{6,7},{7,6},{8,9},{9,8},{10,11... | collective-permute-start | bytes 1597448 | tf_op jit(solution)/shard_map/ppermute | solution.py:539
  21.4 10.2 %collective-permute-start.6 = (bf16[2,1040,128]{2,1,0:T(8,128)(2,1)S(1)}, bf16[2,1040,128]{2,1,0:T(8,128)(2,1)S(1)}, u32[]{:S(2)}, u32[]{:S(2)}) collective-permute-start(bf16[2,1040,128]{2,1,0:T(8,128)(2,1)S(1)} %pad_maximum_fusion.1.refs_0_.refs_1_), channel_id=1, source_target_pairs={{0,8},{9,1},{2,10},{11,3},{8,16},{17,9},{10,18},{19,11},{16,24},{2... | collective-permute-start | bytes 1597448 | tf_op jit(solution)/shard_map/ppermute | solution.py:535
  24.8 27.9 %copy-start.2 = (bf16[2,1040,128]{2,1,0:T(8,128)(2,1)}, bf16[2,1040,128]{2,1,0:T(8,128)(2,1)S(1)}, u32[]{:S(2)}) copy-start(bf16[2,1040,128]{2,1,0:T(8,128)(2,1)S(1)} %collective-permute-done.3.refs_1_.refs_2_) | copy-start | bytes 1597444
  24.8 12.5 %collective-permute-start.4 = (bf16[2,1040,128]{2,1,0:T(8,128)(2,1)S(1)}, bf16[2,1040,128]{2,1,0:T(8,128)(2,1)S(1)}, u32[]{:S(2)}, u32[]{:S(2)}) collective-permute-start(bf16[2,1040,128]{2,1,0:T(8,128)(2,1)S(1)} %collective-permute-done.3.refs_1_.refs_2_), channel_id=1, source_target_pairs={{0,8},{9,1},{2,10},{11,3},{8,16},{17,9},{10,18},{19,11},{16,24},{2... | collective-permute-start | bytes 1597448 | tf_op jit(solution)/shard_map/ppermute | solution.py:535
  31.6 21.1 %copy-start.3 = (bf16[2,1040,128]{2,1,0:T(8,128)(2,1)}, bf16[2,1040,128]{2,1,0:T(8,128)(2,1)S(1)}, u32[]{:S(2)}) copy-start(bf16[2,1040,128]{2,1,0:T(8,128)(2,1)S(1)} %collective-permute-done.6.refs_2_.refs_3_) | copy-start | bytes 1597444
  31.6 11.4 %collective-permute-start.7 = (bf16[2,1040,128]{2,1,0:T(8,128)(2,1)S(1)}, bf16[2,1040,128]{2,1,0:T(8,128)(2,1)}, u32[]{:S(2)}, u32[]{:S(2)}) collective-permute-start(bf16[2,1040,128]{2,1,0:T(8,128)(2,1)S(1)} %collective-permute-done.6.refs_2_.refs_3_), channel_id=1, source_target_pairs={{0,8},{9,1},{2,10},{11,3},{8,16},{17,9},{10,18},{19,11},{16,24},{2... | collective-permute-start | bytes 1597448 | tf_op jit(solution)/shard_map/ppermute | solution.py:535
  37.3 15.4 %copy-start.4 = (bf16[2,1040,128]{2,1,0:T(8,128)(2,1)}, bf16[2,1040,128]{2,1,0:T(8,128)(2,1)S(1)}, u32[]{:S(2)}) copy-start(bf16[2,1040,128]{2,1,0:T(8,128)(2,1)S(1)} %collective-permute-done.4.refs_4_.refs_5_) | copy-start | bytes 1597444
  37.3 11.4 %collective-permute-start.5 = (bf16[2,1040,128]{2,1,0:T(8,128)(2,1)S(1)}, bf16[2,1040,128]{2,1,0:T(8,128)(2,1)}, u32[]{:S(2)}, u32[]{:S(2)}) collective-permute-start(bf16[2,1040,128]{2,1,0:T(8,128)(2,1)S(1)} %collective-permute-done.4.refs_4_.refs_5_), channel_id=1, source_target_pairs={{0,8},{9,1},{2,10},{11,3},{8,16},{17,9},{10,18},{19,11},{16,24},{2... | collective-permute-start | bytes 1597448 | tf_op jit(solution)/shard_map/ppermute | solution.py:535
  39.8 11.5 %collective-permute-start.18 = (bf16[544,128]{1,0:T(8,128)(2,1)S(1)}, bf16[544,128]{1,0:T(8,128)(2,1)S(1)}, u32[]{:S(2)}, u32[]{:S(2)}) collective-permute-start(bf16[544,128]{1,0:T(8,128)(2,1)S(1)} %pad_maximum_fusion.3), channel_id=1, source_target_pairs={{0,2},{1,3},{2,0},{3,1},{4,6},{5,7},{6,4},{7,5},{8,10},{9,11},{10,... | collective-permute-start | bytes 417800 | tf_op jit(solution)/shard_map/ppermute | solution.py:517
  40.4 11.6 %collective-permute-start.12 = (bf16[2,1040,128]{2,1,0:T(8,128)(2,1)S(1)}, bf16[2,1040,128]{2,1,0:T(8,128)(2,1)S(1)}, u32[]{:S(2)}, u32[]{:S(2)}) collective-permute-start(bf16[2,1040,128]{2,1,0:T(8,128)(2,1)S(1)} %collective-permute-done.6.refs_2_.refs_3_), channel_id=1, source_target_pairs={{0,1},{1,0},{2,3},{3,2},{4,5},{5,4},{6,7},{7,6},{8,9},{9,8},{10,11... | collective-permute-start | bytes 1597448 | tf_op jit(solution)/shard_map/ppermute | solution.py:539
  40.5 12.2 %collective-permute-start.13 = (bf16[2,1040,128]{2,1,0:T(8,128)(2,1)S(1)}, bf16[2,1040,128]{2,1,0:T(8,128)(2,1)S(1)}, u32[]{:S(2)}, u32[]{:S(2)}) collective-permute-start(bf16[2,1040,128]{2,1,0:T(8,128)(2,1)S(1)} %collective-permute-done.4.refs_4_.refs_5_), channel_id=1, source_target_pairs={{0,1},{1,0},{2,3},{3,2},{4,5},{5,4},{6,7},{7,6},{8,9},{9,8},{10,11... | collective-permute-start | bytes 1597448 | tf_op jit(solution)/shard_map/ppermute | solution.py:539
  43.0 15.7 %collective-permute-start.8 = (bf16[2,1040,128]{2,1,0:T(8,128)(2,1)}, bf16[2,1040,128]{2,1,0:T(8,128)(2,1)}, u32[]{:S(2)}, u32[]{:S(2)}) collective-permute-start(bf16[2,1040,128]{2,1,0:T(8,128)(2,1)} %collective-permute-done.7.refs_0_.refs_7_), channel_id=1, source_target_pairs={{0,8},{9,1},{2,10},{11,3},{8,16},{17,9},{10,18},{19,11},{16,24},{2... | collective-permute-start | bytes 1597448 | tf_op jit(solution)/shard_map/ppermute | solution.py:535
  48.7 11.5 %collective-permute-start.10 = (bf16[2,1040,128]{2,1,0:T(8,128)(2,1)}, bf16[2,1040,128]{2,1,0:T(8,128)(2,1)}, u32[]{:S(2)}, u32[]{:S(2)}) collective-permute-start(bf16[2,1040,128]{2,1,0:T(8,128)(2,1)} %collective-permute-done.5.refs_2_.refs_9_), channel_id=1, source_target_pairs={{0,8},{9,1},{2,10},{11,3},{8,16},{17,9},{10,18},{19,11},{16,24},{2... | collective-permute-start | bytes 1597448 | tf_op jit(solution)/shard_map/ppermute | solution.py:535
  52.1 10.6 %collective-permute-start.19 = (bf16[2,544,128]{2,1,0:T(8,128)(2,1)}, bf16[2,544,128]{2,1,0:T(8,128)(2,1)}, u32[]{:S(2)}, u32[]{:S(2)}) collective-permute-start(bf16[2,544,128]{2,1,0:T(8,128)(2,1)} %pad_maximum_fusion.2), channel_id=1, source_target_pairs={{0,1},{1,0},{2,3},{3,2},{4,5},{5,4},{6,7},{7,6},{8,9},{9,8},{10,11... | collective-permute-start | bytes 835592 | tf_op jit(solution)/shard_map/ppermute | solution.py:539
  52.1 11.7 %collective-permute-start.15 = (bf16[2,1040,128]{2,1,0:T(8,128)(2,1)}, bf16[2,1040,128]{2,1,0:T(8,128)(2,1)}, u32[]{:S(2)}, u32[]{:S(2)}) collective-permute-start(bf16[2,1040,128]{2,1,0:T(8,128)(2,1)} %collective-permute-done.7.refs_0_.refs_7_), channel_id=1, source_target_pairs={{0,1},{1,0},{2,3},{3,2},{4,5},{5,4},{6,7},{7,6},{8,9},{9,8},{10,11... | collective-permute-start | bytes 1597448 | tf_op jit(solution)/shard_map/ppermute | solution.py:539
  52.6 11.2 %collective-permute-start.16 = (bf16[2,1040,128]{2,1,0:T(8,128)(2,1)}, bf16[2,1040,128]{2,1,0:T(8,128)(2,1)}, u32[]{:S(2)}, u32[]{:S(2)}) collective-permute-start(bf16[2,1040,128]{2,1,0:T(8,128)(2,1)} %collective-permute-done.5.refs_2_.refs_9_), channel_id=1, source_target_pairs={{0,1},{1,0},{2,3},{3,2},{4,5},{5,4},{6,7},{7,6},{8,9},{9,8},{10,11... | collective-permute-start | bytes 1597448 | tf_op jit(solution)/shard_map/ppermute | solution.py:539
  60.2 10.5 %collective-permute-start.14 = (bf16[2,1040,128]{2,1,0:T(8,128)(2,1)}, bf16[2,1040,128]{2,1,0:T(8,128)(2,1)S(1)}, u32[]{:S(2)}, u32[]{:S(2)}) collective-permute-start(bf16[2,1040,128]{2,1,0:T(8,128)(2,1)} %collective-permute-done.8.refs_0_.refs_11_), channel_id=1, source_target_pairs={{0,8},{9,1},{2,10},{11,3},{8,16},{17,9},{10,18},{19,11},{16,24},{2... | collective-permute-start | bytes 1597448 | tf_op jit(solution)/shard_map/ppermute | solution.py:535
  63.8 6.3 %copy-start.1 = (bf16[2,2,544,128]{3,2,1,0:T(8,128)(2,1)}, bf16[2,2,544,128]{3,2,1,0:T(8,128)(2,1)S(1)}, u32[]{:S(2)}) copy-start(bf16[2,2,544,128]{3,2,1,0:T(8,128)(2,1)S(1)} %pad_maximum_fusion.refs_0_) | copy-start | bytes 1671172
  63.8 11.9 %collective-permute-start.20 = (bf16[2,2,544,128]{3,2,1,0:T(8,128)(2,1)S(1)}, bf16[2,2,544,128]{3,2,1,0:T(8,128)(2,1)S(1)}, u32[]{:S(2)}, u32[]{:S(2)}) collective-permute-start(bf16[2,2,544,128]{3,2,1,0:T(8,128)(2,1)S(1)} %pad_maximum_fusion.refs_0_), channel_id=1, source_target_pairs={{0,8},{9,1},{2,10},{11,3},{8,16},{17,9},{10,18},{19,11},{16,24},{2... | collective-permute-start | bytes 1671176 | tf_op jit(solution)/shard_map/ppermute | solution.py:535
  65.4 5.4 %collective-permute-start.9 = (bf16[2,1040,128]{2,1,0:T(8,128)(2,1)}, bf16[2,1040,128]{2,1,0:T(8,128)(2,1)S(1)}, u32[]{:S(2)}, u32[]{:S(2)}) collective-permute-start(bf16[2,1040,128]{2,1,0:T(8,128)(2,1)} %collective-permute-done.8.refs_0_.refs_11_), channel_id=1, source_target_pairs={{0,1},{1,0},{2,3},{3,2},{4,5},{5,4},{6,7},{7,6},{8,9},{9,8},{10,11... | collective-permute-start | bytes 1597448 | tf_op jit(solution)/shard_map/ppermute | solution.py:539
  70.1 2.3 %collective-permute-start.11 = (bf16[2,1040,128]{2,1,0:T(8,128)(2,1)}, bf16[2,1040,128]{2,1,0:T(8,128)(2,1)S(1)}, u32[]{:S(2)}, u32[]{:S(2)}) collective-permute-start(bf16[2,1040,128]{2,1,0:T(8,128)(2,1)} %collective-permute-done.10.refs_2_.refs_13_), channel_id=1, source_target_pairs={{0,1},{1,0},{2,3},{3,2},{4,5},{5,4},{6,7},{7,6},{8,9},{9,8},{10,11... | collective-permute-start | bytes 1597448 | tf_op jit(solution)/shard_map/ppermute | solution.py:539
  70.7 7.7 %copy-start.7 = (bf16[2,1040,128]{2,1,0:T(8,128)(2,1)}, bf16[2,1040,128]{2,1,0:T(8,128)(2,1)S(1)}, u32[]{:S(2)}) copy-start(bf16[2,1040,128]{2,1,0:T(8,128)(2,1)S(1)} %collective-permute-done.14.refs_4_.refs_15_) | copy-start | bytes 1597444
  70.7 5.0 %collective-permute-start.17 = (bf16[2,1040,128]{2,1,0:T(8,128)(2,1)S(1)}, bf16[2,1040,128]{2,1,0:T(8,128)(2,1)S(1)}, u32[]{:S(2)}, u32[]{:S(2)}) collective-permute-start(bf16[2,1040,128]{2,1,0:T(8,128)(2,1)S(1)} %collective-permute-done.14.refs_4_.refs_15_), channel_id=1, source_target_pairs={{0,1},{1,0},{2,3},{3,2},{4,5},{5,4},{6,7},{7,6},{8,9},{9,8},{10,11... | collective-permute-start | bytes 1597448 | tf_op jit(solution)/shard_map/ppermute | solution.py:539
  70.8 7.6 %copy-start.8 = (bf16[2,1040,128]{2,1,0:T(8,128)(2,1)}, bf16[2,1040,128]{2,1,0:T(8,128)(2,1)S(1)}, u32[]{:S(2)}) copy-start(bf16[2,1040,128]{2,1,0:T(8,128)(2,1)S(1)} %collective-permute-done.9.refs_1_.refs_12_) | copy-start | bytes 1597444
  72.5 5.9 %copy-start.9 = (bf16[2,1040,128]{2,1,0:T(8,128)(2,1)}, bf16[2,1040,128]{2,1,0:T(8,128)(2,1)S(1)}, u32[]{:S(2)}) copy-start(bf16[2,1040,128]{2,1,0:T(8,128)(2,1)S(1)} %collective-permute-done.11.refs_3_.refs_14_) | copy-start | bytes 1597444
  75.7 24.4 %copy-start.13 = (bf16[2,2,544,128]{3,2,1,0:T(8,128)(2,1)}, bf16[2,2,544,128]{3,2,1,0:T(8,128)(2,1)S(1)}, u32[]{:S(2)}) copy-start(bf16[2,2,544,128]{3,2,1,0:T(8,128)(2,1)S(1)} %collective-permute-done.20.refs_1_) | copy-start | bytes 1671172
  75.7 2.7 %copy-start.10 = (bf16[2,1040,128]{2,1,0:T(8,128)(2,1)}, bf16[2,1040,128]{2,1,0:T(8,128)(2,1)S(1)}, u32[]{:S(2)}) copy-start(bf16[2,1040,128]{2,1,0:T(8,128)(2,1)S(1)} %collective-permute-done.17.refs_5_.refs_16_) | copy-start | bytes 1597444
  75.7 12.2 %collective-permute-start.22 = (bf16[2,2,544,128]{3,2,1,0:T(8,128)(2,1)S(1)}, bf16[2,2,544,128]{3,2,1,0:T(8,128)(2,1)}, u32[]{:S(2)}, u32[]{:S(2)}) collective-permute-start(bf16[2,2,544,128]{3,2,1,0:T(8,128)(2,1)S(1)} %collective-permute-done.20.refs_1_), channel_id=1, source_target_pairs={{0,8},{9,1},{2,10},{11,3},{8,16},{17,9},{10,18},{19,11},{16,24},{2... | collective-permute-start | bytes 1671176 | tf_op jit(solution)/shard_map/ppermute | solution.py:535
  87.9 9.8 %collective-permute-start.24 = (bf16[2,2,544,128]{3,2,1,0:T(8,128)(2,1)}, bf16[2,2,544,128]{3,2,1,0:T(8,128)(2,1)S(1)}, u32[]{:S(2)}, u32[]{:S(2)}) collective-permute-start(bf16[2,2,544,128]{3,2,1,0:T(8,128)(2,1)} %collective-permute-done.22.refs_3_), channel_id=1, source_target_pairs={{0,8},{9,1},{2,10},{11,3},{8,16},{17,9},{10,18},{19,11},{16,24},{2... | collective-permute-start | bytes 1671176 | tf_op jit(solution)/shard_map/ppermute | solution.py:535
  89.5 15.7 %collective-permute-start.21 = (bf16[2,2,544,128]{3,2,1,0:T(8,128)(2,1)S(1)}, bf16[2,2,544,128]{3,2,1,0:T(8,128)(2,1)S(1)}, u32[]{:S(2)}, u32[]{:S(2)}) collective-permute-start(bf16[2,2,544,128]{3,2,1,0:T(8,128)(2,1)S(1)} %collective-permute-done.20.refs_1_), channel_id=1, source_target_pairs={{0,1},{1,0},{2,3},{3,2},{4,5},{5,4},{6,7},{7,6},{8,9},{9,8},{10,11... | collective-permute-start | bytes 1671176 | tf_op jit(solution)/shard_map/ppermute | solution.py:539
  94.7 18.6 %collective-permute-start.23 = (bf16[2,2,544,128]{3,2,1,0:T(8,128)(2,1)}, bf16[2,2,544,128]{3,2,1,0:T(8,128)(2,1)S(1)}, u32[]{:S(2)}, u32[]{:S(2)}) collective-permute-start(bf16[2,2,544,128]{3,2,1,0:T(8,128)(2,1)} %collective-permute-done.22.refs_3_), channel_id=1, source_target_pairs={{0,1},{1,0},{2,3},{3,2},{4,5},{5,4},{6,7},{7,6},{8,9},{9,8},{10,11... | collective-permute-start | bytes 1671176 | tf_op jit(solution)/shard_map/ppermute | solution.py:539
  97.7 15.6 %copy-start.11 = (bf16[2,2,544,128]{3,2,1,0:T(8,128)(2,1)}, bf16[2,2,544,128]{3,2,1,0:T(8,128)(2,1)S(1)}, u32[]{:S(2)}) copy-start(bf16[2,2,544,128]{3,2,1,0:T(8,128)(2,1)S(1)} %collective-permute-done.24.refs_5_) | copy-start | bytes 1671172
  98.5 6.8 %collective-permute-start.26 = (bf16[2,544,128]{2,1,0:T(8,128)(2,1)}, bf16[2,544,128]{2,1,0:T(8,128)(2,1)S(1)}, u32[]{:S(2)}, u32[]{:S(2)}) collective-permute-start(bf16[2,544,128]{2,1,0:T(8,128)(2,1)} %dynamic-slice_bitcast_fusion), channel_id=1, source_target_pairs={{0,8},{9,1},{2,10},{11,3},{8,16},{17,9},{10,18},{19,11},{16,24},{2... | collective-permute-start | bytes 835592 | tf_op jit(solution)/shard_map/ppermute | solution.py:535
  100.1 13.2 %collective-permute-start.25 = (bf16[2,2,544,128]{3,2,1,0:T(8,128)(2,1)S(1)}, bf16[2,2,544,128]{3,2,1,0:T(8,128)(2,1)S(1)}, u32[]{:S(2)}, u32[]{:S(2)}) collective-permute-start(bf16[2,2,544,128]{3,2,1,0:T(8,128)(2,1)S(1)} %collective-permute-done.24.refs_5_), channel_id=1, source_target_pairs={{0,1},{1,0},{2,3},{3,2},{4,5},{5,4},{6,7},{7,6},{8,9},{9,8},{10,11... | collective-permute-start | bytes 1671176 | tf_op jit(solution)/shard_map/ppermute | solution.py:539
  100.1 13.2 %all-to-all-start = ((bf16[8,16,1024]{2,1,0:T(8,128)(2,1)}), bf16[8,16,1024]{2,1,0:T(8,128)(2,1)S(1)}, u32[]{:S(2)}, u32[]{:S(2)}) async-start(bf16[8,16,1024]{2,1,0:T(8,128)(2,1)} %bitcast.33), calls=%async_computation | async-start | bytes 524288 | tf_op jit(solution)/shard_map/all_to_all | solution.py:648
  105.2 8.1 %copy-start.17 = (bf16[2,544,128]{2,1,0:T(8,128)(2,1)}, bf16[2,544,128]{2,1,0:T(8,128)(2,1)S(1)}, u32[]{:S(2)}) copy-start(bf16[2,544,128]{2,1,0:T(8,128)(2,1)S(1)} %collective-permute-done.26.refs_7_) | copy-start | bytes 835588
  105.2 8.1 %collective-permute-start.27 = (bf16[2,544,128]{2,1,0:T(8,128)(2,1)S(1)}, bf16[2,544,128]{2,1,0:T(8,128)(2,1)}, u32[]{:S(2)}, u32[]{:S(2)}) collective-permute-start(bf16[2,544,128]{2,1,0:T(8,128)(2,1)S(1)} %collective-permute-done.26.refs_7_), channel_id=1, source_target_pairs={{0,1},{1,0},{2,3},{3,2},{4,5},{5,4},{6,7},{7,6},{8,9},{9,8},{10,11... | collective-permute-start | bytes 835592 | tf_op jit(solution)/shard_map/ppermute | solution.py:539
  105.2 8.1 %copy-start.14 = (bf16[2,2,544,128]{3,2,1,0:T(8,128)(2,1)}, bf16[2,2,544,128]{3,2,1,0:T(8,128)(2,1)S(1)}, u32[]{:S(2)}) copy-start(bf16[2,2,544,128]{3,2,1,0:T(8,128)(2,1)S(1)} %collective-permute-done.21.refs_2_) | copy-start | bytes 1671172
  113.3 0.9 copy-start.15
  113.3 1.1 copy-start.16
  (3 other events, 2.3 us)

commit v4 on v2

--- a/solution.py
+++ b/solution.py
@@ -20,7 +20,7 @@
 BANDS = 4
 CHUNKS = (0, 2, 1, 3)
 RING = (0, 2, 4, 6, 7, 5, 3, 1)
-VMEM = 60 * 1024 * 1024
+VMEM = 62 * 1024 * 1024
 SMALL = pl.CostEstimate(flops=1000, bytes_accessed=1000, transcendentals=0)
 F32 = jnp.float32
 BF16 = jnp.bfloat16

time: 121 us -> 122 us (level)
  transfers between devices with their start and end apart: 29 -> 29, of which waited for: 11 -> 11; matrix products, arithmetic and copies ran while one was open for 4% -> 3% of each run, Pallas kernels for 23% -> 23%
where the time goes in v4:
time: 122 us; the launch traced here: 121 us
  Pallas kernels  41.9 us (34%)
  starting transfers between devices  40.1 us (33%)
  waiting for transfers between devices  32.9 us (27%)
  local copies, waits for them, and re-layouts  2.87 us (2%)
  other arithmetic  2.86 us (2%)
    ppermute x11, starting transfers between devices, carry(): return lax.ppermute(block, ('seq', 'band'), pairs)  26.1 us
    ppermute x11, waiting for transfers between devices, carry(): return lax.ppermute(block, ('seq', 'band'), pairs)  14.6 us
    pallas_call x1, Pallas kernels, decode(): pl.pallas_call(functools.partial(decode_kernel, layout, outputs // GROUPS...  10.9 us
    pallas_call x2, Pallas kernels, project(): pl.pallas_call(functools.partial(project_kernel, layout, riding), out_sha...  9.97 us
    pallas_call x1, Pallas kernels, attend(): pl.pallas_call(functools.partial(attend_kernel, layout, ready, riding), o...  9.45 us
    ppermute x1, waiting for transfers between devices, local(): left = lax.ppermute(states[tok - HALF:], 'seq', up)  7.72 us
    all_to_all x1, waiting for transfers between devices, local(): lax.all_to_all(found.reshape(shards, SLOTS, width), 'seq', split_axis=0,...  6.6 us
    pallas_call x1, Pallas kernels, mix(): pl.pallas_call(functools.partial(mix_kernel, layout, ids is None), out_sh...  5.12 us
  transfers between devices with their start and end apart: 29, of which 11 were waited for; matrix products, arithmetic and copies ran while one was open for 3% of the time, Pallas kernels for 23%

profile of v4, /device:TPU:0, one launch (start us, length us, event | category | flops | bytes accessed | tf_op | source)
XLA Modules:
  0.0 121.1 jit_solution(1117056620948078832)
XLA Ops:
  0.0 3.0 %tables.1 = (f32[256,128]{1,0:T(8,128)}, bf16[1,128]{1,0:T(2,128)(2,1)}, bf16[1040,128]{1,0:T(8,128)(2,1)}) custom-call(s32[8,256]{1,0:T(8,128)} %bitcast.34, s32[1,256]{1,0:T(1,128)} %bitcast.39, s32[1,128]{1,0:T(1,128)} %constant.32.clone.low, f32[1,128]{1,0:T(1,128)} %constant.33.clone.rank, bf16[256,256]{1,0:T(8,128)(2,1)} %constant.34.clone.tri, ...), custom_call_target="tpu_custom_call" | custom-call | flops 1000 | bytes 1000 | tf_op jit(solution)/shard_map/tables/pallas_call | solution.py:181
  3.0 2.9 %collective-permute-start.2 = (bf16[1040,128]{1,0:T(8,128)(2,1)}, bf16[1040,128]{1,0:T(8,128)(2,1)S(1)}, u32[]{:S(2)}, u32[]{:S(2)}) collective-permute-start(bf16[1040,128]{1,0:T(8,128)(2,1)} %get-tuple-element.24), channel_id=1, source_target_pairs={{0,2},{1,3},{2,0},{3,1},{4,6},{5,7},{6,4},{7,5},{8,10},{9,11},{10,... | collective-permute-start | bytes 798728 | tf_op jit(solution)/shard_map/ppermute | solution.py:517
  6.0 1.1 slice_bitcast_fusion
  7.0 3.4 %collective-permute-start = (bf16[128,1024]{1,0:T(8,128)(2,1)S(1)}, bf16[128,1024]{1,0:T(8,128)(2,1)S(1)}, u32[]{:S(2)}, u32[]{:S(2)}) collective-permute-start(bf16[128,1024]{1,0:T(8,128)(2,1)S(1)} %get-tuple-element.46), channel_id=1, source_target_pairs={{0,4},{4,8},{8,12},{12,16},{16,20},{20,24},{24,28},{1,5},{5,9},{9,... | collective-permute-start | bytes 786440 | tf_op jit(solution)/shard_map/ppermute | solution.py:593
  10.5 1.3 %collective-permute-start.1 = (bf16[128,1024]{1,0:T(8,128)(2,1)S(1)}, bf16[128,1024]{1,0:T(8,128)(2,1)S(1)}, u32[]{:S(2)}, u32[]{:S(2)}) collective-permute-start(bf16[128,1024]{1,0:T(8,128)(2,1)S(1)} %get-tuple-element.45), channel_id=1, source_target_pairs={{4,0},{8,4},{12,8},{16,12},{20,16},{24,20},{28,24},{5,1},{9,5},{13... | collective-permute-start | bytes 786440 | tf_op jit(solution)/shard_map/ppermute | solution.py:594
  11.8 0.8 collective-permute-done.2
  12.6 1.0 select_bitcast_fusion.3
  13.6 0.1 pad_maximum_fusion.1.refs_0_.refs_1_
  13.6 7.7 %collective-permute-done.left = bf16[128,1024]{1,0:T(8,128)(2,1)S(1)} collective-permute-done((bf16[128,1024]{1,0:T(8,128)(2,1)S(1)}, bf16[128,1024]{1,0:T(8,128)(2,1)S(1)}, u32[]{:S(2)}, u32[]{:S(2)}) %collective-permute-start) | collective-permute-done | bytes 262176 | tf_op jit(solution)/shard_map/ppermute | solution.py:593
  21.4 3.4 %collective-permute-start.6 = (bf16[2,1040,128]{2,1,0:T(8,128)(2,1)S(1)}, bf16[2,1040,128]{2,1,0:T(8,128)(2,1)S(1)}, u32[]{:S(2)}, u32[]{:S(2)}) collective-permute-start(bf16[2,1040,128]{2,1,0:T(8,128)(2,1)S(1)} %pad_maximum_fusion.1.refs_0_.refs_1_), channel_id=1, source_target_pairs={{0,8},{9,1},{2,10},{11,3},{8,16},{17,9},{10,18},{19,11},{16,24},{2... | collective-permute-start | bytes 1597448 | tf_op jit(solution)/shard_map/ppermute | solution.py:535
  24.8 1.9 %collective-permute-start.4 = (bf16[2,1040,128]{2,1,0:T(8,128)(2,1)S(1)}, bf16[2,1040,128]{2,1,0:T(8,128)(2,1)}, u32[]{:S(2)}, u32[]{:S(2)}) collective-permute-start(bf16[2,1040,128]{2,1,0:T(8,128)(2,1)S(1)} %collective-permute-done.3.refs_1_.refs_2_), channel_id=1, source_target_pairs={{0,8},{9,1},{2,10},{11,3},{8,16},{17,9},{10,18},{19,11},{16,24},{2... | collective-permute-start | bytes 1597448 | tf_op jit(solution)/shard_map/ppermute | solution.py:535
  26.7 3.5 %prepare.1 = (bf16[512,1024]{1,0:T(8,128)(2,1)}, f32[2,128,384]{2,1,0:T(8,128)}, f32[256,256]{1,0:T(8,128)}) custom-call(bf16[128,1024]{1,0:T(8,128)(2,1)} %copy-done.16, bf16[256,1024]{1,0:T(8,128)(2,1)} %bitcast.29, bf16[128,1024]{1,0:T(8,128)(2,1)} %copy-done.17, f32[1,1024]{1,0:T(1,128)} %bitcast.37, s32[1,256]{1,0:T(1,128)} %bitcast.41, ...), custom_call_target="tpu_custom_call" | custom-call | flops 1000 | bytes 1000 | tf_op jit(solution)/shard_map/prepare/pallas_call | solution.py:117
  30.2 1.4 %collective-permute-done.6.refs_2_.refs_3_ = bf16[2,1040,128]{2,1,0:T(8,128)(2,1)S(1)} collective-permute-done((bf16[2,1040,128]{2,1,0:T(8,128)(2,1)S(1)}, bf16[2,1040,128]{2,1,0:T(8,128)(2,1)S(1)}, u32[]{:S(2)}, u32[]{:S(2)}) %collective-permute-start.6) | collective-permute-done | bytes 532512 | tf_op jit(solution)/shard_map/ppermute | solution.py:535
  31.6 2.5 %collective-permute-start.7 = (bf16[2,1040,128]{2,1,0:T(8,128)(2,1)S(1)}, bf16[2,1040,128]{2,1,0:T(8,128)(2,1)}, u32[]{:S(2)}, u32[]{:S(2)}) collective-permute-start(bf16[2,1040,128]{2,1,0:T(8,128)(2,1)S(1)} %collective-permute-done.6.refs_2_.refs_3_), channel_id=1, source_target_pairs={{0,8},{9,1},{2,10},{11,3},{8,16},{17,9},{10,18},{19,11},{16,24},{2... | collective-permute-start | bytes 1597448 | tf_op jit(solution)/shard_map/ppermute | solution.py:535
  34.1 3.2 %collective-permute-done.4.refs_4_.refs_5_ = bf16[2,1040,128]{2,1,0:T(8,128)(2,1)} collective-permute-done((bf16[2,1040,128]{2,1,0:T(8,128)(2,1)S(1)}, bf16[2,1040,128]{2,1,0:T(8,128)(2,1)}, u32[]{:S(2)}, u32[]{:S(2)}) %collective-permute-start.4) | collective-permute-done | bytes 532512 | tf_op jit(solution)/shard_map/ppermute | solution.py:535
  37.3 2.6 %collective-permute-start.5 = (bf16[2,1040,128]{2,1,0:T(8,128)(2,1)}, bf16[2,1040,128]{2,1,0:T(8,128)(2,1)}, u32[]{:S(2)}, u32[]{:S(2)}) collective-permute-start(bf16[2,1040,128]{2,1,0:T(8,128)(2,1)} %collective-permute-done.4.refs_4_.refs_5_), channel_id=1, source_target_pairs={{0,8},{9,1},{2,10},{11,3},{8,16},{17,9},{10,18},{19,11},{16,24},{2... | collective-permute-start | bytes 1597448 | tf_op jit(solution)/shard_map/ppermute | solution.py:535
  39.9 0.6 collective-permute-start.18
  40.5 0.5 collective-permute-start.13
  41.0 2.0 %collective-permute-done.7.refs_0_.refs_7_ = bf16[2,1040,128]{2,1,0:T(8,128)(2,1)} collective-permute-done((bf16[2,1040,128]{2,1,0:T(8,128)(2,1)S(1)}, bf16[2,1040,128]{2,1,0:T(8,128)(2,1)}, u32[]{:S(2)}, u32[]{:S(2)}) %collective-permute-start.7) | collective-permute-done | bytes 532512 | tf_op jit(solution)/shard_map/ppermute | solution.py:535
  43.0 2.6 %collective-permute-start.8 = (bf16[2,1040,128]{2,1,0:T(8,128)(2,1)}, bf16[2,1040,128]{2,1,0:T(8,128)(2,1)}, u32[]{:S(2)}, u32[]{:S(2)}) collective-permute-start(bf16[2,1040,128]{2,1,0:T(8,128)(2,1)} %collective-permute-done.7.refs_0_.refs_7_), channel_id=1, source_target_pairs={{0,8},{9,1},{2,10},{11,3},{8,16},{17,9},{10,18},{19,11},{16,24},{2... | collective-permute-start | bytes 1597448 | tf_op jit(solution)/shard_map/ppermute | solution.py:535
  45.6 3.2 %collective-permute-done.5.refs_2_.refs_9_ = bf16[2,1040,128]{2,1,0:T(8,128)(2,1)} collective-permute-done((bf16[2,1040,128]{2,1,0:T(8,128)(2,1)}, bf16[2,1040,128]{2,1,0:T(8,128)(2,1)}, u32[]{:S(2)}, u32[]{:S(2)}) %collective-permute-start.5) | collective-permute-done | bytes 532512 | tf_op jit(solution)/shard_map/ppermute | solution.py:535
  48.8 2.5 %collective-permute-start.10 = (bf16[2,1040,128]{2,1,0:T(8,128)(2,1)}, bf16[2,1040,128]{2,1,0:T(8,128)(2,1)}, u32[]{:S(2)}, u32[]{:S(2)}) collective-permute-start(bf16[2,1040,128]{2,1,0:T(8,128)(2,1)} %collective-permute-done.5.refs_2_.refs_9_), channel_id=1, source_target_pairs={{0,8},{9,1},{2,10},{11,3},{8,16},{17,9},{10,18},{19,11},{16,24},{2... | collective-permute-start | bytes 1597448 | tf_op jit(solution)/shard_map/ppermute | solution.py:535
  51.3 0.7 pad_maximum_fusion.2
  52.1 0.8 copy-done.4
  52.9 0.5 collective-permute-start.15
  53.4 5.3 %project.2.refs_4_ = bf16[24,512,128]{2,1,0:T(8,128)(2,1)} custom-call(bf16[512,1024]{1,0:T(8,128)(2,1)} %get-tuple-element.27.normed, bf16[2,1040,128]{2,1,0:T(8,128)(2,1)} %copy-done, bf16[2,1040,128]{2,1,0:T(8,128)(2,1)} %copy-done.2, bf16[2,1040,128]{2,1,0:T(8,128)(2,1)} %copy-done.3, bf16[2,1040,128]{2,1,0:T(8,128)(2,1)} %copy-done.4, ...), custom_call_target="tpu_custom_call" | custom-call | flops 1000 | bytes 1000 | tf_op jit(solution)/shard_map/project/pallas_call | solution.py:274
  58.7 1.5 %collective-permute-done.10.refs_2_.refs_13_ = bf16[2,1040,128]{2,1,0:T(8,128)(2,1)} collective-permute-done((bf16[2,1040,128]{2,1,0:T(8,128)(2,1)}, bf16[2,1040,128]{2,1,0:T(8,128)(2,1)}, u32[]{:S(2)}, u32[]{:S(2)}) %collective-permute-start.10) | collective-permute-done | bytes 532512 | tf_op jit(solution)/shard_map/ppermute | solution.py:535
  60.2 2.5 %collective-permute-start.14 = (bf16[2,1040,128]{2,1,0:T(8,128)(2,1)}, bf16[2,1040,128]{2,1,0:T(8,128)(2,1)S(1)}, u32[]{:S(2)}, u32[]{:S(2)}) collective-permute-start(bf16[2,1040,128]{2,1,0:T(8,128)(2,1)} %collective-permute-done.8.refs_0_.refs_11_), channel_id=1, source_target_pairs={{0,8},{9,1},{2,10},{11,3},{8,16},{17,9},{10,18},{19,11},{16,24},{2... | collective-permute-start | bytes 1597448 | tf_op jit(solution)/shard_map/ppermute | solution.py:535
  62.7 1.0 select_bitcast_fusion.1
  63.7 0.1 pad_maximum_fusion.refs_0_
  63.8 1.6 %collective-permute-start.20 = (bf16[2,2,544,128]{3,2,1,0:T(8,128)(2,1)S(1)}, bf16[2,2,544,128]{3,2,1,0:T(8,128)(2,1)}, u32[]{:S(2)}, u32[]{:S(2)}) collective-permute-start(bf16[2,2,544,128]{3,2,1,0:T(8,128)(2,1)S(1)} %pad_maximum_fusion.refs_0_), channel_id=1, source_target_pairs={{0,8},{9,1},{2,10},{11,3},{8,16},{17,9},{10,18},{19,11},{16,24},{2... | collective-permute-start | bytes 1671176 | tf_op jit(solution)/shard_map/ppermute | solution.py:535
  65.4 4.7 %project.3.refs_6_ = bf16[24,512,128]{2,1,0:T(8,128)(2,1)} custom-call(bf16[512,1024]{1,0:T(8,128)(2,1)} %get-tuple-element.27.normed, bf16[2,1040,128]{2,1,0:T(8,128)(2,1)} %collective-permute-done.7.refs_0_.refs_7_, bf16[2,1040,128]{2,1,0:T(8,128)(2,1)} %collective-permute-done.15.refs_1_.refs_8_, ...), custom_call_target="tpu_custom_call", output_to_operand_aliasing={{}: (5, {})} | custom-call | flops 1000 | bytes 1000 | tf_op jit(solution)/shard_map/project/pallas_call | solution.py:274
  70.1 0.6 collective-permute-start.11
  70.7 0.1 collective-permute-start.17
  70.8 1.7 %collective-permute-done.11.refs_3_.refs_14_ = bf16[2,1040,128]{2,1,0:T(8,128)(2,1)S(1)} collective-permute-done((bf16[2,1040,128]{2,1,0:T(8,128)(2,1)}, bf16[2,1040,128]{2,1,0:T(8,128)(2,1)S(1)}, u32[]{:S(2)}, u32[]{:S(2)}) %collective-permute-start.11) | collective-permute-done | bytes 532512 | tf_op jit(solution)/shard_map/ppermute | solution.py:539
  72.5 3.3 %collective-permute-done.20.refs_1_ = bf16[2,2,544,128]{3,2,1,0:T(8,128)(2,1)} collective-permute-done((bf16[2,2,544,128]{3,2,1,0:T(8,128)(2,1)S(1)}, bf16[2,2,544,128]{3,2,1,0:T(8,128)(2,1)}, u32[]{:S(2)}, u32[]{:S(2)}) %collective-permute-start.20) | collective-permute-done | bytes 557088 | tf_op jit(solution)/shard_map/ppermute | solution.py:535
  75.8 2.7 %collective-permute-start.22 = (bf16[2,2,544,128]{3,2,1,0:T(8,128)(2,1)}, bf16[2,2,544,128]{3,2,1,0:T(8,128)(2,1)}, u32[]{:S(2)}, u32[]{:S(2)}) collective-permute-start(bf16[2,2,544,128]{3,2,1,0:T(8,128)(2,1)} %collective-permute-done.20.refs_1_), channel_id=1, source_target_pairs={{0,8},{9,1},{2,10},{11,3},{8,16},{17,9},{10,18},{19,11},{16,24},{2... | collective-permute-start | bytes 1671176 | tf_op jit(solution)/shard_map/ppermute | solution.py:535
  78.5 9.4 %attend.1.refs_0_ = bf16[256,1024]{1,0:T(8,128)(2,1)} custom-call(bf16[512,1024]{1,0:T(8,128)(2,1)} %get-tuple-element.27.normed, f32[2,128,384]{2,1,0:T(8,128)} %get-tuple-element.28.bias, bf16[2,1040,128]{2,1,0:T(8,128)(2,1)} %collective-permute-done.8.refs_0_.refs_11_, bf16[2,1040,128]{2,1,0:T(8,128)(2,1)} %copy-done.6, ...), custom_call_target="tpu_custom_call" | custom-call | flops 1000 | bytes 1000 | tf_op jit(solution)/shard_map/attend/pallas_call | solution.py:332
  88.0 1.6 %collective-permute-start.24 = (bf16[2,2,544,128]{3,2,1,0:T(8,128)(2,1)}, bf16[2,2,544,128]{3,2,1,0:T(8,128)(2,1)S(1)}, u32[]{:S(2)}, u32[]{:S(2)}) collective-permute-start(bf16[2,2,544,128]{3,2,1,0:T(8,128)(2,1)} %collective-permute-done.22.refs_3_), channel_id=1, source_target_pairs={{0,8},{9,1},{2,10},{11,3},{8,16},{17,9},{10,18},{19,11},{16,24},{2... | collective-permute-start | bytes 1671176 | tf_op jit(solution)/shard_map/ppermute | solution.py:535
  89.6 5.1 %mix.1 = (bf16[256,1024]{1,0:T(8,128)(2,1)}, bf16[128,1024]{1,0:T(8,128)(2,1)}) custom-call(bf16[256,1024]{1,0:T(8,128)(2,1)} %bitcast.30, f32[1,1024]{1,0:T(1,128)} %bitcast.38, bf16[256,1024]{1,0:T(8,128)(2,1)} %attend.1.refs_0_, bf16[2,1040,128]{2,1,0:T(8,128)(2,1)} %copy-done, bf16[2,1040,128]{2,1,0:T(8,128)(2,1)} %copy-done.2, ...), custom_call_target="tpu_custom_call" | custom-call | flops 1000 | bytes 1000 | tf_op jit(solution)/shard_map/mix/pallas_call | solution.py:412
  94.7 3.4 %all-to-all-start = ((bf16[8,16,1024]{2,1,0:T(8,128)(2,1)}), bf16[8,16,1024]{2,1,0:T(8,128)(2,1)S(1)}, u32[]{:S(2)}, u32[]{:S(2)}) async-start(bf16[8,16,1024]{2,1,0:T(8,128)(2,1)} %bitcast.33), calls=%async_computation | async-start | bytes 524288 | tf_op jit(solution)/shard_map/all_to_all | solution.py:649
  98.2 2.2 %collective-permute-start.26 = (bf16[2,544,128]{2,1,0:T(8,128)(2,1)S(1)}, bf16[2,544,128]{2,1,0:T(8,128)(2,1)S(1)}, u32[]{:S(2)}, u32[]{:S(2)}) collective-permute-start(bf16[2,544,128]{2,1,0:T(8,128)(2,1)S(1)} %dynamic-slice_bitcast_fusion), channel_id=1, source_target_pairs={{0,8},{9,1},{2,10},{11,3},{8,16},{17,9},{10,18},{19,11},{16,24},{2... | collective-permute-start | bytes 835592 | tf_op jit(solution)/shard_map/ppermute | solution.py:535
  100.4 0.5 collective-permute-start.23
  100.9 6.6 %all-to-all-done = bf16[8,16,1024]{2,1,0:T(8,128)(2,1)S(1)} async-done(((bf16[8,16,1024]{2,1,0:T(8,128)(2,1)}), bf16[8,16,1024]{2,1,0:T(8,128)(2,1)S(1)}, u32[]{:S(2)}, u32[]{:S(2)}) %all-to-all-start) | async-done | bytes 262176 | tf_op jit(solution)/shard_map/all_to_all | solution.py:649
  107.5 0.1 collective-permute-start.27
  107.6 1.5 %collective-permute-done.27.refs_8_ = bf16[2,544,128]{2,1,0:T(8,128)(2,1)S(1)} collective-permute-done((bf16[2,544,128]{2,1,0:T(8,128)(2,1)S(1)}, bf16[2,544,128]{2,1,0:T(8,128)(2,1)S(1)}, u32[]{:S(2)}, u32[]{:S(2)}) %collective-permute-start.27) | collective-permute-done | bytes 278560 | tf_op jit(solution)/shard_map/ppermute | solution.py:539
  109.2 0.8 copy-done.13
  110.1 10.9 %decode.1 = bf16[96,256]{1,0:T(8,128)(2,1)} custom-call(bf16[256,1024]{1,0:T(8,128)(2,1)} %bitcast.32, bf16[256,1024]{1,0:T(8,128)(2,1)} %get-tuple-element.31.decoded, bf16[128,1024]{1,0:T(8,128)(2,1)} %bitcast.31, f32[256,256]{1,0:T(8,128)} %get-tuple-element.33.here, f32[256,128]{1,0:T(8,128)} %get-tuple-element.34.there, ...), custom_call_target="tpu_custom_call" | custom-call | flops 1000 | bytes 1000 | tf_op jit(solution)/shard_map/decode/pallas_call | solution.py:490
  (68 shorter events, 0.3 us)
Async XLA Ops:
  0.0 39.9 %copy-start.19 = (bf16[256,12]{0,1:T(8,128)(2,1)S(1)}, bf16[256,12]{0,1:T(8,128)(2,1)}, u32[]{:S(2)}) copy-start(bf16[256,12]{0,1:T(8,128)(2,1)} %param.20) | copy-start | bytes 18436
  0.0 39.9 %copy-start.18 = (bf16[256,256]{1,0:T(8,128)(2,1)S(1)}, bf16[256,256]{1,0:T(8,128)(2,1)}, u32[]{:S(2)}) copy-start(bf16[256,256]{1,0:T(8,128)(2,1)} %param.19) | copy-start | bytes 393220
  3.0 9.5 %collective-permute-start.2 = (bf16[1040,128]{1,0:T(8,128)(2,1)}, bf16[1040,128]{1,0:T(8,128)(2,1)S(1)}, u32[]{:S(2)}, u32[]{:S(2)}) collective-permute-start(bf16[1040,128]{1,0:T(8,128)(2,1)} %get-tuple-element.24), channel_id=1, source_target_pairs={{0,2},{1,3},{2,0},{3,1},{4,6},{5,7},{6,4},{7,5},{8,10},{9,11},{10,... | collective-permute-start | bytes 798728 | tf_op jit(solution)/shard_map/ppermute | solution.py:517
  7.0 14.3 %collective-permute-start = (bf16[128,1024]{1,0:T(8,128)(2,1)S(1)}, bf16[128,1024]{1,0:T(8,128)(2,1)S(1)}, u32[]{:S(2)}, u32[]{:S(2)}) collective-permute-start(bf16[128,1024]{1,0:T(8,128)(2,1)S(1)} %get-tuple-element.46), channel_id=1, source_target_pairs={{0,4},{4,8},{8,12},{12,16},{16,20},{20,24},{24,28},{1,5},{5,9},{9,... | collective-permute-start | bytes 786440 | tf_op jit(solution)/shard_map/ppermute | solution.py:593
  10.5 10.9 %collective-permute-start.1 = (bf16[128,1024]{1,0:T(8,128)(2,1)S(1)}, bf16[128,1024]{1,0:T(8,128)(2,1)S(1)}, u32[]{:S(2)}, u32[]{:S(2)}) collective-permute-start(bf16[128,1024]{1,0:T(8,128)(2,1)S(1)} %get-tuple-element.45), channel_id=1, source_target_pairs={{4,0},{8,4},{12,8},{16,12},{20,16},{24,20},{28,24},{5,1},{9,5},{13... | collective-permute-start | bytes 786440 | tf_op jit(solution)/shard_map/ppermute | solution.py:594
  13.6 39.8 %copy-start = (bf16[2,1040,128]{2,1,0:T(8,128)(2,1)}, bf16[2,1040,128]{2,1,0:T(8,128)(2,1)S(1)}, u32[]{:S(2)}) copy-start(bf16[2,1040,128]{2,1,0:T(8,128)(2,1)S(1)} %pad_maximum_fusion.1.refs_0_.refs_1_) | copy-start | bytes 1597444
  21.3 5.4 %copy-start.16 = (bf16[128,1024]{1,0:T(8,128)(2,1)}, bf16[128,1024]{1,0:T(8,128)(2,1)S(1)}, u32[]{:S(2)}) copy-start(bf16[128,1024]{1,0:T(8,128)(2,1)S(1)} %collective-permute-done.left) | copy-start | bytes 786436
  21.4 3.5 %copy-start.17 = (bf16[128,1024]{1,0:T(8,128)(2,1)}, bf16[128,1024]{1,0:T(8,128)(2,1)S(1)}, u32[]{:S(2)}) copy-start(bf16[128,1024]{1,0:T(8,128)(2,1)S(1)} %collective-permute-done.1.right) | copy-start | bytes 786436
  21.4 3.4 %collective-permute-start.3 = (bf16[2,1040,128]{2,1,0:T(8,128)(2,1)S(1)}, bf16[2,1040,128]{2,1,0:T(8,128)(2,1)S(1)}, u32[]{:S(2)}, u32[]{:S(2)}) collective-permute-start(bf16[2,1040,128]{2,1,0:T(8,128)(2,1)S(1)} %pad_maximum_fusion.1.refs_0_.refs_1_), channel_id=1, source_target_pairs={{0,1},{1,0},{2,3},{3,2},{4,5},{5,4},{6,7},{7,6},{8,9},{9,8},{10,11... | collective-permute-start | bytes 1597448 | tf_op jit(solution)/shard_map/ppermute | solution.py:539
  21.4 10.2 %collective-permute-start.6 = (bf16[2,1040,128]{2,1,0:T(8,128)(2,1)S(1)}, bf16[2,1040,128]{2,1,0:T(8,128)(2,1)S(1)}, u32[]{:S(2)}, u32[]{:S(2)}) collective-permute-start(bf16[2,1040,128]{2,1,0:T(8,128)(2,1)S(1)} %pad_maximum_fusion.1.refs_0_.refs_1_), channel_id=1, source_target_pairs={{0,8},{9,1},{2,10},{11,3},{8,16},{17,9},{10,18},{19,11},{16,24},{2... | collective-permute-start | bytes 1597448 | tf_op jit(solution)/shard_map/ppermute | solution.py:535
  24.8 28.6 %copy-start.2 = (bf16[2,1040,128]{2,1,0:T(8,128)(2,1)}, bf16[2,1040,128]{2,1,0:T(8,128)(2,1)S(1)}, u32[]{:S(2)}) copy-start(bf16[2,1040,128]{2,1,0:T(8,128)(2,1)S(1)} %collective-permute-done.3.refs_1_.refs_2_) | copy-start | bytes 1597444
  24.8 12.5 %collective-permute-start.4 = (bf16[2,1040,128]{2,1,0:T(8,128)(2,1)S(1)}, bf16[2,1040,128]{2,1,0:T(8,128)(2,1)}, u32[]{:S(2)}, u32[]{:S(2)}) collective-permute-start(bf16[2,1040,128]{2,1,0:T(8,128)(2,1)S(1)} %collective-permute-done.3.refs_1_.refs_2_), channel_id=1, source_target_pairs={{0,8},{9,1},{2,10},{11,3},{8,16},{17,9},{10,18},{19,11},{16,24},{2... | collective-permute-start | bytes 1597448 | tf_op jit(solution)/shard_map/ppermute | solution.py:535
  31.6 21.8 %copy-start.3 = (bf16[2,1040,128]{2,1,0:T(8,128)(2,1)}, bf16[2,1040,128]{2,1,0:T(8,128)(2,1)S(1)}, u32[]{:S(2)}) copy-start(bf16[2,1040,128]{2,1,0:T(8,128)(2,1)S(1)} %collective-permute-done.6.refs_2_.refs_3_) | copy-start | bytes 1597444
  31.6 11.4 %collective-permute-start.7 = (bf16[2,1040,128]{2,1,0:T(8,128)(2,1)S(1)}, bf16[2,1040,128]{2,1,0:T(8,128)(2,1)}, u32[]{:S(2)}, u32[]{:S(2)}) collective-permute-start(bf16[2,1040,128]{2,1,0:T(8,128)(2,1)S(1)} %collective-permute-done.6.refs_2_.refs_3_), channel_id=1, source_target_pairs={{0,8},{9,1},{2,10},{11,3},{8,16},{17,9},{10,18},{19,11},{16,24},{2... | collective-permute-start | bytes 1597448 | tf_op jit(solution)/shard_map/ppermute | solution.py:535
  37.3 11.5 %collective-permute-start.5 = (bf16[2,1040,128]{2,1,0:T(8,128)(2,1)}, bf16[2,1040,128]{2,1,0:T(8,128)(2,1)}, u32[]{:S(2)}, u32[]{:S(2)}) collective-permute-start(bf16[2,1040,128]{2,1,0:T(8,128)(2,1)} %collective-permute-done.4.refs_4_.refs_5_), channel_id=1, source_target_pairs={{0,8},{9,1},{2,10},{11,3},{8,16},{17,9},{10,18},{19,11},{16,24},{2... | collective-permute-start | bytes 1597448 | tf_op jit(solution)/shard_map/ppermute | solution.py:535
  39.9 11.4 %collective-permute-start.18 = (bf16[544,128]{1,0:T(8,128)(2,1)S(1)}, bf16[544,128]{1,0:T(8,128)(2,1)S(1)}, u32[]{:S(2)}, u32[]{:S(2)}) collective-permute-start(bf16[544,128]{1,0:T(8,128)(2,1)S(1)} %pad_maximum_fusion.3), channel_id=1, source_target_pairs={{0,2},{1,3},{2,0},{3,1},{4,6},{5,7},{6,4},{7,5},{8,10},{9,11},{10,... | collective-permute-start | bytes 417800 | tf_op jit(solution)/shard_map/ppermute | solution.py:517
  40.5 11.5 %collective-permute-start.12 = (bf16[2,1040,128]{2,1,0:T(8,128)(2,1)S(1)}, bf16[2,1040,128]{2,1,0:T(8,128)(2,1)S(1)}, u32[]{:S(2)}, u32[]{:S(2)}) collective-permute-start(bf16[2,1040,128]{2,1,0:T(8,128)(2,1)S(1)} %collective-permute-done.6.refs_2_.refs_3_), channel_id=1, source_target_pairs={{0,1},{1,0},{2,3},{3,2},{4,5},{5,4},{6,7},{7,6},{8,9},{9,8},{10,11... | collective-permute-start | bytes 1597448 | tf_op jit(solution)/shard_map/ppermute | solution.py:539
  40.5 12.8 %collective-permute-start.13 = (bf16[2,1040,128]{2,1,0:T(8,128)(2,1)}, bf16[2,1040,128]{2,1,0:T(8,128)(2,1)}, u32[]{:S(2)}, u32[]{:S(2)}) collective-permute-start(bf16[2,1040,128]{2,1,0:T(8,128)(2,1)} %collective-permute-done.4.refs_4_.refs_5_), channel_id=1, source_target_pairs={{0,1},{1,0},{2,3},{3,2},{4,5},{5,4},{6,7},{7,6},{8,9},{9,8},{10,11... | collective-permute-start | bytes 1597448 | tf_op jit(solution)/shard_map/ppermute | solution.py:539
  43.0 15.7 %collective-permute-start.8 = (bf16[2,1040,128]{2,1,0:T(8,128)(2,1)}, bf16[2,1040,128]{2,1,0:T(8,128)(2,1)}, u32[]{:S(2)}, u32[]{:S(2)}) collective-permute-start(bf16[2,1040,128]{2,1,0:T(8,128)(2,1)} %collective-permute-done.7.refs_0_.refs_7_), channel_id=1, source_target_pairs={{0,8},{9,1},{2,10},{11,3},{8,16},{17,9},{10,18},{19,11},{16,24},{2... | collective-permute-start | bytes 1597448 | tf_op jit(solution)/shard_map/ppermute | solution.py:535
  48.8 11.4 %collective-permute-start.10 = (bf16[2,1040,128]{2,1,0:T(8,128)(2,1)}, bf16[2,1040,128]{2,1,0:T(8,128)(2,1)}, u32[]{:S(2)}, u32[]{:S(2)}) collective-permute-start(bf16[2,1040,128]{2,1,0:T(8,128)(2,1)} %collective-permute-done.5.refs_2_.refs_9_), channel_id=1, source_target_pairs={{0,8},{9,1},{2,10},{11,3},{8,16},{17,9},{10,18},{19,11},{16,24},{2... | collective-permute-start | bytes 1597448 | tf_op jit(solution)/shard_map/ppermute | solution.py:535
  52.1 10.7 %collective-permute-start.19 = (bf16[2,544,128]{2,1,0:T(8,128)(2,1)}, bf16[2,544,128]{2,1,0:T(8,128)(2,1)}, u32[]{:S(2)}, u32[]{:S(2)}) collective-permute-start(bf16[2,544,128]{2,1,0:T(8,128)(2,1)} %pad_maximum_fusion.2), channel_id=1, source_target_pairs={{0,1},{1,0},{2,3},{3,2},{4,5},{5,4},{6,7},{7,6},{8,9},{9,8},{10,11... | collective-permute-start | bytes 835592 | tf_op jit(solution)/shard_map/ppermute | solution.py:539
  52.9 10.9 %collective-permute-start.15 = (bf16[2,1040,128]{2,1,0:T(8,128)(2,1)}, bf16[2,1040,128]{2,1,0:T(8,128)(2,1)}, u32[]{:S(2)}, u32[]{:S(2)}) collective-permute-start(bf16[2,1040,128]{2,1,0:T(8,128)(2,1)} %collective-permute-done.7.refs_0_.refs_7_), channel_id=1, source_target_pairs={{0,1},{1,0},{2,3},{3,2},{4,5},{5,4},{6,7},{7,6},{8,9},{9,8},{10,11... | collective-permute-start | bytes 1597448 | tf_op jit(solution)/shard_map/ppermute | solution.py:539
  53.4 10.4 %collective-permute-start.16 = (bf16[2,1040,128]{2,1,0:T(8,128)(2,1)}, bf16[2,1040,128]{2,1,0:T(8,128)(2,1)}, u32[]{:S(2)}, u32[]{:S(2)}) collective-permute-start(bf16[2,1040,128]{2,1,0:T(8,128)(2,1)} %collective-permute-done.5.refs_2_.refs_9_), channel_id=1, source_target_pairs={{0,1},{1,0},{2,3},{3,2},{4,5},{5,4},{6,7},{7,6},{8,9},{9,8},{10,11... | collective-permute-start | bytes 1597448 | tf_op jit(solution)/shard_map/ppermute | solution.py:539
  60.2 10.5 %collective-permute-start.14 = (bf16[2,1040,128]{2,1,0:T(8,128)(2,1)}, bf16[2,1040,128]{2,1,0:T(8,128)(2,1)S(1)}, u32[]{:S(2)}, u32[]{:S(2)}) collective-permute-start(bf16[2,1040,128]{2,1,0:T(8,128)(2,1)} %collective-permute-done.8.refs_0_.refs_11_), channel_id=1, source_target_pairs={{0,8},{9,1},{2,10},{11,3},{8,16},{17,9},{10,18},{19,11},{16,24},{2... | collective-permute-start | bytes 1597448 | tf_op jit(solution)/shard_map/ppermute | solution.py:535
  63.8 6.4 %copy-start.1 = (bf16[2,2,544,128]{3,2,1,0:T(8,128)(2,1)}, bf16[2,2,544,128]{3,2,1,0:T(8,128)(2,1)S(1)}, u32[]{:S(2)}) copy-start(bf16[2,2,544,128]{3,2,1,0:T(8,128)(2,1)S(1)} %pad_maximum_fusion.refs_0_) | copy-start | bytes 1671172
  63.8 12.0 %collective-permute-start.20 = (bf16[2,2,544,128]{3,2,1,0:T(8,128)(2,1)S(1)}, bf16[2,2,544,128]{3,2,1,0:T(8,128)(2,1)}, u32[]{:S(2)}, u32[]{:S(2)}) collective-permute-start(bf16[2,2,544,128]{3,2,1,0:T(8,128)(2,1)S(1)} %pad_maximum_fusion.refs_0_), channel_id=1, source_target_pairs={{0,8},{9,1},{2,10},{11,3},{8,16},{17,9},{10,18},{19,11},{16,24},{2... | collective-permute-start | bytes 1671176 | tf_op jit(solution)/shard_map/ppermute | solution.py:535
  65.4 5.4 %collective-permute-start.9 = (bf16[2,1040,128]{2,1,0:T(8,128)(2,1)}, bf16[2,1040,128]{2,1,0:T(8,128)(2,1)S(1)}, u32[]{:S(2)}, u32[]{:S(2)}) collective-permute-start(bf16[2,1040,128]{2,1,0:T(8,128)(2,1)} %collective-permute-done.8.refs_0_.refs_11_), channel_id=1, source_target_pairs={{0,1},{1,0},{2,3},{3,2},{4,5},{5,4},{6,7},{7,6},{8,9},{9,8},{10,11... | collective-permute-start | bytes 1597448 | tf_op jit(solution)/shard_map/ppermute | solution.py:539
  70.1 2.3 %collective-permute-start.11 = (bf16[2,1040,128]{2,1,0:T(8,128)(2,1)}, bf16[2,1040,128]{2,1,0:T(8,128)(2,1)S(1)}, u32[]{:S(2)}, u32[]{:S(2)}) collective-permute-start(bf16[2,1040,128]{2,1,0:T(8,128)(2,1)} %collective-permute-done.10.refs_2_.refs_13_), channel_id=1, source_target_pairs={{0,1},{1,0},{2,3},{3,2},{4,5},{5,4},{6,7},{7,6},{8,9},{9,8},{10,11... | collective-permute-start | bytes 1597448 | tf_op jit(solution)/shard_map/ppermute | solution.py:539
  70.7 7.8 %copy-start.5 = (bf16[2,1040,128]{2,1,0:T(8,128)(2,1)}, bf16[2,1040,128]{2,1,0:T(8,128)(2,1)S(1)}, u32[]{:S(2)}) copy-start(bf16[2,1040,128]{2,1,0:T(8,128)(2,1)S(1)} %collective-permute-done.14.refs_4_.refs_15_) | copy-start | bytes 1597444
  70.7 5.1 %collective-permute-start.17 = (bf16[2,1040,128]{2,1,0:T(8,128)(2,1)S(1)}, bf16[2,1040,128]{2,1,0:T(8,128)(2,1)S(1)}, u32[]{:S(2)}, u32[]{:S(2)}) collective-permute-start(bf16[2,1040,128]{2,1,0:T(8,128)(2,1)S(1)} %collective-permute-done.14.refs_4_.refs_15_), channel_id=1, source_target_pairs={{0,1},{1,0},{2,3},{3,2},{4,5},{5,4},{6,7},{7,6},{8,9},{9,8},{10,11... | collective-permute-start | bytes 1597448 | tf_op jit(solution)/shard_map/ppermute | solution.py:539
  70.8 7.7 %copy-start.6 = (bf16[2,1040,128]{2,1,0:T(8,128)(2,1)}, bf16[2,1040,128]{2,1,0:T(8,128)(2,1)S(1)}, u32[]{:S(2)}) copy-start(bf16[2,1040,128]{2,1,0:T(8,128)(2,1)S(1)} %collective-permute-done.9.refs_1_.refs_12_) | copy-start | bytes 1597444
  72.5 3.3 %copy-start.7 = (bf16[2,1040,128]{2,1,0:T(8,128)(2,1)}, bf16[2,1040,128]{2,1,0:T(8,128)(2,1)S(1)}, u32[]{:S(2)}) copy-start(bf16[2,1040,128]{2,1,0:T(8,128)(2,1)S(1)} %collective-permute-done.11.refs_3_.refs_14_) | copy-start | bytes 1597444
  75.8 2.7 %copy-start.8 = (bf16[2,1040,128]{2,1,0:T(8,128)(2,1)}, bf16[2,1040,128]{2,1,0:T(8,128)(2,1)S(1)}, u32[]{:S(2)}) copy-start(bf16[2,1040,128]{2,1,0:T(8,128)(2,1)S(1)} %collective-permute-done.17.refs_5_.refs_16_) | copy-start | bytes 1597444
  75.8 12.2 %collective-permute-start.22 = (bf16[2,2,544,128]{3,2,1,0:T(8,128)(2,1)}, bf16[2,2,544,128]{3,2,1,0:T(8,128)(2,1)}, u32[]{:S(2)}, u32[]{:S(2)}) collective-permute-start(bf16[2,2,544,128]{3,2,1,0:T(8,128)(2,1)} %collective-permute-done.20.refs_1_), channel_id=1, source_target_pairs={{0,8},{9,1},{2,10},{11,3},{8,16},{17,9},{10,18},{19,11},{16,24},{2... | collective-permute-start | bytes 1671176 | tf_op jit(solution)/shard_map/ppermute | solution.py:535
  88.0 10.2 %collective-permute-start.24 = (bf16[2,2,544,128]{3,2,1,0:T(8,128)(2,1)}, bf16[2,2,544,128]{3,2,1,0:T(8,128)(2,1)S(1)}, u32[]{:S(2)}, u32[]{:S(2)}) collective-permute-start(bf16[2,2,544,128]{3,2,1,0:T(8,128)(2,1)} %collective-permute-done.22.refs_3_), channel_id=1, source_target_pairs={{0,8},{9,1},{2,10},{11,3},{8,16},{17,9},{10,18},{19,11},{16,24},{2... | collective-permute-start | bytes 1671176 | tf_op jit(solution)/shard_map/ppermute | solution.py:535
  94.7 12.8 %all-to-all-start = ((bf16[8,16,1024]{2,1,0:T(8,128)(2,1)}), bf16[8,16,1024]{2,1,0:T(8,128)(2,1)S(1)}, u32[]{:S(2)}, u32[]{:S(2)}) async-start(bf16[8,16,1024]{2,1,0:T(8,128)(2,1)} %bitcast.33), calls=%async_computation | async-start | bytes 524288 | tf_op jit(solution)/shard_map/all_to_all | solution.py:649
  98.2 11.9 %copy-start.9 = (bf16[2,2,544,128]{3,2,1,0:T(8,128)(2,1)}, bf16[2,2,544,128]{3,2,1,0:T(8,128)(2,1)S(1)}, u32[]{:S(2)}) copy-start(bf16[2,2,544,128]{3,2,1,0:T(8,128)(2,1)S(1)} %collective-permute-done.24.refs_5_) | copy-start | bytes 1671172
  98.2 9.3 %collective-permute-start.26 = (bf16[2,544,128]{2,1,0:T(8,128)(2,1)S(1)}, bf16[2,544,128]{2,1,0:T(8,128)(2,1)S(1)}, u32[]{:S(2)}, u32[]{:S(2)}) collective-permute-start(bf16[2,544,128]{2,1,0:T(8,128)(2,1)S(1)} %dynamic-slice_bitcast_fusion), channel_id=1, source_target_pairs={{0,8},{9,1},{2,10},{11,3},{8,16},{17,9},{10,18},{19,11},{16,24},{2... | collective-permute-start | bytes 835592 | tf_op jit(solution)/shard_map/ppermute | solution.py:535
  100.4 7.2 %collective-permute-start.21 = (bf16[2,2,544,128]{3,2,1,0:T(8,128)(2,1)}, bf16[2,2,544,128]{3,2,1,0:T(8,128)(2,1)S(1)}, u32[]{:S(2)}, u32[]{:S(2)}) collective-permute-start(bf16[2,2,544,128]{3,2,1,0:T(8,128)(2,1)} %collective-permute-done.20.refs_1_), channel_id=1, source_target_pairs={{0,1},{1,0},{2,3},{3,2},{4,5},{5,4},{6,7},{7,6},{8,9},{9,8},{10,11... | collective-permute-start | bytes 1671176 | tf_op jit(solution)/shard_map/ppermute | solution.py:539
  100.4 7.2 %collective-permute-start.23 = (bf16[2,2,544,128]{3,2,1,0:T(8,128)(2,1)}, bf16[2,2,544,128]{3,2,1,0:T(8,128)(2,1)S(1)}, u32[]{:S(2)}, u32[]{:S(2)}) collective-permute-start(bf16[2,2,544,128]{3,2,1,0:T(8,128)(2,1)} %collective-permute-done.22.refs_3_), channel_id=1, source_target_pairs={{0,1},{1,0},{2,3},{3,2},{4,5},{5,4},{6,7},{7,6},{8,9},{9,8},{10,11... | collective-permute-start | bytes 1671176 | tf_op jit(solution)/shard_map/ppermute | solution.py:539
  100.9 8.2 %collective-permute-start.25 = (bf16[2,2,544,128]{3,2,1,0:T(8,128)(2,1)S(1)}, bf16[2,2,544,128]{3,2,1,0:T(8,128)(2,1)S(1)}, u32[]{:S(2)}, u32[]{:S(2)}) collective-permute-start(bf16[2,2,544,128]{3,2,1,0:T(8,128)(2,1)S(1)} %collective-permute-done.24.refs_5_), channel_id=1, source_target_pairs={{0,1},{1,0},{2,3},{3,2},{4,5},{5,4},{6,7},{7,6},{8,9},{9,8},{10,11... | collective-permute-start | bytes 1671176 | tf_op jit(solution)/shard_map/ppermute | solution.py:539
  107.5 2.5 %copy-start.10 = (bf16[8,16,1024]{2,1,0:T(8,128)(2,1)}, bf16[8,16,1024]{2,1,0:T(8,128)(2,1)S(1)}, u32[]{:S(2)}) copy-start(bf16[8,16,1024]{2,1,0:T(8,128)(2,1)S(1)} %all-to-all-done) | copy-start | bytes 786436
  107.5 2.5 %copy-start.14 = (bf16[2,544,128]{2,1,0:T(8,128)(2,1)}, bf16[2,544,128]{2,1,0:T(8,128)(2,1)S(1)}, u32[]{:S(2)}) copy-start(bf16[2,544,128]{2,1,0:T(8,128)(2,1)S(1)} %collective-permute-done.26.refs_7_) | copy-start | bytes 835588
  107.5 1.6 %collective-permute-start.27 = (bf16[2,544,128]{2,1,0:T(8,128)(2,1)S(1)}, bf16[2,544,128]{2,1,0:T(8,128)(2,1)S(1)}, u32[]{:S(2)}, u32[]{:S(2)}) collective-permute-start(bf16[2,544,128]{2,1,0:T(8,128)(2,1)S(1)} %collective-permute-done.26.refs_7_), channel_id=1, source_target_pairs={{0,1},{1,0},{2,3},{3,2},{4,5},{5,4},{6,7},{7,6},{8,9},{9,8},{10,11... | collective-permute-start | bytes 835592 | tf_op jit(solution)/shard_map/ppermute | solution.py:539
  107.6 2.4 %copy-start.11 = (bf16[2,2,544,128]{3,2,1,0:T(8,128)(2,1)}, bf16[2,2,544,128]{3,2,1,0:T(8,128)(2,1)S(1)}, u32[]{:S(2)}) copy-start(bf16[2,2,544,128]{3,2,1,0:T(8,128)(2,1)S(1)} %collective-permute-done.21.refs_2_) | copy-start | bytes 1671172
  107.6 2.4 %copy-start.12 = (bf16[2,2,544,128]{3,2,1,0:T(8,128)(2,1)}, bf16[2,2,544,128]{3,2,1,0:T(8,128)(2,1)S(1)}, u32[]{:S(2)}) copy-start(bf16[2,2,544,128]{3,2,1,0:T(8,128)(2,1)S(1)} %collective-permute-done.23.refs_4_) | copy-start | bytes 1671172
  109.2 0.9 copy-start.15
  109.2 0.8 copy-start.13
  (1 other events, 0.8 us)
